TPU v7x, 1024 devices: a whole 8x8x8 slice. The times are simulated.
1024 devices in a mesh: gx: 64 (over y, z), gz: 16 (over x, core).
Axes of the slice: x: 8, y: 8, z: 8, core: 2. Of those that a mesh axis runs over, the one named last changes fastest.
Arguments:
- previous_basis: float32 [4, 512, 128, 128], P(None, 'gx', 'gz'), may hold values from -4 to 4
- restart_column: int32 [1], replicated, may hold values from 0 to 3
- diffusivity: float32 [3, 512, 128, 128], P(None, 'gx', 'gz'), may hold values from 0.05 to 0.5
- speed: float32 [3, 512, 128, 128], P(None, 'gx', 'gz'), may hold values from 0.05 to 0.5
- upwind: int32 [3, 512, 128, 128], P(None, 'gx', 'gz'), may hold values from 0 to 1
Outputs:
- basis_q: float32 [9, 512, 128, 128], P(None, 'gx', 'gz')
- factor_r: float32 [9, 9], replicated
- hessenberg: float32 [9, 8], replicated
Inputs may be any that keep to these rules, and one draw needn't show every extreme that they name: `upwind`: 1 means the flow across the face runs toward the upper neighbour, 0 toward the cell. `restart_column`: index into the first dimension of previous_basis.
All inputs are finite; a program needn't handle non-finite values.
Results may differ from a plain program's by a relative error of at most 0.0003.
Values sent between devices are 32-bit elements; how exact they have to be, the bound alone decides.
No kernel may reach another device: no remote copies, remote signals or barrier semaphores. Data moves between devices by JAX's collectives and lax.ppermute only.
A program may use at most 32 MiB of HBM per device.

v0:
```python
import math

import jax
import jax.numpy as jnp
import numpy as np
from jax import lax
from jax.sharding import PartitionSpec as P

S = 8


CENTER = 2.5
HALF = 1.5


def shifted(block, axis, distance):
    devices = range(lax.axis_size(axis))
    route = [(i - distance, i) for i in devices if i - distance in devices]
    return lax.ppermute(block, axis, route)


def extended_2(cells, sides, width):
    for axis, dim in sides:
        count = lax.axis_size(axis)
        ends = count - 1
        head = lax.slice_in_dim(cells, 0, width, axis=dim)
        tail = lax.slice_in_dim(cells, cells.shape[dim] - width, cells.shape[dim], axis=dim)
        cells = jnp.concatenate(
            [
                lax.ppermute(tail, axis, [(i, (i + 1) % count) for i in range(ends)]),
                cells,
                lax.ppermute(head, axis, [((i + 1) % count, i) for i in range(ends)]),
            ],
            axis=dim,
        )
    return cells


def stencil(field, pco, qco):
    f = jnp.pad(field, ((0, 0), (0, 0), (1, 1)))
    p = jnp.pad(pco, ((0, 0), (0, 0), (0, 0), (1, 1)))
    q = jnp.pad(qco, ((0, 0), (0, 0), (0, 0), (1, 1)))
    centre = f[1:-1, 1:-1, 1:-1]
    total = centre
    total = (
        total
        + p[0, 1:-1, 1:-1, 1:-1] * (centre - f[2:, 1:-1, 1:-1])
        - q[0, :-2, 1:-1, 1:-1] * (f[:-2, 1:-1, 1:-1] - centre)
    )
    total = (
        total
        + p[1, 1:-1, 1:-1, 1:-1] * (centre - f[1:-1, 2:, 1:-1])
        - q[1, 1:-1, :-2, 1:-1] * (f[1:-1, :-2, 1:-1] - centre)
    )
    total = (
        total
        + p[2, 1:-1, 1:-1, 1:-1] * (centre - f[1:-1, 1:-1, 2:])
        - q[2, 1:-1, 1:-1, :-2] * (f[1:-1, 1:-1, :-2] - centre)
    )
    return total


def upper_inverse(upper):
    order = upper.shape[0]
    identity = jnp.eye(order, dtype=jnp.float32)
    rows = [None] * order
    for row_index in reversed(range(order)):
        remainder = identity[row_index]
        for other in range(row_index + 1, order):
            remainder = remainder - upper[row_index, other] * rows[other]
        rows[row_index] = remainder / upper[row_index, row_index]
    return jnp.stack(rows, 0)


def gram_of(block):
    return jnp.einsum("kxyz,lxyz->kl", block, block, precision=lax.Precision.HIGHEST)


def chol_upper(gram):
    return jnp.transpose(jnp.linalg.cholesky(gram))


def apply_inverse(block, upper):
    inverse = upper_inverse(upper)
    return jnp.einsum("jk,jxyz->kxyz", inverse, block, precision=lax.Precision.HIGHEST)


def change_matrix():
    table = np.zeros((9, 8))
    for col in range(8):
        table[col, col] = CENTER
        if col == 0:
            table[1, 0] = HALF
        else:
            table[col - 1, col] = 0.5 * HALF
            table[col + 1, col] = 0.5 * HALF
    return jnp.asarray(table, dtype=jnp.float32)


def hessenberg_of(upper):
    product = jnp.dot(upper, change_matrix(), precision=lax.Precision.HIGHEST)
    inverse = upper_inverse(upper[:8, :8])
    return jnp.dot(product, inverse, precision=lax.Precision.HIGHEST)


def global_gram(block):
    return lax.psum(gram_of(block), ("gx", "gz"))


def body(previous_basis, restart_column, diffusivity, speed, upwind):
    flow = upwind.astype(jnp.float32)
    p_face = diffusivity + speed * flow
    q_face = diffusivity + speed * (1.0 - flow)
    start = lax.dynamic_index_in_dim(previous_basis, restart_column[0], 0, keepdims=False)
    rows_x = start.shape[0]
    rows_y = start.shape[1]
    lower_x = shifted(q_face[0, rows_x - 1], "gx", 1)
    lower_y = shifted(q_face[1, :, rows_y - 1], "gz", 1)
    p_rim = jnp.pad(p_face, ((0, 0), (1, 1), (1, 1), (0, 0)))
    q_rim = jnp.pad(q_face, ((0, 0), (1, 1), (1, 1), (0, 0)))
    q_rim = q_rim.at[0, 0, 1:-1].set(lower_x)
    q_rim = q_rim.at[1, 1:-1, 0].set(lower_y)
    vectors = [start]
    for step in range(S):
        field = vectors[-1]
        extended = extended_2(field, (("gx", 0), ("gz", 1)), 1)
        zed = (stencil(extended, p_rim, q_rim) - CENTER * field) / HALF
        if step == 0:
            vectors.append(zed)
        else:
            vectors.append(2.0 * zed - vectors[-2])
    block = jnp.stack(vectors, 0)
    upper_one = chol_upper(global_gram(block))
    first_q = apply_inverse(block, upper_one)
    upper_two = chol_upper(global_gram(first_q))
    final_q = apply_inverse(first_q, upper_two)
    upper = jnp.dot(upper_two, upper_one, precision=lax.Precision.HIGHEST)
    scale = math.sqrt(rows_x * rows_y * block.shape[3] * lax.axis_size("gx") * lax.axis_size("gz"))
    return (final_q * scale, upper / scale, hessenberg_of(upper))


def solution(mesh):
    return jax.shard_map(
        body,
        mesh=mesh,
        in_specs=(
            P(None, "gx", "gz", None),
            P(),
            P(None, "gx", "gz", None),
            P(None, "gx", "gz", None),
            P(None, "gx", "gz", None),
        ),
        out_specs=(P(None, "gx", "gz", None), P(), P()),
        check_vma=False,
    )
```

profile of v0, /device:TPU:1, one launch (start us, length us, event | category | flops | bytes accessed | tf_op | source)
XLA Modules:
  0.0 495.1 jit_solution(5491051960017484969)
XLA Ops:
  2.0 1.3 collective-permute-start
  3.3 6.5 %collective-permute-start.3 = (f32[1,8,128]{2,1,0:T(8,128)S(1)}, f32[1,8,128]{2,1,0:T(8,128)S(1)}, u32[]{:S(2)}, u32[]{:S(2)}) collective-permute-start(f32[1,8,128]{2,1,0:T(8,128)S(1)} %get-tuple-element.64), channel_id=1, source_target_pairs={{0,16},{16,32},{32,48},{48,64},{64,80},{80,96},{96,112},{112,128},... | collective-permute-start | bytes 12296 | tf_op jit(solution)/shard_map/ppermute | solution.py:30
  9.8 1.0 multiply_add_fusion.1
  10.9 4.9 collective-permute-start.1
  15.8 4.2 collective-permute-start.2
  20.1 8.3 %collective-permute-start.4 = (f32[10,1,128]{2,1,0:T(1,128)S(1)}, f32[10,1,128]{2,1,0:T(1,128)S(1)}, u32[]{:S(2)}, u32[]{:S(2)}) collective-permute-start(f32[10,1,128]{2,1,0:T(1,128)S(1)} %get-tuple-element.84), channel_id=1, source_target_pairs={{1,0},{2,1},{3,2},{4,3},{5,4},{6,5},{7,6},{8,7},{9,8},{10,9},{11,1... | collective-permute-start | bytes 15368 | tf_op jit(solution)/shard_map/ppermute | solution.py:32
  28.4 1.9 collective-permute-start.5
  30.6 0.9 collective-permute-done.5
  31.7 1.3 collective-permute-start.6
  33.0 4.0 collective-permute-start.7
  37.1 0.7 collective-permute-done.7
  37.8 3.2 collective-permute-start.8
  41.0 3.6 collective-permute-start.9
  44.7 0.7 collective-permute-done.9
  45.7 1.3 collective-permute-start.10
  47.0 4.5 collective-permute-start.11
  51.5 0.7 collective-permute-done.11
  52.3 1.9 collective-permute-start.12
  54.2 5.0 %collective-permute-start.13 = (f32[10,1,128]{2,1,0:T(1,128)S(1)}, f32[10,1,128]{2,1,0:T(1,128)S(1)}, u32[]{:S(2)}, u32[]{:S(2)}) collective-permute-start(f32[10,1,128]{2,1,0:T(1,128)S(1)} %get-tuple-element.79), channel_id=1, source_target_pairs={{0,1},{1,2},{2,3},{3,4},{4,5},{5,6},{6,7},{7,8},{8,9},{9,10},{10,1... | collective-permute-start | bytes 15368 | tf_op jit(solution)/shard_map/ppermute | solution.py:30
  59.2 0.7 collective-permute-done.13
  60.2 1.3 collective-permute-start.14
  61.5 4.5 collective-permute-start.15
  66.1 0.7 collective-permute-done.15
  66.8 1.9 collective-permute-start.16
  68.8 5.0 %collective-permute-start.17 = (f32[10,1,128]{2,1,0:T(1,128)S(1)}, f32[10,1,128]{2,1,0:T(1,128)S(1)}, u32[]{:S(2)}, u32[]{:S(2)}) collective-permute-start(f32[10,1,128]{2,1,0:T(1,128)S(1)} %get-tuple-element.77), channel_id=1, source_target_pairs={{0,1},{1,2},{2,3},{3,4},{4,5},{5,6},{6,7},{7,8},{8,9},{9,10},{10,1... | collective-permute-start | bytes 15368 | tf_op jit(solution)/shard_map/ppermute | solution.py:30
  73.8 0.7 collective-permute-done.17
  74.8 1.3 collective-permute-start.18
  76.1 4.5 collective-permute-start.19
  80.7 0.7 collective-permute-done.19
  81.4 1.9 collective-permute-start.20
  83.3 5.0 %collective-permute-start.21 = (f32[10,1,128]{2,1,0:T(1,128)S(1)}, f32[10,1,128]{2,1,0:T(1,128)S(1)}, u32[]{:S(2)}, u32[]{:S(2)}) collective-permute-start(f32[10,1,128]{2,1,0:T(1,128)S(1)} %get-tuple-element.75), channel_id=1, source_target_pairs={{0,1},{1,2},{2,3},{3,4},{4,5},{5,6},{6,7},{7,8},{8,9},{9,10},{10,1... | collective-permute-start | bytes 15368 | tf_op jit(solution)/shard_map/ppermute | solution.py:30
  88.4 0.7 collective-permute-done.21
  89.4 1.3 collective-permute-start.22
  90.7 5.6 %collective-permute-start.23 = (f32[1,8,128]{2,1,0:T(8,128)S(1)}, f32[1,8,128]{2,1,0:T(8,128)S(1)}, u32[]{:S(2)}, u32[]{:S(2)}) collective-permute-start(f32[1,8,128]{2,1,0:T(8,128)S(1)} %get-tuple-element.89), channel_id=1, source_target_pairs={{0,16},{16,32},{32,48},{48,64},{64,80},{80,96},{96,112},{112,128},... | collective-permute-start | bytes 12296 | tf_op jit(solution)/shard_map/ppermute | solution.py:30
  96.3 0.7 collective-permute-done.23
  97.1 1.9 collective-permute-start.24
  99.0 5.0 %collective-permute-start.25 = (f32[10,1,128]{2,1,0:T(1,128)S(1)}, f32[10,1,128]{2,1,0:T(1,128)S(1)}, u32[]{:S(2)}, u32[]{:S(2)}) collective-permute-start(f32[10,1,128]{2,1,0:T(1,128)S(1)} %get-tuple-element.73), channel_id=1, source_target_pairs={{0,1},{1,2},{2,3},{3,4},{4,5},{5,6},{6,7},{7,8},{8,9},{9,10},{10,1... | collective-permute-start | bytes 15368 | tf_op jit(solution)/shard_map/ppermute | solution.py:30
  104.0 0.7 collective-permute-done.25
  105.0 1.3 collective-permute-start.26
  106.3 5.7 %collective-permute-start.27 = (f32[1,8,128]{2,1,0:T(8,128)S(1)}, f32[1,8,128]{2,1,0:T(8,128)S(1)}, u32[]{:S(2)}, u32[]{:S(2)}) collective-permute-start(f32[1,8,128]{2,1,0:T(8,128)S(1)} %get-tuple-element.87), channel_id=1, source_target_pairs={{0,16},{16,32},{32,48},{48,64},{64,80},{80,96},{96,112},{112,128},... | collective-permute-start | bytes 12296 | tf_op jit(solution)/shard_map/ppermute | solution.py:30
  112.1 0.7 collective-permute-done.27
  112.8 1.9 collective-permute-start.28
  114.8 5.0 %collective-permute-start.29 = (f32[10,1,128]{2,1,0:T(1,128)S(1)}, f32[10,1,128]{2,1,0:T(1,128)S(1)}, u32[]{:S(2)}, u32[]{:S(2)}) collective-permute-start(f32[10,1,128]{2,1,0:T(1,128)S(1)} %get-tuple-element.71), channel_id=1, source_target_pairs={{0,1},{1,2},{2,3},{3,4},{4,5},{5,6},{6,7},{7,8},{8,9},{9,10},{10,1... | collective-permute-start | bytes 15368 | tf_op jit(solution)/shard_map/ppermute | solution.py:30
  120.8 1.3 collective-permute-start.30
  122.1 5.7 %collective-permute-start.31 = (f32[1,8,128]{2,1,0:T(8,128)S(1)}, f32[1,8,128]{2,1,0:T(8,128)S(1)}, u32[]{:S(2)}, u32[]{:S(2)}) collective-permute-start(f32[1,8,128]{2,1,0:T(8,128)S(1)} %get-tuple-element.85), channel_id=1, source_target_pairs={{0,16},{16,32},{32,48},{48,64},{64,80},{80,96},{96,112},{112,128},... | collective-permute-start | bytes 12296 | tf_op jit(solution)/shard_map/ppermute | solution.py:30
  128.6 1.9 collective-permute-start.32
  130.6 5.0 %collective-permute-start.33 = (f32[10,1,128]{2,1,0:T(1,128)S(1)}, f32[10,1,128]{2,1,0:T(1,128)S(1)}, u32[]{:S(2)}, u32[]{:S(2)}) collective-permute-start(f32[10,1,128]{2,1,0:T(1,128)S(1)} %get-tuple-element.69), channel_id=1, source_target_pairs={{0,1},{1,2},{2,3},{3,4},{4,5},{5,6},{6,7},{7,8},{8,9},{9,10},{10,1... | collective-permute-start | bytes 15368 | tf_op jit(solution)/shard_map/ppermute | solution.py:30
  135.6 0.7 collective-permute-done.33
  137.0 0.8 convolution_bitcast_fusion.1
  137.8 152.9 %psum.14 = f32[9,9]{0,1:T(8,128)S(1)} all-reduce(f32[9,9]{0,1:T(8,128)S(1)} %convolution_bitcast_fusion.1), channel_id=1, replica_groups=mesh['gx'=64,'gz'=16] {'gx','gz'}, use_global_device_ids=true, to_apply=%region_0.1 | all-reduce | flops 81 | bytes 648 | tf_op jit(solution)/shard_map/psum | solution.py:107
  290.8 0.8 cholesky.44
  293.0 0.7 fusion.185
  295.1 28.2 %subtract_divide_fusion.15 = (f32[1,9]{1,0:T(1,128)S(1)}, f32[1,9]{1,0:T(1,128)S(1)}, f32[1,9]{1,0:T(1,128)S(1)}, f32[1,9]{1,0:T(1,128)S(1)}, f32[1,9]{1,0:T(1,1...) fusion(f32[9,9]{1,0:T(8,128)S(1)} %fusion.158, f32[]{:T(128)} %bitcast.78, ...), kind=kLoop, calls=%fused_computation.346 | loop fusion | flops 729 | bytes 828 | tf_op jit(solution)/shard_map/div | solution.py:71
  323.9 0.8 convolution_bitcast_fusion
  324.7 109.4 %psum.15 = f32[9,9]{0,1:T(8,128)S(1)} all-reduce(f32[9,9]{0,1:T(8,128)S(1)} %convolution_bitcast_fusion), channel_id=1, replica_groups=mesh['gx'=64,'gz'=16] {'gx','gz'}, use_global_device_ids=true, to_apply=%region_3.5 | all-reduce | flops 81 | bytes 648 | tf_op jit(solution)/shard_map/psum | solution.py:107
  434.2 0.8 cholesky.55
  435.7 2.1 broadcast_multiply_fusion.1
  437.8 0.7 fusion.179
  438.6 0.7 fusion.180
  439.9 0.7 fusion.182
  442.2 28.1 %subtract_divide_fusion.7 = (f32[1,9]{1,0:T(1,128)S(1)}, f32[1,9]{1,0:T(1,128)S(1)}, f32[1,9]{1,0:T(1,128)S(1)}, f32[1,9]{1,0:T(1,128)S(1)}, f32[1,9]{1,0:T(1,12...) fusion(f32[9,9]{1,0:T(8,128)S(1)} %fusion.158, f32[]{:T(128)} %bitcast.127, ...), kind=kLoop, calls=%fused_computation.338 | loop fusion | flops 729 | bytes 828 | tf_op jit(solution)/shard_map/div | solution.py:71
  470.9 0.8 copy.56
  471.7 22.5 %subtract_divide_fusion = (f32[1,8]{1,0:T(1,128)S(1)}, f32[1,8]{1,0:T(1,128)S(1)}, f32[1,8]{1,0:T(1,128)S(1)}, f32[1,8]{1,0:T(1,128)S(1)}, f32[1,8]{1,0:T(1,128)...) fusion(f32[8,8]{1,0:T(8,128)S(1)} %fusion.165, f32[]{:T(128)} %bitcast.164, f32[]{:T(128)} %bitcast.163, ...), kind=kLoop, calls=%fused_computation.330 | loop fusion | flops 512 | bytes 656 | tf_op jit(solution)/shard_map/div | solution.py:71
  494.3 0.8 fusion.188
  (89 shorter events, 12.0 us)
Async XLA Ops:
  2.0 18.1 %collective-permute-start = (f32[1,8,128]{2,1,0:T(8,128)S(1)}, f32[1,8,128]{2,1,0:T(8,128)S(1)}, u32[]{:S(2)}, u32[]{:S(2)}) collective-permute-start(f32[1,8,128]{2,1,0:T(8,128)S(1)} %get-tuple-element.65), channel_id=1, source_target_pairs={{16,0},{32,16},{48,32},{64,48},{80,64},{96,80},{112,96},{128,112},... | collective-permute-start | bytes 12296 | tf_op jit(solution)/shard_map/ppermute | solution.py:32
  3.3 16.8 %copy-start = (f32[4,8,8,128]{3,2,1,0:T(8,128)S(1)}, f32[4,8,8,128]{3,2,1,0:T(8,128)}, u32[]{:S(2)}) copy-start(f32[4,8,8,128]{3,2,1,0:T(8,128)} %param.11) | copy-start | bytes 393220
  3.3 16.8 %collective-permute-start.3 = (f32[1,8,128]{2,1,0:T(8,128)S(1)}, f32[1,8,128]{2,1,0:T(8,128)S(1)}, u32[]{:S(2)}, u32[]{:S(2)}) collective-permute-start(f32[1,8,128]{2,1,0:T(8,128)S(1)} %get-tuple-element.64), channel_id=1, source_target_pairs={{0,16},{16,32},{32,48},{48,64},{64,80},{80,96},{96,112},{112,128},... | collective-permute-start | bytes 12296 | tf_op jit(solution)/shard_map/ppermute | solution.py:30
  10.9 19.5 %collective-permute-start.1 = (f32[8,128]{1,0:T(8,128)S(1)}, f32[8,128]{1,0:T(8,128)S(1)}, u32[]{:S(2)}, u32[]{:S(2)}) collective-permute-start(f32[8,128]{1,0:T(8,128)S(1)} %bitcast.297), channel_id=1, source_target_pairs={{0,16},{16,32},{32,48},{48,64},{64,80},{80,96},{96,112},{112,128},... | collective-permute-start | bytes 12296 | tf_op jit(solution)/shard_map/ppermute | solution.py:19
  15.8 14.7 %collective-permute-start.2 = (f32[8,128]{1,0:T(8,128)S(1)}, f32[8,128]{1,0:T(8,128)S(1)}, u32[]{:S(2)}, u32[]{:S(2)}) collective-permute-start(f32[8,128]{1,0:T(8,128)S(1)} %slice_bitcast_fusion.2), channel_id=1, source_target_pairs={{0,1},{1,2},{2,3},{3,4},{4,5},{5,6},{6,7},{7,8},{8,9},{9,10},{10,1... | collective-permute-start | bytes 12296 | tf_op jit(solution)/shard_map/ppermute | solution.py:19
  20.1 10.5 %collective-permute-start.4 = (f32[10,1,128]{2,1,0:T(1,128)S(1)}, f32[10,1,128]{2,1,0:T(1,128)S(1)}, u32[]{:S(2)}, u32[]{:S(2)}) collective-permute-start(f32[10,1,128]{2,1,0:T(1,128)S(1)} %get-tuple-element.84), channel_id=1, source_target_pairs={{1,0},{2,1},{3,2},{4,3},{5,4},{6,5},{7,6},{8,7},{9,8},{10,9},{11,1... | collective-permute-start | bytes 15368 | tf_op jit(solution)/shard_map/ppermute | solution.py:32
  28.4 3.1 collective-permute-start.5
  31.7 5.3 %collective-permute-start.6 = (f32[1,8,128]{2,1,0:T(8,128)S(1)}, f32[1,8,128]{2,1,0:T(8,128)S(1)}, u32[]{:S(2)}, u32[]{:S(2)}) collective-permute-start(f32[1,8,128]{2,1,0:T(8,128)S(1)} %get-tuple-element.98), channel_id=1, source_target_pairs={{16,0},{32,16},{48,32},{64,48},{80,64},{96,80},{112,96},{128,112},... | collective-permute-start | bytes 12296 | tf_op jit(solution)/shard_map/ppermute | solution.py:32
  33.0 4.7 collective-permute-start.7
  37.8 6.9 %collective-permute-start.8 = (f32[10,1,128]{2,1,0:T(1,128)S(1)}, f32[10,1,128]{2,1,0:T(1,128)S(1)}, u32[]{:S(2)}, u32[]{:S(2)}) collective-permute-start(f32[10,1,128]{2,1,0:T(1,128)S(1)} %get-tuple-element.82), channel_id=1, source_target_pairs={{1,0},{2,1},{3,2},{4,3},{5,4},{6,5},{7,6},{8,7},{9,8},{10,9},{11,1... | collective-permute-start | bytes 15368 | tf_op jit(solution)/shard_map/ppermute | solution.py:32
  41.0 4.4 collective-permute-start.9
  45.7 5.8 %collective-permute-start.10 = (f32[1,8,128]{2,1,0:T(8,128)S(1)}, f32[1,8,128]{2,1,0:T(8,128)S(1)}, u32[]{:S(2)}, u32[]{:S(2)}) collective-permute-start(f32[1,8,128]{2,1,0:T(8,128)S(1)} %get-tuple-element.96), channel_id=1, source_target_pairs={{16,0},{32,16},{48,32},{64,48},{80,64},{96,80},{112,96},{128,112},... | collective-permute-start | bytes 12296 | tf_op jit(solution)/shard_map/ppermute | solution.py:32
  47.0 5.3 %collective-permute-start.11 = (f32[1,8,128]{2,1,0:T(8,128)S(1)}, f32[1,8,128]{2,1,0:T(8,128)S(1)}, u32[]{:S(2)}, u32[]{:S(2)}) collective-permute-start(f32[1,8,128]{2,1,0:T(8,128)S(1)} %get-tuple-element.95), channel_id=1, source_target_pairs={{0,16},{16,32},{32,48},{48,64},{64,80},{80,96},{96,112},{112,128},... | collective-permute-start | bytes 12296 | tf_op jit(solution)/shard_map/ppermute | solution.py:30
  52.3 7.0 %collective-permute-start.12 = (f32[10,1,128]{2,1,0:T(1,128)S(1)}, f32[10,1,128]{2,1,0:T(1,128)S(1)}, u32[]{:S(2)}, u32[]{:S(2)}) collective-permute-start(f32[10,1,128]{2,1,0:T(1,128)S(1)} %get-tuple-element.80), channel_id=1, source_target_pairs={{1,0},{2,1},{3,2},{4,3},{5,4},{6,5},{7,6},{8,7},{9,8},{10,9},{11,1... | collective-permute-start | bytes 15368 | tf_op jit(solution)/shard_map/ppermute | solution.py:32
  54.2 5.8 %collective-permute-start.13 = (f32[10,1,128]{2,1,0:T(1,128)S(1)}, f32[10,1,128]{2,1,0:T(1,128)S(1)}, u32[]{:S(2)}, u32[]{:S(2)}) collective-permute-start(f32[10,1,128]{2,1,0:T(1,128)S(1)} %get-tuple-element.79), channel_id=1, source_target_pairs={{0,1},{1,2},{2,3},{3,4},{4,5},{5,6},{6,7},{7,8},{8,9},{9,10},{10,1... | collective-permute-start | bytes 15368 | tf_op jit(solution)/shard_map/ppermute | solution.py:30
  60.2 5.8 %collective-permute-start.14 = (f32[1,8,128]{2,1,0:T(8,128)S(1)}, f32[1,8,128]{2,1,0:T(8,128)S(1)}, u32[]{:S(2)}, u32[]{:S(2)}) collective-permute-start(f32[1,8,128]{2,1,0:T(8,128)S(1)} %get-tuple-element.94), channel_id=1, source_target_pairs={{16,0},{32,16},{48,32},{64,48},{80,64},{96,80},{112,96},{128,112},... | collective-permute-start | bytes 12296 | tf_op jit(solution)/shard_map/ppermute | solution.py:32
  61.5 5.3 %collective-permute-start.15 = (f32[1,8,128]{2,1,0:T(8,128)S(1)}, f32[1,8,128]{2,1,0:T(8,128)S(1)}, u32[]{:S(2)}, u32[]{:S(2)}) collective-permute-start(f32[1,8,128]{2,1,0:T(8,128)S(1)} %get-tuple-element.93), channel_id=1, source_target_pairs={{0,16},{16,32},{32,48},{48,64},{64,80},{80,96},{96,112},{112,128},... | collective-permute-start | bytes 12296 | tf_op jit(solution)/shard_map/ppermute | solution.py:30
  66.8 7.0 %collective-permute-start.16 = (f32[10,1,128]{2,1,0:T(1,128)S(1)}, f32[10,1,128]{2,1,0:T(1,128)S(1)}, u32[]{:S(2)}, u32[]{:S(2)}) collective-permute-start(f32[10,1,128]{2,1,0:T(1,128)S(1)} %get-tuple-element.78), channel_id=1, source_target_pairs={{1,0},{2,1},{3,2},{4,3},{5,4},{6,5},{7,6},{8,7},{9,8},{10,9},{11,1... | collective-permute-start | bytes 15368 | tf_op jit(solution)/shard_map/ppermute | solution.py:32
  68.8 5.8 %collective-permute-start.17 = (f32[10,1,128]{2,1,0:T(1,128)S(1)}, f32[10,1,128]{2,1,0:T(1,128)S(1)}, u32[]{:S(2)}, u32[]{:S(2)}) collective-permute-start(f32[10,1,128]{2,1,0:T(1,128)S(1)} %get-tuple-element.77), channel_id=1, source_target_pairs={{0,1},{1,2},{2,3},{3,4},{4,5},{5,6},{6,7},{7,8},{8,9},{9,10},{10,1... | collective-permute-start | bytes 15368 | tf_op jit(solution)/shard_map/ppermute | solution.py:30
  74.8 5.8 %collective-permute-start.18 = (f32[1,8,128]{2,1,0:T(8,128)S(1)}, f32[1,8,128]{2,1,0:T(8,128)S(1)}, u32[]{:S(2)}, u32[]{:S(2)}) collective-permute-start(f32[1,8,128]{2,1,0:T(8,128)S(1)} %get-tuple-element.92), channel_id=1, source_target_pairs={{16,0},{32,16},{48,32},{64,48},{80,64},{96,80},{112,96},{128,112},... | collective-permute-start | bytes 12296 | tf_op jit(solution)/shard_map/ppermute | solution.py:32
  76.1 5.3 %collective-permute-start.19 = (f32[1,8,128]{2,1,0:T(8,128)S(1)}, f32[1,8,128]{2,1,0:T(8,128)S(1)}, u32[]{:S(2)}, u32[]{:S(2)}) collective-permute-start(f32[1,8,128]{2,1,0:T(8,128)S(1)} %get-tuple-element.91), channel_id=1, source_target_pairs={{0,16},{16,32},{32,48},{48,64},{64,80},{80,96},{96,112},{112,128},... | collective-permute-start | bytes 12296 | tf_op jit(solution)/shard_map/ppermute | solution.py:30
  81.4 7.0 %collective-permute-start.20 = (f32[10,1,128]{2,1,0:T(1,128)S(1)}, f32[10,1,128]{2,1,0:T(1,128)S(1)}, u32[]{:S(2)}, u32[]{:S(2)}) collective-permute-start(f32[10,1,128]{2,1,0:T(1,128)S(1)} %get-tuple-element.76), channel_id=1, source_target_pairs={{1,0},{2,1},{3,2},{4,3},{5,4},{6,5},{7,6},{8,7},{9,8},{10,9},{11,1... | collective-permute-start | bytes 15368 | tf_op jit(solution)/shard_map/ppermute | solution.py:32
  83.3 5.8 %collective-permute-start.21 = (f32[10,1,128]{2,1,0:T(1,128)S(1)}, f32[10,1,128]{2,1,0:T(1,128)S(1)}, u32[]{:S(2)}, u32[]{:S(2)}) collective-permute-start(f32[10,1,128]{2,1,0:T(1,128)S(1)} %get-tuple-element.75), channel_id=1, source_target_pairs={{0,1},{1,2},{2,3},{3,4},{4,5},{5,6},{6,7},{7,8},{8,9},{9,10},{10,1... | collective-permute-start | bytes 15368 | tf_op jit(solution)/shard_map/ppermute | solution.py:30
  89.4 6.9 %collective-permute-start.22 = (f32[1,8,128]{2,1,0:T(8,128)S(1)}, f32[1,8,128]{2,1,0:T(8,128)S(1)}, u32[]{:S(2)}, u32[]{:S(2)}) collective-permute-start(f32[1,8,128]{2,1,0:T(8,128)S(1)} %get-tuple-element.90), channel_id=1, source_target_pairs={{16,0},{32,16},{48,32},{64,48},{80,64},{96,80},{112,96},{128,112},... | collective-permute-start | bytes 12296 | tf_op jit(solution)/shard_map/ppermute | solution.py:32
  90.7 6.3 %collective-permute-start.23 = (f32[1,8,128]{2,1,0:T(8,128)S(1)}, f32[1,8,128]{2,1,0:T(8,128)S(1)}, u32[]{:S(2)}, u32[]{:S(2)}) collective-permute-start(f32[1,8,128]{2,1,0:T(8,128)S(1)} %get-tuple-element.89), channel_id=1, source_target_pairs={{0,16},{16,32},{32,48},{48,64},{64,80},{80,96},{96,112},{112,128},... | collective-permute-start | bytes 12296 | tf_op jit(solution)/shard_map/ppermute | solution.py:30
  97.1 7.0 %collective-permute-start.24 = (f32[10,1,128]{2,1,0:T(1,128)S(1)}, f32[10,1,128]{2,1,0:T(1,128)S(1)}, u32[]{:S(2)}, u32[]{:S(2)}) collective-permute-start(f32[10,1,128]{2,1,0:T(1,128)S(1)} %get-tuple-element.74), channel_id=1, source_target_pairs={{1,0},{2,1},{3,2},{4,3},{5,4},{6,5},{7,6},{8,7},{9,8},{10,9},{11,1... | collective-permute-start | bytes 15368 | tf_op jit(solution)/shard_map/ppermute | solution.py:32
  99.0 5.8 %collective-permute-start.25 = (f32[10,1,128]{2,1,0:T(1,128)S(1)}, f32[10,1,128]{2,1,0:T(1,128)S(1)}, u32[]{:S(2)}, u32[]{:S(2)}) collective-permute-start(f32[10,1,128]{2,1,0:T(1,128)S(1)} %get-tuple-element.73), channel_id=1, source_target_pairs={{0,1},{1,2},{2,3},{3,4},{4,5},{5,6},{6,7},{7,8},{8,9},{9,10},{10,1... | collective-permute-start | bytes 15368 | tf_op jit(solution)/shard_map/ppermute | solution.py:30
  105.0 7.1 %collective-permute-start.26 = (f32[1,8,128]{2,1,0:T(8,128)S(1)}, f32[1,8,128]{2,1,0:T(8,128)S(1)}, u32[]{:S(2)}, u32[]{:S(2)}) collective-permute-start(f32[1,8,128]{2,1,0:T(8,128)S(1)} %get-tuple-element.88), channel_id=1, source_target_pairs={{16,0},{32,16},{48,32},{64,48},{80,64},{96,80},{112,96},{128,112},... | collective-permute-start | bytes 12296 | tf_op jit(solution)/shard_map/ppermute | solution.py:32
  106.3 6.5 %collective-permute-start.27 = (f32[1,8,128]{2,1,0:T(8,128)S(1)}, f32[1,8,128]{2,1,0:T(8,128)S(1)}, u32[]{:S(2)}, u32[]{:S(2)}) collective-permute-start(f32[1,8,128]{2,1,0:T(8,128)S(1)} %get-tuple-element.87), channel_id=1, source_target_pairs={{0,16},{16,32},{32,48},{48,64},{64,80},{80,96},{96,112},{112,128},... | collective-permute-start | bytes 12296 | tf_op jit(solution)/shard_map/ppermute | solution.py:30
  112.8 7.0 %collective-permute-start.28 = (f32[10,1,128]{2,1,0:T(1,128)S(1)}, f32[10,1,128]{2,1,0:T(1,128)S(1)}, u32[]{:S(2)}, u32[]{:S(2)}) collective-permute-start(f32[10,1,128]{2,1,0:T(1,128)S(1)} %get-tuple-element.72), channel_id=1, source_target_pairs={{1,0},{2,1},{3,2},{4,3},{5,4},{6,5},{7,6},{8,7},{9,8},{10,9},{11,1... | collective-permute-start | bytes 15368 | tf_op jit(solution)/shard_map/ppermute | solution.py:32
  114.8 5.8 %collective-permute-start.29 = (f32[10,1,128]{2,1,0:T(1,128)S(1)}, f32[10,1,128]{2,1,0:T(1,128)S(1)}, u32[]{:S(2)}, u32[]{:S(2)}) collective-permute-start(f32[10,1,128]{2,1,0:T(1,128)S(1)} %get-tuple-element.71), channel_id=1, source_target_pairs={{0,1},{1,2},{2,3},{3,4},{4,5},{5,6},{6,7},{7,8},{8,9},{9,10},{10,1... | collective-permute-start | bytes 15368 | tf_op jit(solution)/shard_map/ppermute | solution.py:30
  120.8 7.1 %collective-permute-start.30 = (f32[1,8,128]{2,1,0:T(8,128)S(1)}, f32[1,8,128]{2,1,0:T(8,128)S(1)}, u32[]{:S(2)}, u32[]{:S(2)}) collective-permute-start(f32[1,8,128]{2,1,0:T(8,128)S(1)} %get-tuple-element.86), channel_id=1, source_target_pairs={{16,0},{32,16},{48,32},{64,48},{80,64},{96,80},{112,96},{128,112},... | collective-permute-start | bytes 12296 | tf_op jit(solution)/shard_map/ppermute | solution.py:32
  122.1 6.5 %collective-permute-start.31 = (f32[1,8,128]{2,1,0:T(8,128)S(1)}, f32[1,8,128]{2,1,0:T(8,128)S(1)}, u32[]{:S(2)}, u32[]{:S(2)}) collective-permute-start(f32[1,8,128]{2,1,0:T(8,128)S(1)} %get-tuple-element.85), channel_id=1, source_target_pairs={{0,16},{16,32},{32,48},{48,64},{64,80},{80,96},{96,112},{112,128},... | collective-permute-start | bytes 12296 | tf_op jit(solution)/shard_map/ppermute | solution.py:30
  128.6 7.0 %collective-permute-start.32 = (f32[10,1,128]{2,1,0:T(1,128)S(1)}, f32[10,1,128]{2,1,0:T(1,128)S(1)}, u32[]{:S(2)}, u32[]{:S(2)}) collective-permute-start(f32[10,1,128]{2,1,0:T(1,128)S(1)} %get-tuple-element.70), channel_id=1, source_target_pairs={{1,0},{2,1},{3,2},{4,3},{5,4},{6,5},{7,6},{8,7},{9,8},{10,9},{11,1... | collective-permute-start | bytes 15368 | tf_op jit(solution)/shard_map/ppermute | solution.py:32
  130.6 5.8 %collective-permute-start.33 = (f32[10,1,128]{2,1,0:T(1,128)S(1)}, f32[10,1,128]{2,1,0:T(1,128)S(1)}, u32[]{:S(2)}, u32[]{:S(2)}) collective-permute-start(f32[10,1,128]{2,1,0:T(1,128)S(1)} %get-tuple-element.69), channel_id=1, source_target_pairs={{0,1},{1,2},{2,3},{3,4},{4,5},{5,6},{6,7},{7,8},{8,9},{9,10},{10,1... | collective-permute-start | bytes 15368 | tf_op jit(solution)/shard_map/ppermute | solution.py:30
  435.0 7.0 %copy-start.1 = (f32[9,8]{1,0:T(8,128)S(1)}, f32[9,8]{1,0:T(8,128)}, u32[]{:S(2)}) copy-start(f32[9,8]{1,0:T(8,128)} %constant.134.clone) | copy-start | bytes 868
where the time goes:
time: 499 us; the launch traced here: 495 us
  blocking collectives  262 us (53%)
  starting transfers between devices  119 us (24%)
  other arithmetic  86.2 us (17%)
  waiting for transfers between devices  11.1 us (2%)
  local copies, waits for them, and re-layouts  8.11 us (2%)
  matrix products  5.87 us (1%)
    psum x2, blocking collectives, global_gram(): return lax.psum(gram_of(block), ('gx', 'gz'))  262 us
    div x3, other arithmetic, upper_inverse(): rows[row_index] = remainder / upper[row_index, row_index]  78.8 us
    ppermute x16, starting transfers between devices, extended_2(): lax.ppermute(tail, axis, [(i, (i + 1) % count) for i in range(ends)])  77 us
    ppermute x16, starting transfers between devices, extended_2(): lax.ppermute(head, axis, [((i + 1) % count, i) for i in range(ends)])  33.3 us
    ppermute x16, waiting for transfers between devices, extended_2(): lax.ppermute(tail, axis, [(i, (i + 1) % count) for i in range(ends)])  11.1 us
  transfers between devices with their start and end apart: 34, of which 15 were waited for; matrix products, arithmetic and copies ran while one was open for 0% of the time, Pallas kernels for 0%

commit v1 on v0

v1 whole, which is shorter than its diff:
```python
import math

import jax
import jax.numpy as jnp
from jax import lax
from jax.experimental import pallas as pl
from jax.experimental.pallas import tpu as pltpu
from jax.sharding import PartitionSpec as P

S = 8
COLS = S + 1
CENTER = 2.5
HALF = 1.5
B = 8
WIDE = 3 * B
LANES = 128
FIELDS = 7
F32 = jnp.float32
VMEM = pl.BlockSpec(memory_space=pltpu.VMEM)
SMEM = pl.BlockSpec(memory_space=pltpu.SMEM)
PARAMS = pltpu.CompilerParams(vmem_limit_bytes=16 * 1024 * 1024)


def iota(shape, dim):
    return lax.broadcasted_iota(jnp.int32, shape, dim)


def two_sum(a, b):
    s = a + b
    t = s - a
    return s, (a - (s - t)) + (b - t)


def fast_two_sum(a, b):
    s = a + b
    return s, b - (s - a)


def split(a):
    c = a * 4097.0
    high = c - (c - a)
    return high, a - high


def two_prod(a, b):
    ah, al = split(a)
    bh, bl = split(b)
    p = a * b
    return p, ((ah * bh - p) + (ah * bl + al * bh)) + al * bl


def pair_add(a, b):
    s, e = two_sum(a[0], b[0])
    return fast_two_sum(s, e + (a[1] + b[1]))


def pair_mul(a, b):
    p, e = two_prod(a[0], b[0])
    return fast_two_sum(p, e + (a[0] * b[1] + a[1] * b[0]))


def pair_roll(a, shift, axis):
    return tuple(pltpu.roll(part, shift, axis) for part in a)


def pair_where(mask, a, b):
    return tuple(jnp.where(mask, x, y) for x, y in zip(a, b))


def pack_kernel(column, basis, diffusivity, speed, upwind, out):
    out[0] = basis[column[0]]
    factor = -2.0 / HALF
    for dim in range(3):
        flow = upwind[dim].astype(F32)
        out[1 + dim] = (diffusivity[dim] + speed[dim] * flow) * factor
        out[4 + dim] = (diffusivity[dim] + speed[dim] * (1.0 - flow)) * factor


def side_kernel(own, below, above, to_next, to_last):
    row = iota((FIELDS, B, LANES), 1)
    to_next[:, 0:B] = own[...]
    to_last[:, 0:B] = own[...]
    for side in range(2):
        layer = (lambda m: below[:, B - m]) if side == 0 else (lambda m: above[:, m - 1])
        for m in range(1, 5):
            near = layer(m)
            at = B + 4 * side + m - 1
            if m == 4:
                to_next[:, at] = near
                to_last[:, at] = near
            else:
                far = layer(B - m)
                to_next[:, at] = jnp.where(row >= m, near, pltpu.roll(far, m, 1))
                to_last[:, at] = jnp.where(row < B - m, near, pltpu.roll(far, B - m, 1))


def basis_kernel(own, below, above, last, following, block, gram, coeff, field, high, low):
    def wide(f, a):
        if B <= a < 2 * B:
            return jnp.concatenate([last[f, a - B], own[f, a - B], following[f, a - B]], 0)
        side = 0 if a < B else 1
        m = B - a if side == 0 else a - (2 * B - 1)
        middle = below[f, a] if side == 0 else above[f, a - 2 * B]
        if m == B:
            lower = upper = jnp.zeros((B, LANES), F32)
        elif m <= 4:
            at = B + 4 * side + m - 1
            lower, upper = last[f, at], following[f, at]
        else:
            other = B - m
            at = B + 4 * side + other - 1
            lower = pltpu.roll(last[f, at], B - other, 0)
            upper = pltpu.roll(following[f, at], other, 0)
        return jnp.concatenate([lower, middle, upper], 0)

    lane = iota((WIDE, LANES), 1)
    zero = jnp.zeros((WIDE, LANES), F32)
    q_below = wide(4, 0)
    field[0, 0] = wide(0, 0)
    field[0, WIDE - 1] = wide(0, WIDE - 1)
    for a in range(1, WIDE - 1):
        field[0, a] = wide(0, a)
        p = [wide(1 + dim, a) for dim in range(3)]
        q = [wide(4 + dim, a) for dim in range(3)]
        inside = p[0] < 0.0
        qx = jnp.where(inside, q_below, zero)
        qy = jnp.where(inside, pltpu.roll(q[1], 1, 0), zero)
        qz = jnp.where(lane == 0, zero, pltpu.roll(q[2], 1, 1))
        q_below = q[0]
        coeff[0, a] = (-2.0 * (CENTER - 1.0) / HALF) - ((p[0] + p[1]) + (p[2] + qx) + (qy + qz))
        coeff[1, a] = p[0]
        coeff[2, a] = qx
        coeff[3, a] = p[1]
        coeff[4, a] = qy
        coeff[5, a] = jnp.where(lane == LANES - 1, zero, p[2])
        coeff[6, a] = qz

    block[0] = own[0]
    for k in range(1, COLS):
        src, dst = (k - 1) % 2, k % 2

        def layer(a, carry, k=k, src=src, dst=dst):
            v = field[src, a]
            x = coeff[0, a] * v + coeff[1, a] * field[src, a + 1] + coeff[2, a] * field[src, a - 1]
            y = coeff[3, a] * pltpu.roll(v, WIDE - 1, 0) + coeff[4, a] * pltpu.roll(v, 1, 0)
            z = coeff[5, a] * pltpu.roll(v, LANES - 1, 1) + coeff[6, a] * pltpu.roll(v, 1, 1)
            total = x + (y + z)
            new = 0.5 * total if k == 1 else total - field[dst, a]
            if k == S:
                block[k, a - B] = new[B : 2 * B]
            else:
                field[dst, a] = new
            return carry

        lax.fori_loop(k, WIDE - k, layer, 0, unroll=2)
        if k < S:
            block[k] = field[dst, B : 2 * B, B : 2 * B, :]

    for k in range(COLS):
        h, l = split(block[k])
        high[k] = h
        low[k] = l

    def product(i, j):
        total = None
        for x in range(B):
            ah, al, bh, bl = high[i, x], low[i, x], high[j, x], low[j, x]
            p = block[i, x] * block[j, x]
            e = ((ah * bh - p) + (ah * bl + al * bh)) + al * bl
            if total is None:
                total, rest = p, e
            else:
                total, err = two_sum(total, p)
                rest = rest + (e + err)
        return fast_two_sum(total, rest)

    row = iota((B, LANES), 0)
    lane = iota((B, LANES), 1)
    nothing = (jnp.zeros((B, LANES), F32),) * 2

    def merged(a, b, distance, axis):
        if a is None and b is None:
            return None
        a = nothing if a is None else a
        b = nothing if b is None else b
        mask = ((row if axis == 0 else lane) & distance) == 0
        return pair_add(pair_where(mask, a, b), pair_roll(pair_where(mask, b, a), distance, axis))

    def fold(items, axis):
        distance = 1
        while len(items) > 1:
            items = [merged(items[t], items[t + 1], distance, axis) for t in range(0, len(items), 2)]
            distance *= 2
        return items[0]

    products = {(i, j): product(i, j) for i in range(COLS) for j in range(i, COLS)}
    slots = []
    for m in range(16):
        if m < COLS:
            items = [products[min(r, m), max(r, m)] for r in range(B)]
        else:
            items = [products[m - COLS, S]] + [products[m - 2, S] if m - 2 < COLS else None] + [None] * 6
        slots.append(fold(items, 0))
    table = fold(slots, 1)
    for distance in (16, 32, 64):
        table = pair_add(table, pair_roll(table, distance, 1))
    mine = lane // 16 == row
    rows = [jnp.sum(jnp.where(mine, part, 0.0), axis=0, keepdims=True) for part in table]
    tile = jnp.where(row % 2 == 0, rows[0], rows[1])
    for t in range(gram.shape[0] // B):
        gram[B * t : B * (t + 1), :] = tile


def summed(ref):
    tiles = [ref[B * t : B * (t + 1), :] for t in range(ref.shape[0] // B)]
    pairs = [(t, pltpu.roll(t, B - 1, 0)) for t in tiles]
    while len(pairs) > 1:
        pairs = [pair_add(pairs[t], pairs[t + 1]) for t in range(0, len(pairs), 2)]
    total = pairs[0]
    for distance in (2, 4):
        total = pair_add(total, pair_roll(total, distance, 0))
    return total


def sum_kernel(parts, out):
    total = summed(parts)
    row = iota((B, LANES), 0)
    tile = jnp.where(row % 2 == 0, total[0], pltpu.roll(total[1], 1, 0))
    for t in range(out.shape[0] // B):
        out[B * t : B * (t + 1), :] = tile


def factor_kernel(scale, parts, block, basis_q, factor_r, hessenberg, inverse):
    shape = (2 * B, LANES)
    row = iota(shape, 0)
    lane = iota(shape, 1)

    def matrix(part):
        line = jnp.broadcast_to(part[0:1, :], shape)
        out = jnp.zeros(shape, F32)
        for r in range(B):
            moved = line if r == 0 else pltpu.roll(line, LANES - 16 * r, 1)
            out = jnp.where((row == r) & (lane < COLS), moved, out)
        out = jnp.where((row == S) & (lane < 7), pltpu.roll(line, LANES - 9, 1), out)
        return jnp.where((row == S) & ((lane == 7) | (lane == 8)), pltpu.roll(line, LANES - 18, 1), out)

    high, low = (matrix(part) for part in summed(parts))
    high = jnp.where((lane == row + 64) & (row < COLS), 1.0, high)
    pivots = jnp.ones(shape, F32)
    for j in range(COLS):
        d = tuple(jnp.broadcast_to(part[j : j + 1, j : j + 1], shape) for part in (high, low))
        pivots = jnp.where(row == j, d[0], pivots)
        if j == S:
            break
        top = tuple(jnp.broadcast_to(part[j : j + 1, :], shape) for part in (high, low))
        col = tuple(jnp.broadcast_to(part[:, j : j + 1], shape) for part in (high, low))
        inv = 1.0 / d[0]
        ratio = col[0] * inv
        back, err = two_prod(ratio, d[0])
        rest = (((col[0] - back) - err) + (col[1] - ratio * d[1])) * inv
        ratio = fast_two_sum(ratio, rest)
        change = pair_mul(ratio, top)
        change = tuple(jnp.where(row > j, -part, 0.0) for part in change)
        high, low = pair_add((high, low), change)
    root = jnp.sqrt(pivots)
    scaled = high / root
    upper = jnp.where((lane >= row) & (lane < COLS) & (row < COLS), scaled, 0.0)
    lower = jnp.where((lane <= row) & (row < COLS), pltpu.roll(scaled, 64, 1), 0.0)
    factor_r[...] = (upper / scale)[:COLS, :COLS]
    right = pltpu.roll(upper, LANES - 1, 1)
    product = CENTER * upper + jnp.where(lane == 0, HALF, 0.5 * HALF) * right + (0.5 * HALF) * pltpu.roll(upper, 1, 1)
    product = jnp.where(lane < S, product, 0.0)
    small = lax.dot_general(
        product,
        jnp.where(lane < S, lower, 0.0),
        (((1,), (1,)), ((), ())),
        precision=lax.Precision.HIGHEST,
        preferred_element_type=F32,
    )
    hessenberg[...] = small[:COLS, :S]
    lower = lower * scale
    for k in range(COLS):
        inverse[k] = jnp.broadcast_to(lower[:, k : k + 1], shape)
    for j in range(COLS):
        total = None
        for k in range(j + 1):
            factor = jnp.broadcast_to(inverse[k, j : j + 1, :], (B, LANES))[None]
            term = factor * block[k]
            total = term if total is None else total + term
        basis_q[j] = total


def moved(array, axis, distance):
    count = lax.axis_size(axis)
    route = [(i, i + distance) for i in range(count) if 0 <= i + distance < count]
    return lax.ppermute(array, axis, route)


def body(previous_basis, restart_column, diffusivity, speed, upwind):
    count_x, count_y = lax.axis_size("gx"), lax.axis_size("gz")
    brick = (FIELDS, B, B, LANES)
    own = pl.pallas_call(
        pack_kernel,
        out_shape=jax.ShapeDtypeStruct(brick, F32),
        in_specs=[SMEM] + [VMEM] * 4,
        out_specs=VMEM,
        compiler_params=PARAMS,
        name="pack",
    )(restart_column, previous_basis, diffusivity, speed, upwind)
    below = moved(own, "gx", 1)
    above = moved(own, "gx", -1)
    sides = jax.ShapeDtypeStruct((FIELDS, 2 * B, B, LANES), F32)
    to_next, to_last = pl.pallas_call(
        side_kernel,
        out_shape=(sides, sides),
        in_specs=[VMEM] * 3,
        out_specs=(VMEM, VMEM),
        compiler_params=PARAMS,
        name="sides",
    )(own, below, above)
    last = moved(to_next, "gz", 1)
    following = moved(to_last, "gz", -1)
    wide = (WIDE, WIDE, LANES)
    block, gram = pl.pallas_call(
        basis_kernel,
        out_shape=(
            jax.ShapeDtypeStruct((COLS, B, B, LANES), F32),
            jax.ShapeDtypeStruct((2 * count_y, LANES), F32),
        ),
        in_specs=[VMEM] * 5,
        out_specs=(VMEM, VMEM),
        scratch_shapes=[
            pltpu.VMEM((FIELDS,) + wide, F32),
            pltpu.VMEM((2,) + wide, F32),
            pltpu.VMEM((COLS, B, B, LANES), F32),
            pltpu.VMEM((COLS, B, B, LANES), F32),
        ],
        compiler_params=PARAMS,
        name="basis",
    )(own, below, above, last, following)
    parts = lax.all_to_all(gram, "gz", 0, 0, tiled=True)
    line = pl.pallas_call(
        sum_kernel,
        out_shape=jax.ShapeDtypeStruct((2 * count_x, LANES), F32),
        in_specs=[VMEM],
        out_specs=VMEM,
        compiler_params=PARAMS,
        name="line_sum",
    )(parts)
    parts = lax.all_to_all(line, "gx", 0, 0, tiled=True)
    scale = math.sqrt(B * B * LANES * count_x * count_y)
    return pl.pallas_call(
        lambda *refs: factor_kernel(scale, *refs),
        out_shape=(
            jax.ShapeDtypeStruct((COLS, B, B, LANES), F32),
            jax.ShapeDtypeStruct((COLS, COLS), F32),
            jax.ShapeDtypeStruct((COLS, S), F32),
        ),
        in_specs=[VMEM] * 2,
        out_specs=(VMEM,) * 3,
        scratch_shapes=[pltpu.VMEM((COLS, 2 * B, LANES), F32)],
        compiler_params=PARAMS,
        name="factor",
    )(parts, block)


def solution(mesh):
    return jax.shard_map(
        body,
        mesh=mesh,
        in_specs=(
            P(None, "gx", "gz", None),
            P(),
            P(None, "gx", "gz", None),
            P(None, "gx", "gz", None),
            P(None, "gx", "gz", None),
        ),
        out_specs=(P(None, "gx", "gz", None), P(), P()),
        check_vma=False,
    )
```

time: 499 us -> 92.6 us (0.19)
  blocking collectives: 262 us -> 49 us
  starting transfers between devices: 119 us -> 23.8 us
  other arithmetic: 86.2 us -> 0 us
  Pallas kernels: 0 us -> 9.43 us
  waiting for transfers between devices: 11.1 us -> 4.35 us
  matrix products: 5.87 us -> 0 us
    psum x2 -> x0, blocking collectives: 262 us -> none  [global_gram(): return lax.psum(gram_of(block), ('gx', 'gz'))]
    ppermute x34 -> x4, starting transfers between devices: 119 us -> 23.8 us  [moved(): return lax.ppermute(array, axis, route)]
    div x6 -> x0, other arithmetic: 78.9 us -> none  [the longest x3 78.8 us: upper_inverse(): rows[row_index] = remainder / upper[row_index, row_index]]
    all_to_all x0 -> x2, blocking collectives: none -> 49 us  [the longest x1 36.6 us: body(): parts = lax.all_to_all(line, 'gx', 0, 0, tiled=True)]
    pallas_call x0 -> x5, Pallas kernels: none -> 9.43 us  [the longest x1 6.94 us: body(): pl.pallas_call(basis_kernel, out_shape=(jax.ShapeDtypeStruct((COLS, B, B,...]
    ppermute x34 -> x4, waiting for transfers between devices: 11.1 us -> 4.35 us  [moved(): return lax.ppermute(array, axis, route)]
    slice x18 -> x0, local copies, waits for them, and re-layouts: 6.38 us -> none  [the longest x5 3.52 us: upper_inverse(): remainder = remainder - upper[row_index, other] * rows[other]]
    dot_general x7 -> x0, matrix products: 5.87 us -> none  [the longest x1 2.1 us: body(): upper = jnp.dot(upper_two, upper_one, precision=lax.Precision.HIGHEST)]
  transfers between devices with their start and end apart: 34 -> 4, of which waited for: 15 -> 3; matrix products, arithmetic and copies ran while one was open for 0% -> 0% of each run, Pallas kernels for 0% -> 0%
where the time goes in v1:
time: 92.6 us; the launch traced here: 92.2 us
  blocking collectives  49 us (53%)
  starting transfers between devices  23.8 us (26%)
  Pallas kernels  9.43 us (10%)
  waiting for transfers between devices  4.35 us (5%)
  local copies, waits for them, and re-layouts  4.24 us (5%)
  between operations  1.34 us (1%)
    all_to_all x1, blocking collectives, body(): parts = lax.all_to_all(line, 'gx', 0, 0, tiled=True)  36.6 us
    ppermute x4, starting transfers between devices, moved(): return lax.ppermute(array, axis, route)  23.8 us
    all_to_all x1, blocking collectives, body(): parts = lax.all_to_all(gram, 'gz', 0, 0, tiled=True)  12.4 us
    pallas_call x1, Pallas kernels, body(): pl.pallas_call(basis_kernel, out_shape=(jax.ShapeDtypeStruct((COLS, B, B,...  6.94 us
    ppermute x4, waiting for transfers between devices, moved(): return lax.ppermute(array, axis, route)  4.35 us
    unnamed x8, local copies, waits for them, and re-layouts  3.57 us
    pallas_call x1, Pallas kernels, body(): pl.pallas_call(lambda *refs: factor_kernel(scale, *refs), out_shape=(jax....  2.36 us
  transfers between devices with their start and end apart: 4, of which 3 were waited for; matrix products, arithmetic and copies ran while one was open for 0% of the time, Pallas kernels for 0%

profile of v1, /device:TPU:1, one launch (start us, length us, event | category | flops | bytes accessed | tf_op | source)
XLA Modules:
  0.0 92.2 jit_solution(16832552902679523096)
XLA Ops:
  1.3 0.0 copy-start
  1.3 0.9 copy-done
  2.2 0.0 copy-start.1
  2.2 0.9 copy-done.1
  3.1 0.0 copy-start.2
  3.1 0.9 copy-done.2
  4.0 0.0 copy-start.3
  4.0 0.9 copy-done.3
  4.9 1.3 %collective-permute-start.1 = (f32[7,8,8,128]{3,2,1,0:T(8,128)S(1)}, f32[7,8,8,128]{3,2,1,0:T(8,128)S(1)}, u32[]{:S(2)}, u32[]{:S(2)}) collective-permute-start(f32[7,8,8,128]{3,2,1,0:T(8,128)S(1)} %pack.1.own), channel_id=1, source_target_pairs={{16,0},{32,16},{48,32},{64,48},{80,64},{96,80},{112,96},{128,112},... | collective-permute-start | bytes 688136 | tf_op jit(solution)/shard_map/ppermute | solution.py:296
  6.2 6.4 %collective-permute-start = (f32[7,8,8,128]{3,2,1,0:T(8,128)S(1)}, f32[7,8,8,128]{3,2,1,0:T(8,128)S(1)}, u32[]{:S(2)}, u32[]{:S(2)}) collective-permute-start(f32[7,8,8,128]{3,2,1,0:T(8,128)S(1)} %pack.1.own), channel_id=1, source_target_pairs={{0,16},{16,32},{32,48},{48,64},{64,80},{80,96},{96,112},{112,128},... | collective-permute-start | bytes 688136 | tf_op jit(solution)/shard_map/ppermute | solution.py:296
  12.6 1.5 %collective-permute-done.1.above = f32[7,8,8,128]{3,2,1,0:T(8,128)S(1)} collective-permute-done((f32[7,8,8,128]{3,2,1,0:T(8,128)S(1)}, f32[7,8,8,128]{3,2,1,0:T(8,128)S(1)}, u32[]{:S(2)}, u32[]{:S(2)}) %collective-permute-start.1) | collective-permute-done | bytes 229408 | tf_op jit(solution)/shard_map/ppermute | solution.py:296
  14.0 1.5 %collective-permute-done.below = f32[7,8,8,128]{3,2,1,0:T(8,128)S(1)} collective-permute-done((f32[7,8,8,128]{3,2,1,0:T(8,128)S(1)}, f32[7,8,8,128]{3,2,1,0:T(8,128)S(1)}, u32[]{:S(2)}, u32[]{:S(2)}) %collective-permute-start) | collective-permute-done | bytes 229408 | tf_op jit(solution)/shard_map/ppermute | solution.py:296
  15.5 0.1 sides.1
  15.6 5.9 %collective-permute-start.2 = (f32[7,16,8,128]{3,2,1,0:T(8,128)S(1)}, f32[7,16,8,128]{3,2,1,0:T(8,128)S(1)}, u32[]{:S(2)}, u32[]{:S(2)}) collective-permute-start(f32[7,16,8,128]{3,2,1,0:T(8,128)S(1)} %get-tuple-element.7), channel_id=1, source_target_pairs={{0,1},{1,2},{2,3},{3,4},{4,5},{5,6},{6,7},{7,8},{8,9},{9,10},{10,1... | collective-permute-start | bytes 1376264 | tf_op jit(solution)/shard_map/ppermute | solution.py:296
  21.5 10.3 %collective-permute-start.3 = (f32[7,16,8,128]{3,2,1,0:T(8,128)S(1)}, f32[7,16,8,128]{3,2,1,0:T(8,128)S(1)}, u32[]{:S(2)}, u32[]{:S(2)}) collective-permute-start(f32[7,16,8,128]{3,2,1,0:T(8,128)S(1)} %get-tuple-element.8), channel_id=1, source_target_pairs={{1,0},{2,1},{3,2},{4,3},{5,4},{6,5},{7,6},{8,7},{9,8},{10,9},{11,1... | collective-permute-start | bytes 1376264 | tf_op jit(solution)/shard_map/ppermute | solution.py:296
  31.7 0.0 collective-permute-done.2.last
  31.8 1.4 %collective-permute-done.3.following = f32[7,16,8,128]{3,2,1,0:T(8,128)S(1)} collective-permute-done((f32[7,16,8,128]{3,2,1,0:T(8,128)S(1)}, f32[7,16,8,128]{3,2,1,0:T(8,128)S(1)}, u32[]{:S(2)}, u32[]{:S(2)}) %collective-permute-start.3) | collective-permute-done | bytes 458784 | tf_op jit(solution)/shard_map/ppermute | solution.py:296
  33.2 6.9 %basis.3 = (f32[9,8,8,128]{3,2,1,0:T(8,128)S(1)}, f32[32,128]{1,0:T(8,128)S(1)}) custom-call(f32[7,8,8,128]{3,2,1,0:T(8,128)S(1)} %pack.1.own, f32[7,8,8,128]{3,2,1,0:T(8,128)S(1)} %collective-permute-done.below, f32[7,8,8,128]{3,2,1,0:T(8,128)S(1)} %collective-permute-done.1.above, f32[7,16,8,128]{3,2,1,0:T(8,128)S(1)} %collective-permute-done.2.last, ...), custom_call_target="tpu_custom_call" | custom-call | tf_op jit(solution)/shard_map/basis/pallas_call | solution.py:324
  40.1 12.4 %all_to_all.22 = f32[16,2,128]{2,1,0:T(2,128)S(1)} all-to-all(f32[16,2,128]{2,1,0:T(2,128)S(1)} %bitcast.7), channel_id=1, replica_groups=mesh['gx'=64,'gz'=16] {'gz'}, dimensions={0} | all-to-all | bytes 32768 | tf_op jit(solution)/shard_map/all_to_all | solution.py:341
  52.5 36.6 %all_to_all.23 = f32[64,2,128]{2,1,0:T(2,128)S(1)} all-to-all(f32[64,2,128]{2,1,0:T(2,128)S(1)} %bitcast.4), channel_id=1, replica_groups=mesh['gx'=64,'gz'=16] {'gx'}, dimensions={0} | all-to-all | bytes 131072 | tf_op jit(solution)/shard_map/all_to_all | solution.py:350
  89.2 2.4 %factor.1 = (f32[9,8,8,128]{3,2,1,0:T(8,128)}, f32[9,9]{1,0:T(8,128)}, f32[9,8]{1,0:T(8,128)S(1)}) custom-call(f32[128,128]{1,0:T(8,128)S(1)} %bitcast.5, f32[9,8,8,128]{3,2,1,0:T(8,128)S(1)} %get-tuple-element.10.refs_1_), custom_call_target="tpu_custom_call" | custom-call | tf_op jit(solution)/shard_map/factor/pallas_call | solution.py:352
  91.5 0.7 copy.8
  (2 shorter events, 0.1 us)
Async XLA Ops:
  1.3 0.9 copy-start
  2.2 0.9 copy-start.1
  3.1 0.9 copy-start.2
  4.0 0.9 copy-start.3
  4.9 9.1 %collective-permute-start.1 = (f32[7,8,8,128]{3,2,1,0:T(8,128)S(1)}, f32[7,8,8,128]{3,2,1,0:T(8,128)S(1)}, u32[]{:S(2)}, u32[]{:S(2)}) collective-permute-start(f32[7,8,8,128]{3,2,1,0:T(8,128)S(1)} %pack.1.own), channel_id=1, source_target_pairs={{16,0},{32,16},{48,32},{64,48},{80,64},{96,80},{112,96},{128,112},... | collective-permute-start | bytes 688136 | tf_op jit(solution)/shard_map/ppermute | solution.py:296
  6.2 9.3 %collective-permute-start = (f32[7,8,8,128]{3,2,1,0:T(8,128)S(1)}, f32[7,8,8,128]{3,2,1,0:T(8,128)S(1)}, u32[]{:S(2)}, u32[]{:S(2)}) collective-permute-start(f32[7,8,8,128]{3,2,1,0:T(8,128)S(1)} %pack.1.own), channel_id=1, source_target_pairs={{0,16},{16,32},{32,48},{48,64},{64,80},{80,96},{96,112},{112,128},... | collective-permute-start | bytes 688136 | tf_op jit(solution)/shard_map/ppermute | solution.py:296
  15.6 16.2 %collective-permute-start.2 = (f32[7,16,8,128]{3,2,1,0:T(8,128)S(1)}, f32[7,16,8,128]{3,2,1,0:T(8,128)S(1)}, u32[]{:S(2)}, u32[]{:S(2)}) collective-permute-start(f32[7,16,8,128]{3,2,1,0:T(8,128)S(1)} %get-tuple-element.7), channel_id=1, source_target_pairs={{0,1},{1,2},{2,3},{3,4},{4,5},{5,6},{6,7},{7,8},{8,9},{9,10},{10,1... | collective-permute-start | bytes 1376264 | tf_op jit(solution)/shard_map/ppermute | solution.py:296
  21.5 11.7 %collective-permute-start.3 = (f32[7,16,8,128]{3,2,1,0:T(8,128)S(1)}, f32[7,16,8,128]{3,2,1,0:T(8,128)S(1)}, u32[]{:S(2)}, u32[]{:S(2)}) collective-permute-start(f32[7,16,8,128]{3,2,1,0:T(8,128)S(1)} %get-tuple-element.8), channel_id=1, source_target_pairs={{1,0},{2,1},{3,2},{4,3},{5,4},{6,5},{7,6},{8,7},{9,8},{10,9},{11,1... | collective-permute-start | bytes 1376264 | tf_op jit(solution)/shard_map/ppermute | solution.py:296

commit v2 on v1

--- a/solution.py
+++ b/solution.py
@@ -17,8 +17,10 @@
 FIELDS = 7
 F32 = jnp.float32
 VMEM = pl.BlockSpec(memory_space=pltpu.VMEM)
+HBM = pl.BlockSpec(memory_space=pltpu.HBM)
 SMEM = pl.BlockSpec(memory_space=pltpu.SMEM)
 PARAMS = pltpu.CompilerParams(vmem_limit_bytes=16 * 1024 * 1024)
+ALL_VMEM = pltpu.CompilerParams(vmem_limit_bytes=63 * 1024 * 1024)
 
 
 def iota(shape, dim):
@@ -67,8 +69,22 @@
     return tuple(jnp.where(mask, x, y) for x, y in zip(a, b))
 
 
-def pack_kernel(column, basis, diffusivity, speed, upwind, out):
-    out[0] = basis[column[0]]
+def pack_kernel(column, basis, diffusivity_in, speed_in, upwind_in, out, diffusivity, speed, upwind, sems):
+    copies = [
+        pltpu.make_async_copy(src, dst, sems.at[n])
+        for n, (src, dst) in enumerate(
+            (
+                (basis.at[column[0]], out.at[0]),
+                (diffusivity_in, diffusivity),
+                (speed_in, speed),
+                (upwind_in, upwind),
+            )
+        )
+    ]
+    for copy in copies:
+        copy.start()
+    for copy in copies:
+        copy.wait()
     factor = -2.0 / HALF
     for dim in range(3):
         flow = upwind[dim].astype(F32)
@@ -76,31 +92,53 @@
         out[4 + dim] = (diffusivity[dim] + speed[dim] * (1.0 - flow)) * factor
 
 
-def side_kernel(own, below, above, to_next, to_last):
+def side_kernel(even, own, first, second, wide, to_first, to_second):
+    @pl.when(even[0] == 1)
+    def _():
+        wide[:, 0:B] = second[...]
+        wide[:, 2 * B : WIDE] = first[...]
+
+    @pl.when(even[0] == 0)
+    def _():
+        wide[:, 0:B] = first[...]
+        wide[:, 2 * B : WIDE] = second[...]
+
+    wide[:, B : 2 * B] = own[...]
+
+    @pl.when(even[1] == 1)
+    def _():
+        emit_sides(wide, to_first, to_second)
+
+    @pl.when(even[1] == 0)
+    def _():
+        emit_sides(wide, to_second, to_first)
+
+
+def emit_sides(wide, to_next, to_last):
     row = iota((FIELDS, B, LANES), 1)
-    to_next[:, 0:B] = own[...]
-    to_last[:, 0:B] = own[...]
+    own = wide[:, B : 2 * B]
+    to_next[:, 0:B] = own
+    to_last[:, 0:B] = own
     for side in range(2):
-        layer = (lambda m: below[:, B - m]) if side == 0 else (lambda m: above[:, m - 1])
         for m in range(1, 5):
-            near = layer(m)
+            near = wide[:, B - m if side == 0 else 2 * B - 1 + m]
             at = B + 4 * side + m - 1
             if m == 4:
                 to_next[:, at] = near
                 to_last[:, at] = near
             else:
-                far = layer(B - m)
+                far = wide[:, m if side == 0 else WIDE - 1 - m]
                 to_next[:, at] = jnp.where(row >= m, near, pltpu.roll(far, m, 1))
                 to_last[:, at] = jnp.where(row < B - m, near, pltpu.roll(far, B - m, 1))
 
 
-def basis_kernel(own, below, above, last, following, block, gram, coeff, field, high, low):
+def start_fields(strip, last, following, coeff, field):
     def wide(f, a):
         if B <= a < 2 * B:
-            return jnp.concatenate([last[f, a - B], own[f, a - B], following[f, a - B]], 0)
+            return jnp.concatenate([last[f, a - B], strip[f, a], following[f, a - B]], 0)
         side = 0 if a < B else 1
         m = B - a if side == 0 else a - (2 * B - 1)
-        middle = below[f, a] if side == 0 else above[f, a - 2 * B]
+        middle = strip[f, a]
         if m == B:
             lower = upper = jnp.zeros((B, LANES), F32)
         elif m <= 4:
@@ -135,7 +173,17 @@
         coeff[5, a] = jnp.where(lane == LANES - 1, zero, p[2])
         coeff[6, a] = qz
 
-    block[0] = own[0]
+
+def basis_kernel(even, strip, first, second, block, gram, coeff, field, high, low):
+    @pl.when(even[1] == 1)
+    def _():
+        start_fields(strip, second, first, coeff, field)
+
+    @pl.when(even[1] == 0)
+    def _():
+        start_fields(strip, first, second, coeff, field)
+
+    block[0] = strip[0, B : 2 * B]
     for k in range(1, COLS):
         src, dst = (k - 1) % 2, k % 2
 
@@ -152,7 +200,7 @@
                 field[dst, a] = new
             return carry
 
-        lax.fori_loop(k, WIDE - k, layer, 0, unroll=2)
+        lax.fori_loop(k, WIDE - k, layer, 0, unroll=True)
         if k < S:
             block[k] = field[dst, B : 2 * B, B : 2 * B, :]
 
@@ -271,13 +319,13 @@
     product = CENTER * upper + jnp.where(lane == 0, HALF, 0.5 * HALF) * right + (0.5 * HALF) * pltpu.roll(upper, 1, 1)
     product = jnp.where(lane < S, product, 0.0)
     small = lax.dot_general(
+        jnp.where(lane < S, lower, 0.0),
         product,
-        jnp.where(lane < S, lower, 0.0),
         (((1,), (1,)), ((), ())),
         precision=lax.Precision.HIGHEST,
         preferred_element_type=F32,
     )
-    hessenberg[...] = small[:COLS, :S]
+    hessenberg[...] = small[:S, :COLS]
     lower = lower * scale
     for k in range(COLS):
         inverse[k] = jnp.broadcast_to(lower[:, k : k + 1], shape)
@@ -290,36 +338,43 @@
         basis_q[j] = total
 
 
-def moved(array, axis, distance):
+def paired(array, axis, first):
     count = lax.axis_size(axis)
-    route = [(i, i + distance) for i in range(count) if 0 <= i + distance < count]
-    return lax.ppermute(array, axis, route)
+    lower = range(first, count - 1, 2)
+    return lax.ppermute(array, axis, [(i, i + 1) for i in lower] + [(i + 1, i) for i in lower])
 
 
 def body(previous_basis, restart_column, diffusivity, speed, upwind):
     count_x, count_y = lax.axis_size("gx"), lax.axis_size("gz")
-    brick = (FIELDS, B, B, LANES)
+    even = jnp.stack([1 - lax.axis_index("gx") % 2, 1 - lax.axis_index("gz") % 2]).astype(jnp.int32)
+    faces = (3, B, B, LANES)
     own = pl.pallas_call(
         pack_kernel,
-        out_shape=jax.ShapeDtypeStruct(brick, F32),
-        in_specs=[SMEM] + [VMEM] * 4,
+        out_shape=jax.ShapeDtypeStruct((FIELDS, B, B, LANES), F32),
+        in_specs=[SMEM] + [HBM] * 4,
         out_specs=VMEM,
-        compiler_params=PARAMS,
+        scratch_shapes=[
+            pltpu.VMEM(faces, F32),
+            pltpu.VMEM(faces, F32),
+            pltpu.VMEM(faces, jnp.int32),
+            pltpu.SemaphoreType.DMA((4,)),
+        ],
+        compiler_params=ALL_VMEM,
         name="pack",
     )(restart_column, previous_basis, diffusivity, speed, upwind)
-    below = moved(own, "gx", 1)
-    above = moved(own, "gx", -1)
+    first = paired(own, "gx", 0)
+    second = paired(own, "gx", 1)
     sides = jax.ShapeDtypeStruct((FIELDS, 2 * B, B, LANES), F32)
-    to_next, to_last = pl.pallas_call(
+    strip, to_first, to_second = pl.pallas_call(
         side_kernel,
-        out_shape=(sides, sides),
-        in_specs=[VMEM] * 3,
-        out_specs=(VMEM, VMEM),
+        out_shape=(jax.ShapeDtypeStruct((FIELDS, WIDE, B, LANES), F32), sides, sides),
+        in_specs=[SMEM] + [VMEM] * 3,
+        out_specs=(VMEM,) * 3,
         compiler_params=PARAMS,
         name="sides",
-    )(own, below, above)
-    last = moved(to_next, "gz", 1)
-    following = moved(to_last, "gz", -1)
+    )(even, own, first, second)
+    first = paired(to_first, "gz", 0)
+    second = paired(to_second, "gz", 1)
     wide = (WIDE, WIDE, LANES)
     block, gram = pl.pallas_call(
         basis_kernel,
@@ -327,7 +382,7 @@
             jax.ShapeDtypeStruct((COLS, B, B, LANES), F32),
             jax.ShapeDtypeStruct((2 * count_y, LANES), F32),
         ),
-        in_specs=[VMEM] * 5,
+        in_specs=[SMEM] + [VMEM] * 3,
         out_specs=(VMEM, VMEM),
         scratch_shapes=[
             pltpu.VMEM((FIELDS,) + wide, F32),
@@ -337,7 +392,7 @@
         ],
         compiler_params=PARAMS,
         name="basis",
-    )(own, below, above, last, following)
+    )(even, strip, first, second)
     parts = lax.all_to_all(gram, "gz", 0, 0, tiled=True)
     line = pl.pallas_call(
         sum_kernel,
@@ -349,12 +404,12 @@
     )(parts)
     parts = lax.all_to_all(line, "gx", 0, 0, tiled=True)
     scale = math.sqrt(B * B * LANES * count_x * count_y)
-    return pl.pallas_call(
+    basis_q, factor_r, hessenberg = pl.pallas_call(
         lambda *refs: factor_kernel(scale, *refs),
         out_shape=(
             jax.ShapeDtypeStruct((COLS, B, B, LANES), F32),
             jax.ShapeDtypeStruct((COLS, COLS), F32),
-            jax.ShapeDtypeStruct((COLS, S), F32),
+            jax.ShapeDtypeStruct((S, COLS), F32),
         ),
         in_specs=[VMEM] * 2,
         out_specs=(VMEM,) * 3,
@@ -362,6 +417,7 @@
         compiler_params=PARAMS,
         name="factor",
     )(parts, block)
+    return basis_q, factor_r, jnp.transpose(hessenberg)
 
 
 def solution(mesh):

time: 92.6 us -> 84.6 us (0.914)
  blocking collectives: 49 us -> 39.4 us
  waiting for transfers between devices: 4.35 us -> 11.4 us
  local copies, waits for them, and re-layouts: 4.24 us -> 0.94 us
  Pallas kernels: 9.43 us -> 7.93 us
    ppermute x4, waiting for transfers between devices: 4.35 us -> 11.4 us  [paired(): lax.ppermute(array, axis, [(i, i + 1) for i in lower] + [(i + 1, i) for i...]
    all_to_all x1, blocking collectives: 36.6 us -> 29.8 us  [body(): parts = lax.all_to_all(line, 'gx', 0, 0, tiled=True)]
    pallas_call x1, Pallas kernels: 6.94 us -> 3.17 us  [body(): pl.pallas_call(basis_kernel, out_shape=(jax.ShapeDtypeStruct((COLS, B, B,...]
    all_to_all x1, blocking collectives: 12.4 us -> 9.57 us  [body(): parts = lax.all_to_all(gram, 'gz', 0, 0, tiled=True)]
    unnamed x8 -> x2, local copies, waits for them, and re-layouts: 3.57 us -> 0.94 us
    pallas_call x2, Pallas kernels: 0.09 us -> 2.42 us  [the longest x1 1.76 us: body(): pl.pallas_call(pack_kernel, out_shape=jax.ShapeDtypeStruct((FIELDS, B, B,...]
  transfers between devices with their start and end apart: 4 -> 4, of which waited for: 3 -> 2; matrix products, arithmetic and copies ran while one was open for 0% -> 0% of each run, Pallas kernels for 0% -> 0%
where the time goes in v2:
time: 84.6 us; the launch traced here: 84.2 us
  blocking collectives  39.4 us (47%)
  starting transfers between devices  23.2 us (27%)
  waiting for transfers between devices  11.4 us (13%)
  Pallas kernels  7.93 us (9%)
  between operations  1.36 us (2%)
  local copies, waits for them, and re-layouts  0.94 us (1%)
    all_to_all x1, blocking collectives, body(): parts = lax.all_to_all(line, 'gx', 0, 0, tiled=True)  29.8 us
    ppermute x4, starting transfers between devices, paired(): lax.ppermute(array, axis, [(i, i + 1) for i in lower] + [(i + 1, i) for i...  23.2 us
    ppermute x4, waiting for transfers between devices, paired(): lax.ppermute(array, axis, [(i, i + 1) for i in lower] + [(i + 1, i) for i...  11.4 us
    all_to_all x1, blocking collectives, body(): parts = lax.all_to_all(gram, 'gz', 0, 0, tiled=True)  9.57 us
    pallas_call x1, Pallas kernels, body(): pl.pallas_call(basis_kernel, out_shape=(jax.ShapeDtypeStruct((COLS, B, B,...  3.17 us
    pallas_call x1, Pallas kernels, body(): pl.pallas_call(lambda *refs: factor_kernel(scale, *refs), out_shape=(jax....  2.3 us
    pallas_call x1, Pallas kernels, body(): pl.pallas_call(pack_kernel, out_shape=jax.ShapeDtypeStruct((FIELDS, B, B,...  1.76 us
  transfers between devices with their start and end apart: 4, of which 2 were waited for; matrix products, arithmetic and copies ran while one was open for 0% of the time, Pallas kernels for 0%

profile of v2, /device:TPU:1, one launch (start us, length us, event | category | flops | bytes accessed | tf_op | source)
XLA Modules:
  0.0 84.2 jit_solution(15485675857369291405)
XLA Ops:
  1.3 1.8 %pack.1.own = f32[7,8,8,128]{3,2,1,0:T(8,128)} custom-call(s32[1]{0:T(128)S(6)} %copy.8.column, f32[4,8,8,128]{3,2,1,0:T(8,128)} %basis.2, f32[3,8,8,128]{3,2,1,0:T(8,128)} %diffusivity_in.1, f32[3,8,8,128]{3,2,1,0:T(8,128)} %speed_in.1, s32[3,8,8,128]{3,2,1,0:T(8,128)} %upwind_in.1), custom_call_target="tpu_custom_call" | custom-call | tf_op jit(solution)/shard_map/pack/pallas_call | solution.py:351
  3.0 0.7 collective-permute-start.1
  3.7 10.0 %collective-permute-start = (f32[7,8,8,128]{3,2,1,0:T(8,128)}, f32[7,8,8,128]{3,2,1,0:T(8,128)S(1)}, u32[]{:S(2)}, u32[]{:S(2)}) collective-permute-start(f32[7,8,8,128]{3,2,1,0:T(8,128)} %pack.1.own), channel_id=1, source_target_pairs={{0,16},{32,48},{64,80},{96,112},{128,144},{160,176},{192,208},{224... | collective-permute-start | bytes 688136 | tf_op jit(solution)/shard_map/ppermute | solution.py:344
  13.7 0.1 pad_add_fusion.even
  13.8 0.0 collective-permute-done.1.second
  13.8 3.5 %collective-permute-done.first = f32[7,8,8,128]{3,2,1,0:T(8,128)S(1)} collective-permute-done((f32[7,8,8,128]{3,2,1,0:T(8,128)}, f32[7,8,8,128]{3,2,1,0:T(8,128)S(1)}, u32[]{:S(2)}, u32[]{:S(2)}) %collective-permute-start) | collective-permute-done | bytes 229408 | tf_op jit(solution)/shard_map/ppermute | solution.py:344
  17.3 0.0 copy-start
  17.3 0.9 %copy-done = f32[7,8,8,128]{3,2,1,0:T(8,128)S(1)} copy-done((f32[7,8,8,128]{3,2,1,0:T(8,128)S(1)}, f32[7,8,8,128]{3,2,1,0:T(8,128)}, u32[]{:S(2)}) %copy-start) | copy-done | bytes 229400
  18.3 0.7 sides.1
  18.9 10.6 %collective-permute-start.2 = (f32[7,16,8,128]{3,2,1,0:T(8,128)S(1)}, f32[7,16,8,128]{3,2,1,0:T(8,128)S(1)}, u32[]{:S(2)}, u32[]{:S(2)}) collective-permute-start(f32[7,16,8,128]{3,2,1,0:T(8,128)S(1)} %get-tuple-element.12), channel_id=1, source_target_pairs={{0,1},{2,3},{4,5},{6,7},{8,9},{10,11},{12,13},{14,15},{1,0},{3,2},... | collective-permute-start | bytes 1376264 | tf_op jit(solution)/shard_map/ppermute | solution.py:344
  29.5 1.9 %collective-permute-start.3 = (f32[7,16,8,128]{3,2,1,0:T(8,128)S(1)}, f32[7,16,8,128]{3,2,1,0:T(8,128)S(1)}, u32[]{:S(2)}, u32[]{:S(2)}) collective-permute-start(f32[7,16,8,128]{3,2,1,0:T(8,128)S(1)} %get-tuple-element.13), channel_id=1, source_target_pairs={{1,2},{3,4},{5,6},{7,8},{9,10},{11,12},{13,14},{2,1},{4,3},{6,5},{... | collective-permute-start | bytes 1376264 | tf_op jit(solution)/shard_map/ppermute | solution.py:344
  31.5 0.0 collective-permute-done.2.first
  31.5 7.9 %collective-permute-done.3.second = f32[7,16,8,128]{3,2,1,0:T(8,128)S(1)} collective-permute-done((f32[7,16,8,128]{3,2,1,0:T(8,128)S(1)}, f32[7,16,8,128]{3,2,1,0:T(8,128)S(1)}, u32[]{:S(2)}, u32[]{:S(2)}) %collective-permute-start.3) | collective-permute-done | bytes 458784 | tf_op jit(solution)/shard_map/ppermute | solution.py:344
  39.3 3.2 %basis.3 = (f32[9,8,8,128]{3,2,1,0:T(8,128)S(1)}, f32[32,128]{1,0:T(8,128)S(1)}) custom-call(s32[2]{0:T(128)S(1)} %pad_add_fusion.even, f32[7,24,8,128]{3,2,1,0:T(8,128)S(1)} %get-tuple-element.11.strip, f32[7,16,8,128]{3,2,1,0:T(8,128)S(1)} %collective-permute-done.2.first, f32[7,16,8,128]{3,2,1,0:T(8,128)S(1)} %collective-permute-done.3.second), custom_call_target="tpu_custom_call" | custom-call | tf_op jit(solution)/shard_map/basis/pallas_call | solution.py:379
  42.5 9.6 %all_to_all.22 = f32[16,2,128]{2,1,0:T(2,128)S(1)} all-to-all(f32[16,2,128]{2,1,0:T(2,128)S(1)} %bitcast.10), channel_id=1, replica_groups=mesh['gx'=64,'gz'=16] {'gz'}, dimensions={0} | all-to-all | bytes 32768 | tf_op jit(solution)/shard_map/all_to_all | solution.py:396
  52.1 29.8 %all_to_all.23 = f32[64,2,128]{2,1,0:T(2,128)S(1)} all-to-all(f32[64,2,128]{2,1,0:T(2,128)S(1)} %bitcast.7), channel_id=1, replica_groups=mesh['gx'=64,'gz'=16] {'gx'}, dimensions={0} | all-to-all | bytes 131072 | tf_op jit(solution)/shard_map/all_to_all | solution.py:405
  81.9 2.3 %factor.1 = (f32[9,8,8,128]{3,2,1,0:T(8,128)}, f32[9,9]{1,0:T(8,128)}, f32[8,9]{1,0:T(8,128)}) custom-call(f32[128,128]{1,0:T(8,128)S(1)} %bitcast.8, f32[9,8,8,128]{3,2,1,0:T(8,128)S(1)} %get-tuple-element.15.refs_1_), custom_call_target="tpu_custom_call" | custom-call | tf_op jit(solution)/shard_map/factor/pallas_call | solution.py:407
  (1 shorter events, 0.0 us)
Async XLA Ops:
  3.0 10.8 %collective-permute-start.1 = (f32[7,8,8,128]{3,2,1,0:T(8,128)}, f32[7,8,8,128]{3,2,1,0:T(8,128)S(1)}, u32[]{:S(2)}, u32[]{:S(2)}) collective-permute-start(f32[7,8,8,128]{3,2,1,0:T(8,128)} %pack.1.own), channel_id=1, source_target_pairs={{16,32},{48,64},{80,96},{112,128},{144,160},{176,192},{208,224},{2... | collective-permute-start | bytes 688136 | tf_op jit(solution)/shard_map/ppermute | solution.py:344
  3.7 13.6 %collective-permute-start = (f32[7,8,8,128]{3,2,1,0:T(8,128)}, f32[7,8,8,128]{3,2,1,0:T(8,128)S(1)}, u32[]{:S(2)}, u32[]{:S(2)}) collective-permute-start(f32[7,8,8,128]{3,2,1,0:T(8,128)} %pack.1.own), channel_id=1, source_target_pairs={{0,16},{32,48},{64,80},{96,112},{128,144},{160,176},{192,208},{224... | collective-permute-start | bytes 688136 | tf_op jit(solution)/shard_map/ppermute | solution.py:344
  17.3 0.9 %copy-start = (f32[7,8,8,128]{3,2,1,0:T(8,128)S(1)}, f32[7,8,8,128]{3,2,1,0:T(8,128)}, u32[]{:S(2)}) copy-start(f32[7,8,8,128]{3,2,1,0:T(8,128)} %pack.1.own) | copy-start | bytes 688132
  18.9 12.5 %collective-permute-start.2 = (f32[7,16,8,128]{3,2,1,0:T(8,128)S(1)}, f32[7,16,8,128]{3,2,1,0:T(8,128)S(1)}, u32[]{:S(2)}, u32[]{:S(2)}) collective-permute-start(f32[7,16,8,128]{3,2,1,0:T(8,128)S(1)} %get-tuple-element.12), channel_id=1, source_target_pairs={{0,1},{2,3},{4,5},{6,7},{8,9},{10,11},{12,13},{14,15},{1,0},{3,2},... | collective-permute-start | bytes 1376264 | tf_op jit(solution)/shard_map/ppermute | solution.py:344
  29.5 9.8 %collective-permute-start.3 = (f32[7,16,8,128]{3,2,1,0:T(8,128)S(1)}, f32[7,16,8,128]{3,2,1,0:T(8,128)S(1)}, u32[]{:S(2)}, u32[]{:S(2)}) collective-permute-start(f32[7,16,8,128]{3,2,1,0:T(8,128)S(1)} %get-tuple-element.13), channel_id=1, source_target_pairs={{1,2},{3,4},{5,6},{7,8},{9,10},{11,12},{13,14},{2,1},{4,3},{6,5},{... | collective-permute-start | bytes 1376264 | tf_op jit(solution)/shard_map/ppermute | solution.py:344

commit v3 on v2

--- a/solution.py
+++ b/solution.py
@@ -92,63 +92,62 @@
         out[4 + dim] = (diffusivity[dim] + speed[dim] * (1.0 - flow)) * factor
 
 
-def side_kernel(even, own, first, second, wide, to_first, to_second):
+def corner_kernel(even, first, second, strip, to_first, to_second):
     @pl.when(even[0] == 1)
     def _():
-        wide[:, 0:B] = second[...]
-        wide[:, 2 * B : WIDE] = first[...]
+        strip[:, 0:B] = second[...]
+        strip[:, B : 2 * B] = first[...]
 
     @pl.when(even[0] == 0)
     def _():
-        wide[:, 0:B] = first[...]
-        wide[:, 2 * B : WIDE] = second[...]
-
-    wide[:, B : 2 * B] = own[...]
+        strip[:, 0:B] = first[...]
+        strip[:, B : 2 * B] = second[...]
 
     @pl.when(even[1] == 1)
     def _():
-        emit_sides(wide, to_first, to_second)
+        emit_corners(strip, to_first, to_second)
 
     @pl.when(even[1] == 0)
     def _():
-        emit_sides(wide, to_second, to_first)
-
-
-def emit_sides(wide, to_next, to_last):
+        emit_corners(strip, to_second, to_first)
+
+
+def emit_corners(strip, to_next, to_last):
     row = iota((FIELDS, B, LANES), 1)
-    own = wide[:, B : 2 * B]
-    to_next[:, 0:B] = own
-    to_last[:, 0:B] = own
     for side in range(2):
         for m in range(1, 5):
-            near = wide[:, B - m if side == 0 else 2 * B - 1 + m]
-            at = B + 4 * side + m - 1
+            near = strip[:, B - m if side == 0 else B - 1 + m]
+            at = 4 * side + m - 1
             if m == 4:
                 to_next[:, at] = near
                 to_last[:, at] = near
             else:
-                far = wide[:, m if side == 0 else WIDE - 1 - m]
+                far = strip[:, m if side == 0 else 2 * B - 1 - m]
                 to_next[:, at] = jnp.where(row >= m, near, pltpu.roll(far, m, 1))
                 to_last[:, at] = jnp.where(row < B - m, near, pltpu.roll(far, B - m, 1))
 
 
-def start_fields(strip, last, following, coeff, field):
+def keep_kernel(own, kept):
+    kept[...] = own[...]
+
+
+def start_fields(kept, strip, last, following, corner_last, corner_following, coeff, field):
     def wide(f, a):
         if B <= a < 2 * B:
-            return jnp.concatenate([last[f, a - B], strip[f, a], following[f, a - B]], 0)
+            return jnp.concatenate([last[f, a - B], kept[f, a - B], following[f, a - B]], 0)
         side = 0 if a < B else 1
         m = B - a if side == 0 else a - (2 * B - 1)
-        middle = strip[f, a]
+        middle = strip[f, a if side == 0 else a - B]
         if m == B:
             lower = upper = jnp.zeros((B, LANES), F32)
         elif m <= 4:
-            at = B + 4 * side + m - 1
-            lower, upper = last[f, at], following[f, at]
+            at = 4 * side + m - 1
+            lower, upper = corner_last[f, at], corner_following[f, at]
         else:
             other = B - m
-            at = B + 4 * side + other - 1
-            lower = pltpu.roll(last[f, at], B - other, 0)
-            upper = pltpu.roll(following[f, at], other, 0)
+            at = 4 * side + other - 1
+            lower = pltpu.roll(corner_last[f, at], B - other, 0)
+            upper = pltpu.roll(corner_following[f, at], other, 0)
         return jnp.concatenate([lower, middle, upper], 0)
 
     lane = iota((WIDE, LANES), 1)
@@ -174,16 +173,18 @@
         coeff[6, a] = qz
 
 
-def basis_kernel(even, strip, first, second, block, gram, coeff, field, high, low):
+def basis_kernel(
+    even, kept, strip, first, second, corner_first, corner_second, block, gram, coeff, field, high, low
+):
     @pl.when(even[1] == 1)
     def _():
-        start_fields(strip, second, first, coeff, field)
+        start_fields(kept, strip, second, first, corner_second, corner_first, coeff, field)
 
     @pl.when(even[1] == 0)
     def _():
-        start_fields(strip, first, second, coeff, field)
-
-    block[0] = strip[0, B : 2 * B]
+        start_fields(kept, strip, first, second, corner_first, corner_second, coeff, field)
+
+    block[0] = kept[0]
     for k in range(1, COLS):
         src, dst = (k - 1) % 2, k % 2
 
@@ -362,19 +363,24 @@
         compiler_params=ALL_VMEM,
         name="pack",
     )(restart_column, previous_basis, diffusivity, speed, upwind)
-    first = paired(own, "gx", 0)
-    second = paired(own, "gx", 1)
-    sides = jax.ShapeDtypeStruct((FIELDS, 2 * B, B, LANES), F32)
+    first_x = paired(own, "gx", 0)
+    second_x = paired(own, "gx", 1)
+    brick = jax.ShapeDtypeStruct((FIELDS, B, B, LANES), F32)
+    kept = pl.pallas_call(
+        keep_kernel, out_shape=brick, in_specs=[VMEM], out_specs=VMEM, compiler_params=PARAMS, name="keep"
+    )(own)
+    first_y = paired(kept, "gz", 0)
+    second_y = paired(kept, "gz", 1)
     strip, to_first, to_second = pl.pallas_call(
-        side_kernel,
-        out_shape=(jax.ShapeDtypeStruct((FIELDS, WIDE, B, LANES), F32), sides, sides),
-        in_specs=[SMEM] + [VMEM] * 3,
+        corner_kernel,
+        out_shape=(jax.ShapeDtypeStruct((FIELDS, 2 * B, B, LANES), F32), brick, brick),
+        in_specs=[SMEM] + [VMEM] * 2,
         out_specs=(VMEM,) * 3,
         compiler_params=PARAMS,
-        name="sides",
-    )(even, own, first, second)
-    first = paired(to_first, "gz", 0)
-    second = paired(to_second, "gz", 1)
+        name="corners",
+    )(even, first_x, second_x)
+    first_corner = paired(to_first, "gz", 0)
+    second_corner = paired(to_second, "gz", 1)
     wide = (WIDE, WIDE, LANES)
     block, gram = pl.pallas_call(
         basis_kernel,
@@ -382,7 +388,7 @@
             jax.ShapeDtypeStruct((COLS, B, B, LANES), F32),
             jax.ShapeDtypeStruct((2 * count_y, LANES), F32),
         ),
-        in_specs=[SMEM] + [VMEM] * 3,
+        in_specs=[SMEM] + [VMEM] * 6,
         out_specs=(VMEM, VMEM),
         scratch_shapes=[
             pltpu.VMEM((FIELDS,) + wide, F32),
@@ -392,7 +398,7 @@
         ],
         compiler_params=PARAMS,
         name="basis",
-    )(even, strip, first, second)
+    )(even, kept, strip, first_y, second_y, first_corner, second_corner)
     parts = lax.all_to_all(gram, "gz", 0, 0, tiled=True)
     line = pl.pallas_call(
         sum_kernel,

time: 84.6 us -> 83 us (0.981)
  waiting for transfers between devices: 11.4 us -> 4.27 us
  starting transfers between devices: 23.2 us -> 26.1 us
  blocking collectives: 39.4 us -> 41.9 us
    ppermute x4 -> x6, waiting for transfers between devices: 11.4 us -> 4.27 us  [paired(): lax.ppermute(array, axis, [(i, i + 1) for i in lower] + [(i + 1, i) for i...]
    ppermute x4 -> x6, starting transfers between devices: 23.2 us -> 26.1 us  [paired(): lax.ppermute(array, axis, [(i, i + 1) for i in lower] + [(i + 1, i) for i...]
    all_to_all x1, blocking collectives: 29.8 us -> 31.9 us  [body(): parts = lax.all_to_all(line, 'gx', 0, 0, tiled=True)]
  transfers between devices with their start and end apart: 4 -> 6, of which waited for: 2 -> 1; matrix products, arithmetic and copies ran while one was open for 0% -> 0% of each run, Pallas kernels for 0% -> 1%
where the time goes in v3:
time: 83 us; the launch traced here: 82.6 us
  blocking collectives  41.9 us (50%)
  starting transfers between devices  26.1 us (31%)
  Pallas kernels  7.89 us (10%)
  waiting for transfers between devices  4.27 us (5%)
  between operations  1.4 us (2%)
  local copies, waits for them, and re-layouts  0.93 us (1%)
    all_to_all x1, blocking collectives, body(): parts = lax.all_to_all(line, 'gx', 0, 0, tiled=True)  31.9 us
    ppermute x6, starting transfers between devices, paired(): lax.ppermute(array, axis, [(i, i + 1) for i in lower] + [(i + 1, i) for i...  26.1 us
    all_to_all x1, blocking collectives, body(): parts = lax.all_to_all(gram, 'gz', 0, 0, tiled=True)  10 us
    ppermute x6, waiting for transfers between devices, paired(): lax.ppermute(array, axis, [(i, i + 1) for i in lower] + [(i + 1, i) for i...  4.27 us
    pallas_call x1, Pallas kernels, body(): pl.pallas_call(basis_kernel, out_shape=(jax.ShapeDtypeStruct((COLS, B, B,...  3.15 us
    pallas_call x1, Pallas kernels, body(): pl.pallas_call(lambda *refs: factor_kernel(scale, *refs), out_shape=(jax....  2.3 us
    pallas_call x1, Pallas kernels, body(): pl.pallas_call(pack_kernel, out_shape=jax.ShapeDtypeStruct((FIELDS, B, B,...  1.76 us
  transfers between devices with their start and end apart: 6, of which 1 were waited for; matrix products, arithmetic and copies ran while one was open for 0% of the time, Pallas kernels for 1%

profile of v3, /device:TPU:1, one launch (start us, length us, event | category | flops | bytes accessed | tf_op | source)
XLA Modules:
  0.0 82.6 jit_solution(4369386370940141314)
XLA Ops:
  1.3 1.8 %pack.1.own = f32[7,8,8,128]{3,2,1,0:T(8,128)} custom-call(s32[1]{0:T(128)S(6)} %copy.8.column, f32[4,8,8,128]{3,2,1,0:T(8,128)} %basis.2, f32[3,8,8,128]{3,2,1,0:T(8,128)} %diffusivity_in.1, f32[3,8,8,128]{3,2,1,0:T(8,128)} %speed_in.1, s32[3,8,8,128]{3,2,1,0:T(8,128)} %upwind_in.1), custom_call_target="tpu_custom_call" | custom-call | tf_op jit(solution)/shard_map/pack/pallas_call | solution.py:352
  3.0 5.7 %collective-permute-start = (f32[7,8,8,128]{3,2,1,0:T(8,128)}, f32[7,8,8,128]{3,2,1,0:T(8,128)S(1)}, u32[]{:S(2)}, u32[]{:S(2)}) collective-permute-start(f32[7,8,8,128]{3,2,1,0:T(8,128)} %pack.1.own), channel_id=1, source_target_pairs={{0,16},{32,48},{64,80},{96,112},{128,144},{160,176},{192,208},{224... | collective-permute-start | bytes 688136 | tf_op jit(solution)/shard_map/ppermute | solution.py:345
  8.8 0.7 collective-permute-start.1
  9.5 0.0 copy-start
  9.5 0.9 %copy-done = f32[7,8,8,128]{3,2,1,0:T(8,128)S(1)} copy-done((f32[7,8,8,128]{3,2,1,0:T(8,128)S(1)}, f32[7,8,8,128]{3,2,1,0:T(8,128)}, u32[]{:S(2)}) %copy-start) | copy-done | bytes 229400
  10.4 12.2 %collective-permute-start.2 = (f32[7,8,8,128]{3,2,1,0:T(8,128)S(1)}, f32[7,8,8,128]{3,2,1,0:T(8,128)S(1)}, u32[]{:S(2)}, u32[]{:S(2)}) collective-permute-start(f32[7,8,8,128]{3,2,1,0:T(8,128)S(1)} %keep.1.kept), channel_id=1, source_target_pairs={{0,1},{2,3},{4,5},{6,7},{8,9},{10,11},{12,13},{14,15},{1,0},{3,2},... | collective-permute-start | bytes 688136 | tf_op jit(solution)/shard_map/ppermute | solution.py:345
  22.7 1.9 %collective-permute-start.3 = (f32[7,8,8,128]{3,2,1,0:T(8,128)S(1)}, f32[7,8,8,128]{3,2,1,0:T(8,128)S(1)}, u32[]{:S(2)}, u32[]{:S(2)}) collective-permute-start(f32[7,8,8,128]{3,2,1,0:T(8,128)S(1)} %keep.1.kept), channel_id=1, source_target_pairs={{1,2},{3,4},{5,6},{7,8},{9,10},{11,12},{13,14},{2,1},{4,3},{6,5},{... | collective-permute-start | bytes 688136 | tf_op jit(solution)/shard_map/ppermute | solution.py:345
  24.6 0.1 pad_add_fusion.even
  24.7 0.0 collective-permute-done.first
  24.7 0.0 collective-permute-done.1.second
  24.7 0.6 corners.1
  25.3 2.5 %collective-permute-start.4 = (f32[7,8,8,128]{3,2,1,0:T(8,128)S(1)}, f32[7,8,8,128]{3,2,1,0:T(8,128)S(1)}, u32[]{:S(2)}, u32[]{:S(2)}) collective-permute-start(f32[7,8,8,128]{3,2,1,0:T(8,128)S(1)} %get-tuple-element.12), channel_id=1, source_target_pairs={{0,1},{2,3},{4,5},{6,7},{8,9},{10,11},{12,13},{14,15},{1,0},{3,2},... | collective-permute-start | bytes 688136 | tf_op jit(solution)/shard_map/ppermute | solution.py:345
  27.9 3.0 %collective-permute-start.5 = (f32[7,8,8,128]{3,2,1,0:T(8,128)S(1)}, f32[7,8,8,128]{3,2,1,0:T(8,128)S(1)}, u32[]{:S(2)}, u32[]{:S(2)}) collective-permute-start(f32[7,8,8,128]{3,2,1,0:T(8,128)S(1)} %get-tuple-element.13), channel_id=1, source_target_pairs={{1,2},{3,4},{5,6},{7,8},{9,10},{11,12},{13,14},{2,1},{4,3},{6,5},{... | collective-permute-start | bytes 688136 | tf_op jit(solution)/shard_map/ppermute | solution.py:345
  30.9 0.0 collective-permute-done.2.first
  30.9 0.0 collective-permute-done.3.second
  30.9 0.0 collective-permute-done.4.corner_first
  31.0 4.3 %collective-permute-done.5.corner_second = f32[7,8,8,128]{3,2,1,0:T(8,128)S(1)} collective-permute-done((f32[7,8,8,128]{3,2,1,0:T(8,128)S(1)}, f32[7,8,8,128]{3,2,1,0:T(8,128)S(1)}, u32[]{:S(2)}, u32[]{:S(2)}) %collective-permute-start.5) | collective-permute-done | bytes 229408 | tf_op jit(solution)/shard_map/ppermute | solution.py:345
  35.2 3.2 %basis.3 = (f32[9,8,8,128]{3,2,1,0:T(8,128)S(1)}, f32[32,128]{1,0:T(8,128)S(1)}) custom-call(s32[2]{0:T(128)S(1)} %pad_add_fusion.even, f32[7,8,8,128]{3,2,1,0:T(8,128)S(1)} %keep.1.kept, f32[7,16,8,128]{3,2,1,0:T(8,128)S(1)} %get-tuple-element.11.strip, f32[7,8,8,128]{3,2,1,0:T(8,128)S(1)} %collective-permute-done.2.first, ...), custom_call_target="tpu_custom_call" | custom-call | tf_op jit(solution)/shard_map/basis/pallas_call | solution.py:385
  38.4 10.0 %all_to_all.22 = f32[16,2,128]{2,1,0:T(2,128)S(1)} all-to-all(f32[16,2,128]{2,1,0:T(2,128)S(1)} %bitcast.10), channel_id=1, replica_groups=mesh['gx'=64,'gz'=16] {'gz'}, dimensions={0} | all-to-all | bytes 32768 | tf_op jit(solution)/shard_map/all_to_all | solution.py:402
  48.5 31.9 %all_to_all.23 = f32[64,2,128]{2,1,0:T(2,128)S(1)} all-to-all(f32[64,2,128]{2,1,0:T(2,128)S(1)} %bitcast.7), channel_id=1, replica_groups=mesh['gx'=64,'gz'=16] {'gx'}, dimensions={0} | all-to-all | bytes 131072 | tf_op jit(solution)/shard_map/all_to_all | solution.py:411
  80.3 2.3 %factor.1 = (f32[9,8,8,128]{3,2,1,0:T(8,128)}, f32[9,9]{1,0:T(8,128)}, f32[8,9]{1,0:T(8,128)}) custom-call(f32[128,128]{1,0:T(8,128)S(1)} %bitcast.8, f32[9,8,8,128]{3,2,1,0:T(8,128)S(1)} %get-tuple-element.15.refs_1_), custom_call_target="tpu_custom_call" | custom-call | tf_op jit(solution)/shard_map/factor/pallas_call | solution.py:413
  (2 shorter events, 0.1 us)
Async XLA Ops:
  3.0 21.7 %collective-permute-start = (f32[7,8,8,128]{3,2,1,0:T(8,128)}, f32[7,8,8,128]{3,2,1,0:T(8,128)S(1)}, u32[]{:S(2)}, u32[]{:S(2)}) collective-permute-start(f32[7,8,8,128]{3,2,1,0:T(8,128)} %pack.1.own), channel_id=1, source_target_pairs={{0,16},{32,48},{64,80},{96,112},{128,144},{160,176},{192,208},{224... | collective-permute-start | bytes 688136 | tf_op jit(solution)/shard_map/ppermute | solution.py:345
  8.8 15.9 %collective-permute-start.1 = (f32[7,8,8,128]{3,2,1,0:T(8,128)}, f32[7,8,8,128]{3,2,1,0:T(8,128)S(1)}, u32[]{:S(2)}, u32[]{:S(2)}) collective-permute-start(f32[7,8,8,128]{3,2,1,0:T(8,128)} %pack.1.own), channel_id=1, source_target_pairs={{16,32},{48,64},{80,96},{112,128},{144,160},{176,192},{208,224},{2... | collective-permute-start | bytes 688136 | tf_op jit(solution)/shard_map/ppermute | solution.py:345
  9.5 0.9 %copy-start = (f32[7,8,8,128]{3,2,1,0:T(8,128)S(1)}, f32[7,8,8,128]{3,2,1,0:T(8,128)}, u32[]{:S(2)}) copy-start(f32[7,8,8,128]{3,2,1,0:T(8,128)} %pack.1.own) | copy-start | bytes 688132
  10.4 20.5 %collective-permute-start.2 = (f32[7,8,8,128]{3,2,1,0:T(8,128)S(1)}, f32[7,8,8,128]{3,2,1,0:T(8,128)S(1)}, u32[]{:S(2)}, u32[]{:S(2)}) collective-permute-start(f32[7,8,8,128]{3,2,1,0:T(8,128)S(1)} %keep.1.kept), channel_id=1, source_target_pairs={{0,1},{2,3},{4,5},{6,7},{8,9},{10,11},{12,13},{14,15},{1,0},{3,2},... | collective-permute-start | bytes 688136 | tf_op jit(solution)/shard_map/ppermute | solution.py:345
  22.7 8.3 %collective-permute-start.3 = (f32[7,8,8,128]{3,2,1,0:T(8,128)S(1)}, f32[7,8,8,128]{3,2,1,0:T(8,128)S(1)}, u32[]{:S(2)}, u32[]{:S(2)}) collective-permute-start(f32[7,8,8,128]{3,2,1,0:T(8,128)S(1)} %keep.1.kept), channel_id=1, source_target_pairs={{1,2},{3,4},{5,6},{7,8},{9,10},{11,12},{13,14},{2,1},{4,3},{6,5},{... | collective-permute-start | bytes 688136 | tf_op jit(solution)/shard_map/ppermute | solution.py:345
  25.3 5.6 %collective-permute-start.4 = (f32[7,8,8,128]{3,2,1,0:T(8,128)S(1)}, f32[7,8,8,128]{3,2,1,0:T(8,128)S(1)}, u32[]{:S(2)}, u32[]{:S(2)}) collective-permute-start(f32[7,8,8,128]{3,2,1,0:T(8,128)S(1)} %get-tuple-element.12), channel_id=1, source_target_pairs={{0,1},{2,3},{4,5},{6,7},{8,9},{10,11},{12,13},{14,15},{1,0},{3,2},... | collective-permute-start | bytes 688136 | tf_op jit(solution)/shard_map/ppermute | solution.py:345
  27.9 7.3 %collective-permute-start.5 = (f32[7,8,8,128]{3,2,1,0:T(8,128)S(1)}, f32[7,8,8,128]{3,2,1,0:T(8,128)S(1)}, u32[]{:S(2)}, u32[]{:S(2)}) collective-permute-start(f32[7,8,8,128]{3,2,1,0:T(8,128)S(1)} %get-tuple-element.13), channel_id=1, source_target_pairs={{1,2},{3,4},{5,6},{7,8},{9,10},{11,12},{13,14},{2,1},{4,3},{6,5},{... | collective-permute-start | bytes 688136 | tf_op jit(solution)/shard_map/ppermute | solution.py:345

commit v4 on v3

--- a/solution.py
+++ b/solution.py
@@ -54,6 +54,11 @@
 def pair_add(a, b):
     s, e = two_sum(a[0], b[0])
     return fast_two_sum(s, e + (a[1] + b[1]))
+
+
+def loose_add(a, b):
+    s, e = two_sum(a[0], b[0])
+    return s, e + (a[1] + b[1])
 
 
 def pair_mul(a, b):
@@ -92,7 +97,7 @@
         out[4 + dim] = (diffusivity[dim] + speed[dim] * (1.0 - flow)) * factor
 
 
-def corner_kernel(even, first, second, strip, to_first, to_second):
+def corner_kernel(even, second, first, strip, to_first, to_second):
     @pl.when(even[0] == 1)
     def _():
         strip[:, 0:B] = second[...]
@@ -174,7 +179,7 @@
 
 
 def basis_kernel(
-    even, kept, strip, first, second, corner_first, corner_second, block, gram, coeff, field, high, low
+    even, kept, strip, second, first, corner_second, corner_first, block, gram, coeff, field, high, low
 ):
     @pl.when(even[1] == 1)
     def _():
@@ -221,7 +226,7 @@
             else:
                 total, err = two_sum(total, p)
                 rest = rest + (e + err)
-        return fast_two_sum(total, rest)
+        return total, rest
 
     row = iota((B, LANES), 0)
     lane = iota((B, LANES), 1)
@@ -233,7 +238,7 @@
         a = nothing if a is None else a
         b = nothing if b is None else b
         mask = ((row if axis == 0 else lane) & distance) == 0
-        return pair_add(pair_where(mask, a, b), pair_roll(pair_where(mask, b, a), distance, axis))
+        return loose_add(pair_where(mask, a, b), pair_roll(pair_where(mask, b, a), distance, axis))
 
     def fold(items, axis):
         distance = 1
@@ -252,7 +257,8 @@
         slots.append(fold(items, 0))
     table = fold(slots, 1)
     for distance in (16, 32, 64):
-        table = pair_add(table, pair_roll(table, distance, 1))
+        table = loose_add(table, pair_roll(table, distance, 1))
+    table = fast_two_sum(*table)
     mine = lane // 16 == row
     rows = [jnp.sum(jnp.where(mine, part, 0.0), axis=0, keepdims=True) for part in table]
     tile = jnp.where(row % 2 == 0, rows[0], rows[1])
@@ -363,14 +369,14 @@
         compiler_params=ALL_VMEM,
         name="pack",
     )(restart_column, previous_basis, diffusivity, speed, upwind)
+    second_x = paired(own, "gx", 1)
     first_x = paired(own, "gx", 0)
-    second_x = paired(own, "gx", 1)
     brick = jax.ShapeDtypeStruct((FIELDS, B, B, LANES), F32)
     kept = pl.pallas_call(
         keep_kernel, out_shape=brick, in_specs=[VMEM], out_specs=VMEM, compiler_params=PARAMS, name="keep"
     )(own)
+    second_y = paired(kept, "gz", 1)
     first_y = paired(kept, "gz", 0)
-    second_y = paired(kept, "gz", 1)
     strip, to_first, to_second = pl.pallas_call(
         corner_kernel,
         out_shape=(jax.ShapeDtypeStruct((FIELDS, 2 * B, B, LANES), F32), brick, brick),
@@ -378,9 +384,9 @@
         out_specs=(VMEM,) * 3,
         compiler_params=PARAMS,
         name="corners",
-    )(even, first_x, second_x)
+    )(even, second_x, first_x)
+    second_corner = paired(to_second, "gz", 1)
     first_corner = paired(to_first, "gz", 0)
-    second_corner = paired(to_second, "gz", 1)
     wide = (WIDE, WIDE, LANES)
     block, gram = pl.pallas_call(
         basis_kernel,
@@ -398,7 +404,7 @@
         ],
         compiler_params=PARAMS,
         name="basis",
-    )(even, kept, strip, first_y, second_y, first_corner, second_corner)
+    )(even, kept, strip, second_y, first_y, second_corner, first_corner)
     parts = lax.all_to_all(gram, "gz", 0, 0, tiled=True)
     line = pl.pallas_call(
         sum_kernel,

time: 83 us -> 79.2 us (0.954)
  waiting for transfers between devices: 4.27 us -> 2.21 us
  starting transfers between devices: 26.1 us -> 24.4 us
    all_to_all x1, blocking collectives: 31.9 us -> 29.7 us  [body(): parts = lax.all_to_all(line, 'gx', 0, 0, tiled=True)]
    all_to_all x1, blocking collectives: 10 us -> 12.2 us  [body(): parts = lax.all_to_all(gram, 'gz', 0, 0, tiled=True)]
    ppermute x6, waiting for transfers between devices: 4.27 us -> 2.21 us  [paired(): lax.ppermute(array, axis, [(i, i + 1) for i in lower] + [(i + 1, i) for i...]
    ppermute x6, starting transfers between devices: 26.1 us -> 24.4 us  [paired(): lax.ppermute(array, axis, [(i, i + 1) for i in lower] + [(i + 1, i) for i...]
where the time goes in v4:
time: 79.2 us; the launch traced here: 78.9 us
  blocking collectives  41.9 us (53%)
  starting transfers between devices  24.4 us (31%)
  Pallas kernels  7.9 us (10%)
  waiting for transfers between devices  2.21 us (3%)
  between operations  1.4 us (2%)
  local copies, waits for them, and re-layouts  0.94 us (1%)
    all_to_all x1, blocking collectives, body(): parts = lax.all_to_all(line, 'gx', 0, 0, tiled=True)  29.7 us
    ppermute x6, starting transfers between devices, paired(): lax.ppermute(array, axis, [(i, i + 1) for i in lower] + [(i + 1, i) for i...  24.4 us
    all_to_all x1, blocking collectives, body(): parts = lax.all_to_all(gram, 'gz', 0, 0, tiled=True)  12.2 us
    pallas_call x1, Pallas kernels, body(): pl.pallas_call(basis_kernel, out_shape=(jax.ShapeDtypeStruct((COLS, B, B,...  3.16 us
    pallas_call x1, Pallas kernels, body(): pl.pallas_call(lambda *refs: factor_kernel(scale, *refs), out_shape=(jax....  2.3 us
    ppermute x6, waiting for transfers between devices, paired(): lax.ppermute(array, axis, [(i, i + 1) for i in lower] + [(i + 1, i) for i...  2.21 us
    pallas_call x1, Pallas kernels, body(): pl.pallas_call(pack_kernel, out_shape=jax.ShapeDtypeStruct((FIELDS, B, B,...  1.76 us
  transfers between devices with their start and end apart: 6, of which 1 were waited for; matrix products, arithmetic and copies ran while one was open for 0% of the time, Pallas kernels for 1%

profile of v4, /device:TPU:1, one launch (start us, length us, event | category | flops | bytes accessed | tf_op | source)
XLA Modules:
  0.0 78.9 jit_solution(3021772420208744754)
XLA Ops:
  1.3 1.8 %pack.1.own = f32[7,8,8,128]{3,2,1,0:T(8,128)} custom-call(s32[1]{0:T(128)S(6)} %copy.8.column, f32[4,8,8,128]{3,2,1,0:T(8,128)} %basis.2, f32[3,8,8,128]{3,2,1,0:T(8,128)} %diffusivity_in.1, f32[3,8,8,128]{3,2,1,0:T(8,128)} %speed_in.1, s32[3,8,8,128]{3,2,1,0:T(8,128)} %upwind_in.1), custom_call_target="tpu_custom_call" | custom-call | tf_op jit(solution)/shard_map/pack/pallas_call | solution.py:358
  3.0 0.7 collective-permute-start
  3.7 10.0 %collective-permute-start.1 = (f32[7,8,8,128]{3,2,1,0:T(8,128)}, f32[7,8,8,128]{3,2,1,0:T(8,128)S(1)}, u32[]{:S(2)}, u32[]{:S(2)}) collective-permute-start(f32[7,8,8,128]{3,2,1,0:T(8,128)} %pack.1.own), channel_id=1, source_target_pairs={{0,16},{32,48},{64,80},{96,112},{128,144},{160,176},{192,208},{224... | collective-permute-start | bytes 688136 | tf_op jit(solution)/shard_map/ppermute | solution.py:351
  13.7 0.0 copy-start
  13.7 0.9 %copy-done = f32[7,8,8,128]{3,2,1,0:T(8,128)S(1)} copy-done((f32[7,8,8,128]{3,2,1,0:T(8,128)S(1)}, f32[7,8,8,128]{3,2,1,0:T(8,128)}, u32[]{:S(2)}) %copy-start) | copy-done | bytes 229400
  14.7 4.2 %collective-permute-start.2 = (f32[7,8,8,128]{3,2,1,0:T(8,128)S(1)}, f32[7,8,8,128]{3,2,1,0:T(8,128)S(1)}, u32[]{:S(2)}, u32[]{:S(2)}) collective-permute-start(f32[7,8,8,128]{3,2,1,0:T(8,128)S(1)} %keep.1.kept), channel_id=1, source_target_pairs={{1,2},{3,4},{5,6},{7,8},{9,10},{11,12},{13,14},{2,1},{4,3},{6,5},{... | collective-permute-start | bytes 688136 | tf_op jit(solution)/shard_map/ppermute | solution.py:351
  18.9 4.4 %collective-permute-start.3 = (f32[7,8,8,128]{3,2,1,0:T(8,128)S(1)}, f32[7,8,8,128]{3,2,1,0:T(8,128)S(1)}, u32[]{:S(2)}, u32[]{:S(2)}) collective-permute-start(f32[7,8,8,128]{3,2,1,0:T(8,128)S(1)} %keep.1.kept), channel_id=1, source_target_pairs={{0,1},{2,3},{4,5},{6,7},{8,9},{10,11},{12,13},{14,15},{1,0},{3,2},... | collective-permute-start | bytes 688136 | tf_op jit(solution)/shard_map/ppermute | solution.py:351
  23.4 0.1 pad_add_fusion.even
  23.5 0.0 collective-permute-done.second
  23.5 0.0 collective-permute-done.1.first
  23.5 0.6 corners.1
  24.1 1.9 %collective-permute-start.4 = (f32[7,8,8,128]{3,2,1,0:T(8,128)S(1)}, f32[7,8,8,128]{3,2,1,0:T(8,128)S(1)}, u32[]{:S(2)}, u32[]{:S(2)}) collective-permute-start(f32[7,8,8,128]{3,2,1,0:T(8,128)S(1)} %get-tuple-element.12), channel_id=1, source_target_pairs={{1,2},{3,4},{5,6},{7,8},{9,10},{11,12},{13,14},{2,1},{4,3},{6,5},{... | collective-permute-start | bytes 688136 | tf_op jit(solution)/shard_map/ppermute | solution.py:351
  26.0 3.2 %collective-permute-start.5 = (f32[7,8,8,128]{3,2,1,0:T(8,128)S(1)}, f32[7,8,8,128]{3,2,1,0:T(8,128)S(1)}, u32[]{:S(2)}, u32[]{:S(2)}) collective-permute-start(f32[7,8,8,128]{3,2,1,0:T(8,128)S(1)} %get-tuple-element.13), channel_id=1, source_target_pairs={{0,1},{2,3},{4,5},{6,7},{8,9},{10,11},{12,13},{14,15},{1,0},{3,2},... | collective-permute-start | bytes 688136 | tf_op jit(solution)/shard_map/ppermute | solution.py:351
  29.2 0.0 collective-permute-done.2.second
  29.2 0.0 collective-permute-done.3.first
  29.3 2.2 %collective-permute-done.4.corner_second = f32[7,8,8,128]{3,2,1,0:T(8,128)S(1)} collective-permute-done((f32[7,8,8,128]{3,2,1,0:T(8,128)S(1)}, f32[7,8,8,128]{3,2,1,0:T(8,128)S(1)}, u32[]{:S(2)}, u32[]{:S(2)}) %collective-permute-start.4) | collective-permute-done | bytes 229408 | tf_op jit(solution)/shard_map/ppermute | solution.py:351
  31.5 0.0 collective-permute-done.5.corner_first
  31.5 3.2 %basis.3 = (f32[9,8,8,128]{3,2,1,0:T(8,128)S(1)}, f32[32,128]{1,0:T(8,128)S(1)}) custom-call(s32[2]{0:T(128)S(1)} %pad_add_fusion.even, f32[7,8,8,128]{3,2,1,0:T(8,128)S(1)} %keep.1.kept, f32[7,16,8,128]{3,2,1,0:T(8,128)S(1)} %get-tuple-element.11.strip, f32[7,8,8,128]{3,2,1,0:T(8,128)S(1)} %collective-permute-done.2.second, ...), custom_call_target="tpu_custom_call" | custom-call | tf_op jit(solution)/shard_map/basis/pallas_call | solution.py:391
  34.6 12.2 %all_to_all.22 = f32[16,2,128]{2,1,0:T(2,128)S(1)} all-to-all(f32[16,2,128]{2,1,0:T(2,128)S(1)} %bitcast.10), channel_id=1, replica_groups=mesh['gx'=64,'gz'=16] {'gz'}, dimensions={0} | all-to-all | bytes 32768 | tf_op jit(solution)/shard_map/all_to_all | solution.py:408
  46.8 29.7 %all_to_all.23 = f32[64,2,128]{2,1,0:T(2,128)S(1)} all-to-all(f32[64,2,128]{2,1,0:T(2,128)S(1)} %bitcast.7), channel_id=1, replica_groups=mesh['gx'=64,'gz'=16] {'gx'}, dimensions={0} | all-to-all | bytes 131072 | tf_op jit(solution)/shard_map/all_to_all | solution.py:417
  76.6 2.3 %factor.1 = (f32[9,8,8,128]{3,2,1,0:T(8,128)}, f32[9,9]{1,0:T(8,128)}, f32[8,9]{1,0:T(8,128)}) custom-call(f32[128,128]{1,0:T(8,128)S(1)} %bitcast.8, f32[9,8,8,128]{3,2,1,0:T(8,128)S(1)} %get-tuple-element.15.refs_1_), custom_call_target="tpu_custom_call" | custom-call | tf_op jit(solution)/shard_map/factor/pallas_call | solution.py:419
  (2 shorter events, 0.1 us)
Async XLA Ops:
  3.0 20.4 %collective-permute-start = (f32[7,8,8,128]{3,2,1,0:T(8,128)}, f32[7,8,8,128]{3,2,1,0:T(8,128)S(1)}, u32[]{:S(2)}, u32[]{:S(2)}) collective-permute-start(f32[7,8,8,128]{3,2,1,0:T(8,128)} %pack.1.own), channel_id=1, source_target_pairs={{16,32},{48,64},{80,96},{112,128},{144,160},{176,192},{208,224},{2... | collective-permute-start | bytes 688136 | tf_op jit(solution)/shard_map/ppermute | solution.py:351
  3.7 19.8 %collective-permute-start.1 = (f32[7,8,8,128]{3,2,1,0:T(8,128)}, f32[7,8,8,128]{3,2,1,0:T(8,128)S(1)}, u32[]{:S(2)}, u32[]{:S(2)}) collective-permute-start(f32[7,8,8,128]{3,2,1,0:T(8,128)} %pack.1.own), channel_id=1, source_target_pairs={{0,16},{32,48},{64,80},{96,112},{128,144},{160,176},{192,208},{224... | collective-permute-start | bytes 688136 | tf_op jit(solution)/shard_map/ppermute | solution.py:351
  13.7 0.9 %copy-start = (f32[7,8,8,128]{3,2,1,0:T(8,128)S(1)}, f32[7,8,8,128]{3,2,1,0:T(8,128)}, u32[]{:S(2)}) copy-start(f32[7,8,8,128]{3,2,1,0:T(8,128)} %pack.1.own) | copy-start | bytes 688132
  14.7 14.6 %collective-permute-start.2 = (f32[7,8,8,128]{3,2,1,0:T(8,128)S(1)}, f32[7,8,8,128]{3,2,1,0:T(8,128)S(1)}, u32[]{:S(2)}, u32[]{:S(2)}) collective-permute-start(f32[7,8,8,128]{3,2,1,0:T(8,128)S(1)} %keep.1.kept), channel_id=1, source_target_pairs={{1,2},{3,4},{5,6},{7,8},{9,10},{11,12},{13,14},{2,1},{4,3},{6,5},{... | collective-permute-start | bytes 688136 | tf_op jit(solution)/shard_map/ppermute | solution.py:351
  18.9 10.3 %collective-permute-start.3 = (f32[7,8,8,128]{3,2,1,0:T(8,128)S(1)}, f32[7,8,8,128]{3,2,1,0:T(8,128)S(1)}, u32[]{:S(2)}, u32[]{:S(2)}) collective-permute-start(f32[7,8,8,128]{3,2,1,0:T(8,128)S(1)} %keep.1.kept), channel_id=1, source_target_pairs={{0,1},{2,3},{4,5},{6,7},{8,9},{10,11},{12,13},{14,15},{1,0},{3,2},... | collective-permute-start | bytes 688136 | tf_op jit(solution)/shard_map/ppermute | solution.py:351
  24.1 7.3 %collective-permute-start.4 = (f32[7,8,8,128]{3,2,1,0:T(8,128)S(1)}, f32[7,8,8,128]{3,2,1,0:T(8,128)S(1)}, u32[]{:S(2)}, u32[]{:S(2)}) collective-permute-start(f32[7,8,8,128]{3,2,1,0:T(8,128)S(1)} %get-tuple-element.12), channel_id=1, source_target_pairs={{1,2},{3,4},{5,6},{7,8},{9,10},{11,12},{13,14},{2,1},{4,3},{6,5},{... | collective-permute-start | bytes 688136 | tf_op jit(solution)/shard_map/ppermute | solution.py:351
  26.0 5.4 %collective-permute-start.5 = (f32[7,8,8,128]{3,2,1,0:T(8,128)S(1)}, f32[7,8,8,128]{3,2,1,0:T(8,128)S(1)}, u32[]{:S(2)}, u32[]{:S(2)}) collective-permute-start(f32[7,8,8,128]{3,2,1,0:T(8,128)S(1)} %get-tuple-element.13), channel_id=1, source_target_pairs={{0,1},{2,3},{4,5},{6,7},{8,9},{10,11},{12,13},{14,15},{1,0},{3,2},... | collective-permute-start | bytes 688136 | tf_op jit(solution)/shard_map/ppermute | solution.py:351

commit v5 on v4

--- a/solution.py
+++ b/solution.py
@@ -20,7 +20,6 @@
 HBM = pl.BlockSpec(memory_space=pltpu.HBM)
 SMEM = pl.BlockSpec(memory_space=pltpu.SMEM)
 PARAMS = pltpu.CompilerParams(vmem_limit_bytes=16 * 1024 * 1024)
-ALL_VMEM = pltpu.CompilerParams(vmem_limit_bytes=63 * 1024 * 1024)
 
 
 def iota(shape, dim):
@@ -132,14 +131,10 @@
                 to_last[:, at] = jnp.where(row < B - m, near, pltpu.roll(far, B - m, 1))
 
 
-def keep_kernel(own, kept):
-    kept[...] = own[...]
-
-
-def start_fields(kept, strip, last, following, corner_last, corner_following, coeff, field):
+def start_fields(own, strip, last, following, corner_last, corner_following, coeff, field):
     def wide(f, a):
         if B <= a < 2 * B:
-            return jnp.concatenate([last[f, a - B], kept[f, a - B], following[f, a - B]], 0)
+            return jnp.concatenate([last[f, a - B], own[f, a - B], following[f, a - B]], 0)
         side = 0 if a < B else 1
         m = B - a if side == 0 else a - (2 * B - 1)
         middle = strip[f, a if side == 0 else a - B]
@@ -179,17 +174,17 @@
 
 
 def basis_kernel(
-    even, kept, strip, second, first, corner_second, corner_first, block, gram, coeff, field, high, low
+    even, own, strip, second, first, corner_second, corner_first, block, gram, coeff, field, high, low
 ):
     @pl.when(even[1] == 1)
     def _():
-        start_fields(kept, strip, second, first, corner_second, corner_first, coeff, field)
+        start_fields(own, strip, second, first, corner_second, corner_first, coeff, field)
 
     @pl.when(even[1] == 0)
     def _():
-        start_fields(kept, strip, first, second, corner_first, corner_second, coeff, field)
-
-    block[0] = kept[0]
+        start_fields(own, strip, first, second, corner_first, corner_second, coeff, field)
+
+    block[0] = own[0]
     for k in range(1, COLS):
         src, dst = (k - 1) % 2, k % 2
 
@@ -351,13 +346,17 @@
     return lax.ppermute(array, axis, [(i, i + 1) for i in lower] + [(i + 1, i) for i in lower])
 
 
+def in_hbm(array):
+    return pltpu.with_memory_space_constraint(array, pltpu.HBM)
+
+
 def body(previous_basis, restart_column, diffusivity, speed, upwind):
     count_x, count_y = lax.axis_size("gx"), lax.axis_size("gz")
     even = jnp.stack([1 - lax.axis_index("gx") % 2, 1 - lax.axis_index("gz") % 2]).astype(jnp.int32)
     faces = (3, B, B, LANES)
     own = pl.pallas_call(
         pack_kernel,
-        out_shape=jax.ShapeDtypeStruct((FIELDS, B, B, LANES), F32),
+        out_shape=pltpu.VMEM((FIELDS, B, B, LANES), F32),
         in_specs=[SMEM] + [HBM] * 4,
         out_specs=VMEM,
         scratch_shapes=[
@@ -366,17 +365,14 @@
             pltpu.VMEM(faces, jnp.int32),
             pltpu.SemaphoreType.DMA((4,)),
         ],
-        compiler_params=ALL_VMEM,
+        compiler_params=PARAMS,
         name="pack",
-    )(restart_column, previous_basis, diffusivity, speed, upwind)
+    )(restart_column, *(in_hbm(array) for array in (previous_basis, diffusivity, speed, upwind)))
     second_x = paired(own, "gx", 1)
     first_x = paired(own, "gx", 0)
     brick = jax.ShapeDtypeStruct((FIELDS, B, B, LANES), F32)
-    kept = pl.pallas_call(
-        keep_kernel, out_shape=brick, in_specs=[VMEM], out_specs=VMEM, compiler_params=PARAMS, name="keep"
-    )(own)
-    second_y = paired(kept, "gz", 1)
-    first_y = paired(kept, "gz", 0)
+    second_y = paired(own, "gz", 1)
+    first_y = paired(own, "gz", 0)
     strip, to_first, to_second = pl.pallas_call(
         corner_kernel,
         out_shape=(jax.ShapeDtypeStruct((FIELDS, 2 * B, B, LANES), F32), brick, brick),
@@ -404,7 +400,7 @@
         ],
         compiler_params=PARAMS,
         name="basis",
-    )(even, kept, strip, second_y, first_y, second_corner, first_corner)
+    )(even, own, strip, second_y, first_y, second_corner, first_corner)
     parts = lax.all_to_all(gram, "gz", 0, 0, tiled=True)
     line = pl.pallas_call(
         sum_kernel,

time: 79.2 us -> 78.4 us (0.990)
  local copies, waits for them, and re-layouts: 0.94 us -> 0 us
  blocking collectives: 41.9 us -> 42.7 us
  starting transfers between devices: 24.4 us -> 25.2 us
    unnamed x2 -> x0, local copies, waits for them, and re-layouts: 0.94 us -> none
    pallas_call x2 -> x1, Pallas kernels: 1.77 us -> 1.07 us  [body(): pl.pallas_call(pack_kernel, out_shape=pltpu.VMEM((FIELDS, B, B, LANES), F...]
where the time goes in v5:
time: 78.4 us; the launch traced here: 78 us
  blocking collectives  42.7 us (54%)
  starting transfers between devices  25.2 us (32%)
  Pallas kernels  7.24 us (9%)
  waiting for transfers between devices  1.45 us (2%)
  between operations  1.39 us (2%)
    all_to_all x1, blocking collectives, body(): parts = lax.all_to_all(line, 'gx', 0, 0, tiled=True)  29.8 us
    ppermute x6, starting transfers between devices, paired(): lax.ppermute(array, axis, [(i, i + 1) for i in lower] + [(i + 1, i) for i...  25.2 us
    all_to_all x1, blocking collectives, body(): parts = lax.all_to_all(gram, 'gz', 0, 0, tiled=True)  12.8 us
    pallas_call x1, Pallas kernels, body(): pl.pallas_call(basis_kernel, out_shape=(jax.ShapeDtypeStruct((COLS, B, B,...  3.19 us
    pallas_call x1, Pallas kernels, body(): pl.pallas_call(lambda *refs: factor_kernel(scale, *refs), out_shape=(jax....  2.3 us
  transfers between devices with their start and end apart: 6, of which 1 were waited for; matrix products, arithmetic and copies ran while one was open for 0% of the time, Pallas kernels for 1%

profile of v5, /device:TPU:1, one launch (start us, length us, event | category | flops | bytes accessed | tf_op | source)
XLA Modules:
  0.0 78.0 jit_solution(1905710896199786925)
XLA Ops:
  1.3 1.1 %pack.1.own = f32[7,8,8,128]{3,2,1,0:T(8,128)S(1)} custom-call(s32[1]{0:T(128)S(6)} %copy.8.column, f32[4,8,8,128]{3,2,1,0:T(8,128)} %basis.2, f32[3,8,8,128]{3,2,1,0:T(8,128)} %diffusivity_in.1, f32[3,8,8,128]{3,2,1,0:T(8,128)} %speed_in.1, s32[3,8,8,128]{3,2,1,0:T(8,128)} %upwind_in.1), custom_call_target="tpu_custom_call" | custom-call | tf_op jit(solution)/shard_map/pack/pallas_call | solution.py:357
  2.4 0.7 collective-permute-start
  3.0 10.0 %collective-permute-start.1 = (f32[7,8,8,128]{3,2,1,0:T(8,128)S(1)}, f32[7,8,8,128]{3,2,1,0:T(8,128)S(1)}, u32[]{:S(2)}, u32[]{:S(2)}) collective-permute-start(f32[7,8,8,128]{3,2,1,0:T(8,128)S(1)} %pack.1.own), channel_id=1, source_target_pairs={{0,16},{32,48},{64,80},{96,112},{128,144},{160,176},{192,208},{224... | collective-permute-start | bytes 688136 | tf_op jit(solution)/shard_map/ppermute | solution.py:346
  13.0 4.2 %collective-permute-start.2 = (f32[7,8,8,128]{3,2,1,0:T(8,128)S(1)}, f32[7,8,8,128]{3,2,1,0:T(8,128)S(1)}, u32[]{:S(2)}, u32[]{:S(2)}) collective-permute-start(f32[7,8,8,128]{3,2,1,0:T(8,128)S(1)} %pack.1.own), channel_id=1, source_target_pairs={{1,2},{3,4},{5,6},{7,8},{9,10},{11,12},{13,14},{2,1},{4,3},{6,5},{... | collective-permute-start | bytes 688136 | tf_op jit(solution)/shard_map/ppermute | solution.py:346
  17.3 4.4 %collective-permute-start.3 = (f32[7,8,8,128]{3,2,1,0:T(8,128)S(1)}, f32[7,8,8,128]{3,2,1,0:T(8,128)S(1)}, u32[]{:S(2)}, u32[]{:S(2)}) collective-permute-start(f32[7,8,8,128]{3,2,1,0:T(8,128)S(1)} %pack.1.own), channel_id=1, source_target_pairs={{0,1},{2,3},{4,5},{6,7},{8,9},{10,11},{12,13},{14,15},{1,0},{3,2},... | collective-permute-start | bytes 688136 | tf_op jit(solution)/shard_map/ppermute | solution.py:346
  21.7 0.1 pad_add_fusion.even
  21.8 0.0 collective-permute-done.second
  21.8 0.0 collective-permute-done.1.first
  21.8 0.6 corners.1
  22.5 1.9 %collective-permute-start.4 = (f32[7,8,8,128]{3,2,1,0:T(8,128)S(1)}, f32[7,8,8,128]{3,2,1,0:T(8,128)S(1)}, u32[]{:S(2)}, u32[]{:S(2)}) collective-permute-start(f32[7,8,8,128]{3,2,1,0:T(8,128)S(1)} %get-tuple-element.12), channel_id=1, source_target_pairs={{1,2},{3,4},{5,6},{7,8},{9,10},{11,12},{13,14},{2,1},{4,3},{6,5},{... | collective-permute-start | bytes 688136 | tf_op jit(solution)/shard_map/ppermute | solution.py:346
  24.4 3.9 %collective-permute-start.5 = (f32[7,8,8,128]{3,2,1,0:T(8,128)S(1)}, f32[7,8,8,128]{3,2,1,0:T(8,128)S(1)}, u32[]{:S(2)}, u32[]{:S(2)}) collective-permute-start(f32[7,8,8,128]{3,2,1,0:T(8,128)S(1)} %get-tuple-element.13), channel_id=1, source_target_pairs={{0,1},{2,3},{4,5},{6,7},{8,9},{10,11},{12,13},{14,15},{1,0},{3,2},... | collective-permute-start | bytes 688136 | tf_op jit(solution)/shard_map/ppermute | solution.py:346
  28.3 0.0 collective-permute-done.2.second
  28.4 0.0 collective-permute-done.3.first
  28.4 1.4 %collective-permute-done.4.corner_second = f32[7,8,8,128]{3,2,1,0:T(8,128)S(1)} collective-permute-done((f32[7,8,8,128]{3,2,1,0:T(8,128)S(1)}, f32[7,8,8,128]{3,2,1,0:T(8,128)S(1)}, u32[]{:S(2)}, u32[]{:S(2)}) %collective-permute-start.4) | collective-permute-done | bytes 229408 | tf_op jit(solution)/shard_map/ppermute | solution.py:346
  29.8 0.0 collective-permute-done.5.corner_first
  29.8 3.2 %basis.3 = (f32[9,8,8,128]{3,2,1,0:T(8,128)S(1)}, f32[32,128]{1,0:T(8,128)S(1)}) custom-call(s32[2]{0:T(128)S(1)} %pad_add_fusion.even, f32[7,8,8,128]{3,2,1,0:T(8,128)S(1)} %pack.1.own, f32[7,16,8,128]{3,2,1,0:T(8,128)S(1)} %get-tuple-element.11.strip, f32[7,8,8,128]{3,2,1,0:T(8,128)S(1)} %collective-permute-done.2.second, ...), custom_call_target="tpu_custom_call" | custom-call | tf_op jit(solution)/shard_map/basis/pallas_call | solution.py:387
  33.0 12.8 %all_to_all.22 = f32[16,2,128]{2,1,0:T(2,128)S(1)} all-to-all(f32[16,2,128]{2,1,0:T(2,128)S(1)} %bitcast.10), channel_id=1, replica_groups=mesh['gx'=64,'gz'=16] {'gz'}, dimensions={0} | all-to-all | bytes 32768 | tf_op jit(solution)/shard_map/all_to_all | solution.py:404
  45.9 29.8 %all_to_all.23 = f32[64,2,128]{2,1,0:T(2,128)S(1)} all-to-all(f32[64,2,128]{2,1,0:T(2,128)S(1)} %bitcast.7), channel_id=1, replica_groups=mesh['gx'=64,'gz'=16] {'gx'}, dimensions={0} | all-to-all | bytes 131072 | tf_op jit(solution)/shard_map/all_to_all | solution.py:413
  75.7 2.3 %factor.1 = (f32[9,8,8,128]{3,2,1,0:T(8,128)}, f32[9,9]{1,0:T(8,128)}, f32[8,9]{1,0:T(8,128)}) custom-call(f32[128,128]{1,0:T(8,128)S(1)} %bitcast.8, f32[9,8,8,128]{3,2,1,0:T(8,128)S(1)} %get-tuple-element.15.refs_1_), custom_call_target="tpu_custom_call" | custom-call | tf_op jit(solution)/shard_map/factor/pallas_call | solution.py:415
  (1 shorter events, 0.0 us)
Async XLA Ops:
  2.4 19.5 %collective-permute-start = (f32[7,8,8,128]{3,2,1,0:T(8,128)S(1)}, f32[7,8,8,128]{3,2,1,0:T(8,128)S(1)}, u32[]{:S(2)}, u32[]{:S(2)}) collective-permute-start(f32[7,8,8,128]{3,2,1,0:T(8,128)S(1)} %pack.1.own), channel_id=1, source_target_pairs={{16,32},{48,64},{80,96},{112,128},{144,160},{176,192},{208,224},{2... | collective-permute-start | bytes 688136 | tf_op jit(solution)/shard_map/ppermute | solution.py:346
  3.0 18.8 %collective-permute-start.1 = (f32[7,8,8,128]{3,2,1,0:T(8,128)S(1)}, f32[7,8,8,128]{3,2,1,0:T(8,128)S(1)}, u32[]{:S(2)}, u32[]{:S(2)}) collective-permute-start(f32[7,8,8,128]{3,2,1,0:T(8,128)S(1)} %pack.1.own), channel_id=1, source_target_pairs={{0,16},{32,48},{64,80},{96,112},{128,144},{160,176},{192,208},{224... | collective-permute-start | bytes 688136 | tf_op jit(solution)/shard_map/ppermute | solution.py:346
  13.0 15.3 %collective-permute-start.2 = (f32[7,8,8,128]{3,2,1,0:T(8,128)S(1)}, f32[7,8,8,128]{3,2,1,0:T(8,128)S(1)}, u32[]{:S(2)}, u32[]{:S(2)}) collective-permute-start(f32[7,8,8,128]{3,2,1,0:T(8,128)S(1)} %pack.1.own), channel_id=1, source_target_pairs={{1,2},{3,4},{5,6},{7,8},{9,10},{11,12},{13,14},{2,1},{4,3},{6,5},{... | collective-permute-start | bytes 688136 | tf_op jit(solution)/shard_map/ppermute | solution.py:346
  17.3 11.1 %collective-permute-start.3 = (f32[7,8,8,128]{3,2,1,0:T(8,128)S(1)}, f32[7,8,8,128]{3,2,1,0:T(8,128)S(1)}, u32[]{:S(2)}, u32[]{:S(2)}) collective-permute-start(f32[7,8,8,128]{3,2,1,0:T(8,128)S(1)} %pack.1.own), channel_id=1, source_target_pairs={{0,1},{2,3},{4,5},{6,7},{8,9},{10,11},{12,13},{14,15},{1,0},{3,2},... | collective-permute-start | bytes 688136 | tf_op jit(solution)/shard_map/ppermute | solution.py:346
  22.5 7.3 %collective-permute-start.4 = (f32[7,8,8,128]{3,2,1,0:T(8,128)S(1)}, f32[7,8,8,128]{3,2,1,0:T(8,128)S(1)}, u32[]{:S(2)}, u32[]{:S(2)}) collective-permute-start(f32[7,8,8,128]{3,2,1,0:T(8,128)S(1)} %get-tuple-element.12), channel_id=1, source_target_pairs={{1,2},{3,4},{5,6},{7,8},{9,10},{11,12},{13,14},{2,1},{4,3},{6,5},{... | collective-permute-start | bytes 688136 | tf_op jit(solution)/shard_map/ppermute | solution.py:346
  24.4 5.4 %collective-permute-start.5 = (f32[7,8,8,128]{3,2,1,0:T(8,128)S(1)}, f32[7,8,8,128]{3,2,1,0:T(8,128)S(1)}, u32[]{:S(2)}, u32[]{:S(2)}) collective-permute-start(f32[7,8,8,128]{3,2,1,0:T(8,128)S(1)} %get-tuple-element.13), channel_id=1, source_target_pairs={{0,1},{2,3},{4,5},{6,7},{8,9},{10,11},{12,13},{14,15},{1,0},{3,2},... | collective-permute-start | bytes 688136 | tf_op jit(solution)/shard_map/ppermute | solution.py:346

commit v6 on v5

--- a/solution.py
+++ b/solution.py
@@ -15,6 +15,13 @@
 WIDE = 3 * B
 LANES = 128
 FIELDS = 7
+NEAR_X = (1, 2, 3, 5, 6)
+FAR_X = 2 * B
+TILES_X = FAR_X + (B - 1) * len(NEAR_X)
+REACH = (8, 7, 7, 7, 8, 8, 7)
+HALVES = tuple(reach // 2 for reach in REACH)
+CORNER = tuple(2 * sum(HALVES[:f]) for f in range(FIELDS))
+TILES_CORNER = 2 * sum(HALVES)
 F32 = jnp.float32
 VMEM = pl.BlockSpec(memory_space=pltpu.VMEM)
 HBM = pl.BlockSpec(memory_space=pltpu.HBM)
@@ -60,9 +67,9 @@
     return s, e + (a[1] + b[1])
 
 
-def pair_mul(a, b):
+def loose_mul(a, b):
     p, e = two_prod(a[0], b[0])
-    return fast_two_sum(p, e + (a[0] * b[1] + a[1] * b[0]))
+    return p, e + (a[0] * b[1] + a[1] * b[0])
 
 
 def pair_roll(a, shift, axis):
@@ -73,7 +80,9 @@
     return tuple(jnp.where(mask, x, y) for x, y in zip(a, b))
 
 
-def pack_kernel(column, basis, diffusivity_in, speed_in, upwind_in, out, diffusivity, speed, upwind, sems):
+def pack_kernel(
+    column, even, basis, diffusivity_in, speed_in, upwind_in, out, to_first, to_second, diffusivity, speed, upwind, sems
+):
     copies = [
         pltpu.make_async_copy(src, dst, sems.at[n])
         for n, (src, dst) in enumerate(
@@ -95,17 +104,40 @@
         out[1 + dim] = (diffusivity[dim] + speed[dim] * flow) * factor
         out[4 + dim] = (diffusivity[dim] + speed[dim] * (1.0 - flow)) * factor
 
+    def emit(target, start):
+        target[0:B] = out[0]
+        target[B:FAR_X] = out[4]
+        for n, f in enumerate(NEAR_X):
+            target[FAR_X + (B - 1) * n : FAR_X + (B - 1) * (n + 1)] = out[f, start : start + B - 1]
+
+    @pl.when(even[0] == 1)
+    def _():
+        emit(to_first, 1)
+        emit(to_second, 0)
+
+    @pl.when(even[0] == 0)
+    def _():
+        emit(to_first, 0)
+        emit(to_second, 1)
+
 
 def corner_kernel(even, second, first, strip, to_first, to_second):
+    def place(part, side, start):
+        strip[0, B * side : B * (side + 1)] = part[0:B]
+        strip[4, B * side : B * (side + 1)] = part[B:FAR_X]
+        for n, f in enumerate(NEAR_X):
+            strip[f, B * side + start : B * (side + 1) - 1 + start] = part[FAR_X + (B - 1) * n : FAR_X + (B - 1) * (n + 1)]
+            strip[f, 0 if side == 0 else 2 * B - 1] = jnp.zeros((B, LANES), F32)
+
     @pl.when(even[0] == 1)
     def _():
-        strip[:, 0:B] = second[...]
-        strip[:, B : 2 * B] = first[...]
+        place(second, 0, 1)
+        place(first, 1, 0)
 
     @pl.when(even[0] == 0)
     def _():
-        strip[:, 0:B] = first[...]
-        strip[:, B : 2 * B] = second[...]
+        place(first, 0, 1)
+        place(second, 1, 0)
 
     @pl.when(even[1] == 1)
     def _():
@@ -117,18 +149,20 @@
 
 
 def emit_corners(strip, to_next, to_last):
-    row = iota((FIELDS, B, LANES), 1)
-    for side in range(2):
-        for m in range(1, 5):
-            near = strip[:, B - m if side == 0 else B - 1 + m]
-            at = 4 * side + m - 1
-            if m == 4:
-                to_next[:, at] = near
-                to_last[:, at] = near
-            else:
-                far = strip[:, m if side == 0 else 2 * B - 1 - m]
-                to_next[:, at] = jnp.where(row >= m, near, pltpu.roll(far, m, 1))
-                to_last[:, at] = jnp.where(row < B - m, near, pltpu.roll(far, B - m, 1))
+    row = iota((B, LANES), 0)
+    for f in range(FIELDS):
+        for side in range(2):
+            for m in range(1, HALVES[f] + 1):
+                near = strip[f, B - m if side == 0 else B - 1 + m]
+                at = CORNER[f] + HALVES[f] * side + m - 1
+                other = REACH[f] - m
+                if m == other:
+                    to_next[at] = near
+                    to_last[at] = near
+                else:
+                    far = strip[f, B - other if side == 0 else B - 1 + other]
+                    to_next[at] = jnp.where(row >= m, near, pltpu.roll(far, m, 0))
+                    to_last[at] = jnp.where(row < B - m, near, pltpu.roll(far, B - m, 0))
 
 
 def start_fields(own, strip, last, following, corner_last, corner_following, coeff, field):
@@ -138,16 +172,15 @@
         side = 0 if a < B else 1
         m = B - a if side == 0 else a - (2 * B - 1)
         middle = strip[f, a if side == 0 else a - B]
-        if m == B:
+        other = REACH[f] - m
+        at = CORNER[f] + HALVES[f] * side + min(m, other) - 1
+        if other <= 0:
             lower = upper = jnp.zeros((B, LANES), F32)
-        elif m <= 4:
-            at = 4 * side + m - 1
-            lower, upper = corner_last[f, at], corner_following[f, at]
+        elif m <= other:
+            lower, upper = corner_last[at], corner_following[at]
         else:
-            other = B - m
-            at = 4 * side + other - 1
-            lower = pltpu.roll(corner_last[f, at], B - other, 0)
-            upper = pltpu.roll(corner_following[f, at], other, 0)
+            lower = pltpu.roll(corner_last[at], B - other, 0)
+            upper = pltpu.roll(corner_following[at], other, 0)
         return jnp.concatenate([lower, middle, upper], 0)
 
     lane = iota((WIDE, LANES), 1)
@@ -214,8 +247,8 @@
         total = None
         for x in range(B):
             ah, al, bh, bl = high[i, x], low[i, x], high[j, x], low[j, x]
-            p = block[i, x] * block[j, x]
-            e = ((ah * bh - p) + (ah * bl + al * bh)) + al * bl
+            p = ah * bh
+            e = ah * bl + al * block[j, x]
             if total is None:
                 total, rest = p, e
             else:
@@ -308,8 +341,7 @@
         ratio = col[0] * inv
         back, err = two_prod(ratio, d[0])
         rest = (((col[0] - back) - err) + (col[1] - ratio * d[1])) * inv
-        ratio = fast_two_sum(ratio, rest)
-        change = pair_mul(ratio, top)
+        change = loose_mul((ratio, rest), top)
         change = tuple(jnp.where(row > j, -part, 0.0) for part in change)
         high, low = pair_add((high, low), change)
     root = jnp.sqrt(pivots)
@@ -354,11 +386,12 @@
     count_x, count_y = lax.axis_size("gx"), lax.axis_size("gz")
     even = jnp.stack([1 - lax.axis_index("gx") % 2, 1 - lax.axis_index("gz") % 2]).astype(jnp.int32)
     faces = (3, B, B, LANES)
-    own = pl.pallas_call(
+    part = (TILES_X, B, LANES)
+    own, to_first, to_second = pl.pallas_call(
         pack_kernel,
-        out_shape=pltpu.VMEM((FIELDS, B, B, LANES), F32),
-        in_specs=[SMEM] + [HBM] * 4,
-        out_specs=VMEM,
+        out_shape=(pltpu.VMEM((FIELDS, B, B, LANES), F32), pltpu.VMEM(part, F32), pltpu.VMEM(part, F32)),
+        in_specs=[SMEM] * 2 + [HBM] * 4,
+        out_specs=(VMEM,) * 3,
         scratch_shapes=[
             pltpu.VMEM(faces, F32),
             pltpu.VMEM(faces, F32),
@@ -367,15 +400,15 @@
         ],
         compiler_params=PARAMS,
         name="pack",
-    )(restart_column, *(in_hbm(array) for array in (previous_basis, diffusivity, speed, upwind)))
-    second_x = paired(own, "gx", 1)
-    first_x = paired(own, "gx", 0)
-    brick = jax.ShapeDtypeStruct((FIELDS, B, B, LANES), F32)
+    )(restart_column, even, *(in_hbm(array) for array in (previous_basis, diffusivity, speed, upwind)))
+    second_x = paired(to_second, "gx", 1)
+    first_x = paired(to_first, "gx", 0)
+    corner = jax.ShapeDtypeStruct((TILES_CORNER, B, LANES), F32)
     second_y = paired(own, "gz", 1)
     first_y = paired(own, "gz", 0)
     strip, to_first, to_second = pl.pallas_call(
         corner_kernel,
-        out_shape=(jax.ShapeDtypeStruct((FIELDS, 2 * B, B, LANES), F32), brick, brick),
+        out_shape=(jax.ShapeDtypeStruct((FIELDS, 2 * B, B, LANES), F32), corner, corner),
         in_specs=[SMEM] + [VMEM] * 2,
         out_specs=(VMEM,) * 3,
         compiler_params=PARAMS,

time: 78.4 us -> 77.9 us (level)
  no operation moved by 1% of the time
where the time goes in v6:
time: 77.9 us; the launch traced here: 77.6 us
  blocking collectives  42.3 us (54%)
  starting transfers between devices  25.1 us (32%)
  Pallas kernels  7.52 us (10%)
  between operations  1.4 us (2%)
  waiting for transfers between devices  1.24 us (2%)
    all_to_all x1, blocking collectives, body(): parts = lax.all_to_all(line, 'gx', 0, 0, tiled=True)  29.8 us
    ppermute x6, starting transfers between devices, paired(): lax.ppermute(array, axis, [(i, i + 1) for i in lower] + [(i + 1, i) for i...  25.1 us
    all_to_all x1, blocking collectives, body(): parts = lax.all_to_all(gram, 'gz', 0, 0, tiled=True)  12.5 us
    pallas_call x1, Pallas kernels, body(): pl.pallas_call(basis_kernel, out_shape=(jax.ShapeDtypeStruct((COLS, B, B,...  3 us
    pallas_call x1, Pallas kernels, body(): pl.pallas_call(lambda *refs: factor_kernel(scale, *refs), out_shape=(jax....  2.22 us
    pallas_call x1, Pallas kernels, body(): pl.pallas_call(pack_kernel, out_shape=(pltpu.VMEM((FIELDS, B, B, LANES),...  1.64 us
  transfers between devices with their start and end apart: 6, of which 1 were waited for; matrix products, arithmetic and copies ran while one was open for 0% of the time, Pallas kernels for 1%

profile of v6, /device:TPU:1, one launch (start us, length us, event | category | flops | bytes accessed | tf_op | source)
XLA Modules:
  0.0 77.6 jit_solution(18129594772616316463)
XLA Ops:
  1.3 0.1 pad_add_fusion.even
  1.4 1.6 %pack.1 = (f32[7,8,8,128]{3,2,1,0:T(8,128)S(1)}, f32[51,8,128]{2,1,0:T(8,128)S(1)}, f32[51,8,128]{2,1,0:T(8,128)S(1)}) custom-call(s32[1]{0:T(128)S(6)} %copy.8.column, s32[2]{0:T(128)S(1)} %pad_add_fusion.even, f32[4,8,8,128]{3,2,1,0:T(8,128)} %basis.2, f32[3,8,8,128]{3,2,1,0:T(8,128)} %diffusivity_in.1, f32[3,8,8,128]{3,2,1,0:T(8,128)} %speed_in.1, ...), custom_call_target="tpu_custom_call" | custom-call | tf_op jit(solution)/shard_map/pack/pallas_call | solution.py:390
  3.0 0.7 collective-permute-start
  3.7 10.0 %collective-permute-start.1 = (f32[51,8,128]{2,1,0:T(8,128)S(1)}, f32[51,8,128]{2,1,0:T(8,128)S(1)}, u32[]{:S(2)}, u32[]{:S(2)}) collective-permute-start(f32[51,8,128]{2,1,0:T(8,128)S(1)} %get-tuple-element.16), channel_id=1, source_target_pairs={{0,16},{32,48},{64,80},{96,112},{128,144},{160,176},{192,208},{224... | collective-permute-start | bytes 626696 | tf_op jit(solution)/shard_map/ppermute | solution.py:378
  13.7 4.2 %collective-permute-start.2 = (f32[7,8,8,128]{3,2,1,0:T(8,128)S(1)}, f32[7,8,8,128]{3,2,1,0:T(8,128)S(1)}, u32[]{:S(2)}, u32[]{:S(2)}) collective-permute-start(f32[7,8,8,128]{3,2,1,0:T(8,128)S(1)} %get-tuple-element.14.own), channel_id=1, source_target_pairs={{1,2},{3,4},{5,6},{7,8},{9,10},{11,12},{13,14},{2,1},{4,3},{6,5},{... | collective-permute-start | bytes 688136 | tf_op jit(solution)/shard_map/ppermute | solution.py:378
  17.9 4.4 %collective-permute-start.3 = (f32[7,8,8,128]{3,2,1,0:T(8,128)S(1)}, f32[7,8,8,128]{3,2,1,0:T(8,128)S(1)}, u32[]{:S(2)}, u32[]{:S(2)}) collective-permute-start(f32[7,8,8,128]{3,2,1,0:T(8,128)S(1)} %get-tuple-element.14.own), channel_id=1, source_target_pairs={{0,1},{2,3},{4,5},{6,7},{8,9},{10,11},{12,13},{14,15},{1,0},{3,2},... | collective-permute-start | bytes 688136 | tf_op jit(solution)/shard_map/ppermute | solution.py:378
  22.4 0.0 collective-permute-done.second
  22.4 0.0 collective-permute-done.1.first
  22.4 0.6 corners.1
  23.0 1.9 %collective-permute-start.4 = (f32[48,8,128]{2,1,0:T(8,128)S(1)}, f32[48,8,128]{2,1,0:T(8,128)S(1)}, u32[]{:S(2)}, u32[]{:S(2)}) collective-permute-start(f32[48,8,128]{2,1,0:T(8,128)S(1)} %get-tuple-element.18), channel_id=1, source_target_pairs={{1,2},{3,4},{5,6},{7,8},{9,10},{11,12},{13,14},{2,1},{4,3},{6,5},{... | collective-permute-start | bytes 589832 | tf_op jit(solution)/shard_map/ppermute | solution.py:378
  25.0 3.8 %collective-permute-start.5 = (f32[48,8,128]{2,1,0:T(8,128)S(1)}, f32[48,8,128]{2,1,0:T(8,128)S(1)}, u32[]{:S(2)}, u32[]{:S(2)}) collective-permute-start(f32[48,8,128]{2,1,0:T(8,128)S(1)} %get-tuple-element.19), channel_id=1, source_target_pairs={{0,1},{2,3},{4,5},{6,7},{8,9},{10,11},{12,13},{14,15},{1,0},{3,2},... | collective-permute-start | bytes 589832 | tf_op jit(solution)/shard_map/ppermute | solution.py:378
  28.8 0.0 collective-permute-done.2.second
  28.8 0.0 collective-permute-done.3.first
  28.8 1.2 %collective-permute-done.4.corner_second = f32[48,8,128]{2,1,0:T(8,128)S(1)} collective-permute-done((f32[48,8,128]{2,1,0:T(8,128)S(1)}, f32[48,8,128]{2,1,0:T(8,128)S(1)}, u32[]{:S(2)}, u32[]{:S(2)}) %collective-permute-start.4) | collective-permute-done | bytes 196640 | tf_op jit(solution)/shard_map/ppermute | solution.py:378
  30.0 0.0 collective-permute-done.5.corner_first
  30.0 3.0 %basis.3 = (f32[9,8,8,128]{3,2,1,0:T(8,128)S(1)}, f32[32,128]{1,0:T(8,128)S(1)}) custom-call(s32[2]{0:T(128)S(1)} %pad_add_fusion.even, f32[7,8,8,128]{3,2,1,0:T(8,128)S(1)} %get-tuple-element.14.own, f32[7,16,8,128]{3,2,1,0:T(8,128)S(1)} %get-tuple-element.17.strip, f32[7,8,8,128]{3,2,1,0:T(8,128)S(1)} %collective-permute-done.2.second, ...), custom_call_target="tpu_custom_call" | custom-call | tf_op jit(solution)/shard_map/basis/pallas_call | solution.py:420
  33.0 12.5 %all_to_all.22 = f32[16,2,128]{2,1,0:T(2,128)S(1)} all-to-all(f32[16,2,128]{2,1,0:T(2,128)S(1)} %bitcast.10), channel_id=1, replica_groups=mesh['gx'=64,'gz'=16] {'gz'}, dimensions={0} | all-to-all | bytes 32768 | tf_op jit(solution)/shard_map/all_to_all | solution.py:437
  45.6 29.8 %all_to_all.23 = f32[64,2,128]{2,1,0:T(2,128)S(1)} all-to-all(f32[64,2,128]{2,1,0:T(2,128)S(1)} %bitcast.7), channel_id=1, replica_groups=mesh['gx'=64,'gz'=16] {'gx'}, dimensions={0} | all-to-all | bytes 131072 | tf_op jit(solution)/shard_map/all_to_all | solution.py:446
  75.4 2.2 %factor.1 = (f32[9,8,8,128]{3,2,1,0:T(8,128)}, f32[9,9]{1,0:T(8,128)}, f32[8,9]{1,0:T(8,128)}) custom-call(f32[128,128]{1,0:T(8,128)S(1)} %bitcast.8, f32[9,8,8,128]{3,2,1,0:T(8,128)S(1)} %get-tuple-element.21.refs_1_), custom_call_target="tpu_custom_call" | custom-call | tf_op jit(solution)/shard_map/factor/pallas_call | solution.py:448
  (1 shorter events, 0.0 us)
Async XLA Ops:
  3.0 19.4 %collective-permute-start = (f32[51,8,128]{2,1,0:T(8,128)S(1)}, f32[51,8,128]{2,1,0:T(8,128)S(1)}, u32[]{:S(2)}, u32[]{:S(2)}) collective-permute-start(f32[51,8,128]{2,1,0:T(8,128)S(1)} %get-tuple-element.15), channel_id=1, source_target_pairs={{16,32},{48,64},{80,96},{112,128},{144,160},{176,192},{208,224},{2... | collective-permute-start | bytes 626696 | tf_op jit(solution)/shard_map/ppermute | solution.py:378
  3.7 18.7 %collective-permute-start.1 = (f32[51,8,128]{2,1,0:T(8,128)S(1)}, f32[51,8,128]{2,1,0:T(8,128)S(1)}, u32[]{:S(2)}, u32[]{:S(2)}) collective-permute-start(f32[51,8,128]{2,1,0:T(8,128)S(1)} %get-tuple-element.16), channel_id=1, source_target_pairs={{0,16},{32,48},{64,80},{96,112},{128,144},{160,176},{192,208},{224... | collective-permute-start | bytes 626696 | tf_op jit(solution)/shard_map/ppermute | solution.py:378
  13.7 15.1 %collective-permute-start.2 = (f32[7,8,8,128]{3,2,1,0:T(8,128)S(1)}, f32[7,8,8,128]{3,2,1,0:T(8,128)S(1)}, u32[]{:S(2)}, u32[]{:S(2)}) collective-permute-start(f32[7,8,8,128]{3,2,1,0:T(8,128)S(1)} %get-tuple-element.14.own), channel_id=1, source_target_pairs={{1,2},{3,4},{5,6},{7,8},{9,10},{11,12},{13,14},{2,1},{4,3},{6,5},{... | collective-permute-start | bytes 688136 | tf_op jit(solution)/shard_map/ppermute | solution.py:378
  17.9 10.9 %collective-permute-start.3 = (f32[7,8,8,128]{3,2,1,0:T(8,128)S(1)}, f32[7,8,8,128]{3,2,1,0:T(8,128)S(1)}, u32[]{:S(2)}, u32[]{:S(2)}) collective-permute-start(f32[7,8,8,128]{3,2,1,0:T(8,128)S(1)} %get-tuple-element.14.own), channel_id=1, source_target_pairs={{0,1},{2,3},{4,5},{6,7},{8,9},{10,11},{12,13},{14,15},{1,0},{3,2},... | collective-permute-start | bytes 688136 | tf_op jit(solution)/shard_map/ppermute | solution.py:378
  23.0 7.0 %collective-permute-start.4 = (f32[48,8,128]{2,1,0:T(8,128)S(1)}, f32[48,8,128]{2,1,0:T(8,128)S(1)}, u32[]{:S(2)}, u32[]{:S(2)}) collective-permute-start(f32[48,8,128]{2,1,0:T(8,128)S(1)} %get-tuple-element.18), channel_id=1, source_target_pairs={{1,2},{3,4},{5,6},{7,8},{9,10},{11,12},{13,14},{2,1},{4,3},{6,5},{... | collective-permute-start | bytes 589832 | tf_op jit(solution)/shard_map/ppermute | solution.py:378
  25.0 5.1 %collective-permute-start.5 = (f32[48,8,128]{2,1,0:T(8,128)S(1)}, f32[48,8,128]{2,1,0:T(8,128)S(1)}, u32[]{:S(2)}, u32[]{:S(2)}) collective-permute-start(f32[48,8,128]{2,1,0:T(8,128)S(1)} %get-tuple-element.19), channel_id=1, source_target_pairs={{0,1},{2,3},{4,5},{6,7},{8,9},{10,11},{12,13},{14,15},{1,0},{3,2},... | collective-permute-start | bytes 589832 | tf_op jit(solution)/shard_map/ppermute | solution.py:378

commit v7 on v6

--- a/solution.py
+++ b/solution.py
@@ -81,7 +81,7 @@
 
 
 def pack_kernel(
-    column, even, basis, diffusivity_in, speed_in, upwind_in, out, to_first, to_second, diffusivity, speed, upwind, sems
+    column, basis, diffusivity_in, speed_in, upwind_in, out, to_first, to_second, diffusivity, speed, upwind, sems
 ):
     copies = [
         pltpu.make_async_copy(src, dst, sems.at[n])
@@ -110,18 +110,18 @@
         for n, f in enumerate(NEAR_X):
             target[FAR_X + (B - 1) * n : FAR_X + (B - 1) * (n + 1)] = out[f, start : start + B - 1]
 
-    @pl.when(even[0] == 1)
+    @pl.when(lax.rem(lax.axis_index("gx"), 2) == 0)
     def _():
         emit(to_first, 1)
         emit(to_second, 0)
 
-    @pl.when(even[0] == 0)
+    @pl.when(lax.rem(lax.axis_index("gx"), 2) == 1)
     def _():
         emit(to_first, 0)
         emit(to_second, 1)
 
 
-def corner_kernel(even, second, first, strip, to_first, to_second):
+def corner_kernel(second, first, strip, to_first, to_second):
     def place(part, side, start):
         strip[0, B * side : B * (side + 1)] = part[0:B]
         strip[4, B * side : B * (side + 1)] = part[B:FAR_X]
@@ -129,21 +129,21 @@
             strip[f, B * side + start : B * (side + 1) - 1 + start] = part[FAR_X + (B - 1) * n : FAR_X + (B - 1) * (n + 1)]
             strip[f, 0 if side == 0 else 2 * B - 1] = jnp.zeros((B, LANES), F32)
 
-    @pl.when(even[0] == 1)
+    @pl.when(lax.rem(lax.axis_index("gx"), 2) == 0)
     def _():
         place(second, 0, 1)
         place(first, 1, 0)
 
-    @pl.when(even[0] == 0)
+    @pl.when(lax.rem(lax.axis_index("gx"), 2) == 1)
     def _():
         place(first, 0, 1)
         place(second, 1, 0)
 
-    @pl.when(even[1] == 1)
+    @pl.when(lax.rem(lax.axis_index("gz"), 2) == 0)
     def _():
         emit_corners(strip, to_first, to_second)
 
-    @pl.when(even[1] == 0)
+    @pl.when(lax.rem(lax.axis_index("gz"), 2) == 1)
     def _():
         emit_corners(strip, to_second, to_first)
 
@@ -207,13 +207,13 @@
 
 
 def basis_kernel(
-    even, own, strip, second, first, corner_second, corner_first, block, gram, coeff, field, high, low
+    own, strip, second, first, corner_second, corner_first, block, gram, coeff, field, high, low
 ):
-    @pl.when(even[1] == 1)
+    @pl.when(lax.rem(lax.axis_index("gz"), 2) == 0)
     def _():
         start_fields(own, strip, second, first, corner_second, corner_first, coeff, field)
 
-    @pl.when(even[1] == 0)
+    @pl.when(lax.rem(lax.axis_index("gz"), 2) == 1)
     def _():
         start_fields(own, strip, first, second, corner_first, corner_second, coeff, field)
 
@@ -384,13 +384,12 @@
 
 def body(previous_basis, restart_column, diffusivity, speed, upwind):
     count_x, count_y = lax.axis_size("gx"), lax.axis_size("gz")
-    even = jnp.stack([1 - lax.axis_index("gx") % 2, 1 - lax.axis_index("gz") % 2]).astype(jnp.int32)
     faces = (3, B, B, LANES)
     part = (TILES_X, B, LANES)
     own, to_first, to_second = pl.pallas_call(
         pack_kernel,
         out_shape=(pltpu.VMEM((FIELDS, B, B, LANES), F32), pltpu.VMEM(part, F32), pltpu.VMEM(part, F32)),
-        in_specs=[SMEM] * 2 + [HBM] * 4,
+        in_specs=[SMEM] + [HBM] * 4,
         out_specs=(VMEM,) * 3,
         scratch_shapes=[
             pltpu.VMEM(faces, F32),
@@ -400,7 +399,7 @@
         ],
         compiler_params=PARAMS,
         name="pack",
-    )(restart_column, even, *(in_hbm(array) for array in (previous_basis, diffusivity, speed, upwind)))
+    )(restart_column, *(in_hbm(array) for array in (previous_basis, diffusivity, speed, upwind)))
     second_x = paired(to_second, "gx", 1)
     first_x = paired(to_first, "gx", 0)
     corner = jax.ShapeDtypeStruct((TILES_CORNER, B, LANES), F32)
@@ -409,11 +408,11 @@
     strip, to_first, to_second = pl.pallas_call(
         corner_kernel,
         out_shape=(jax.ShapeDtypeStruct((FIELDS, 2 * B, B, LANES), F32), corner, corner),
-        in_specs=[SMEM] + [VMEM] * 2,
+        in_specs=[VMEM] * 2,
         out_specs=(VMEM,) * 3,
         compiler_params=PARAMS,
         name="corners",
-    )(even, second_x, first_x)
+    )(second_x, first_x)
     second_corner = paired(to_second, "gz", 1)
     first_corner = paired(to_first, "gz", 0)
     wide = (WIDE, WIDE, LANES)
@@ -423,7 +422,7 @@
             jax.ShapeDtypeStruct((COLS, B, B, LANES), F32),
             jax.ShapeDtypeStruct((2 * count_y, LANES), F32),
         ),
-        in_specs=[SMEM] + [VMEM] * 6,
+        in_specs=[VMEM] * 6,
         out_specs=(VMEM, VMEM),
         scratch_shapes=[
             pltpu.VMEM((FIELDS,) + wide, F32),
@@ -433,7 +432,7 @@
         ],
         compiler_params=PARAMS,
         name="basis",
-    )(even, own, strip, second_y, first_y, second_corner, first_corner)
+    )(own, strip, second_y, first_y, second_corner, first_corner)
     parts = lax.all_to_all(gram, "gz", 0, 0, tiled=True)
     line = pl.pallas_call(
         sum_kernel,

time: 77.9 us -> 76.2 us (0.978)
  Pallas kernels: 7.52 us -> 5.85 us
  transfers between devices with their start and end apart: 6 -> 6, of which waited for: 1 -> 1; matrix products, arithmetic and copies ran while one was open for 0% -> 0% of each run, Pallas kernels for 1% -> 0%
where the time goes in v7:
time: 76.2 us; the launch traced here: 75.8 us
  blocking collectives  42.3 us (56%)
  starting transfers between devices  25 us (33%)
  Pallas kernels  5.85 us (8%)
  between operations  1.38 us (2%)
  waiting for transfers between devices  1.26 us (2%)
    all_to_all x1, blocking collectives, body(): parts = lax.all_to_all(line, 'gx', 0, 0, tiled=True)  29.8 us
    ppermute x6, starting transfers between devices, paired(): lax.ppermute(array, axis, [(i, i + 1) for i in lower] + [(i + 1, i) for i...  25 us
    all_to_all x1, blocking collectives, body(): parts = lax.all_to_all(gram, 'gz', 0, 0, tiled=True)  12.5 us
    pallas_call x1, Pallas kernels, body(): pl.pallas_call(basis_kernel, out_shape=(jax.ShapeDtypeStruct((COLS, B, B,...  2.4 us
    pallas_call x1, Pallas kernels, body(): pl.pallas_call(lambda *refs: factor_kernel(scale, *refs), out_shape=(jax....  2.22 us
  transfers between devices with their start and end apart: 6, of which 1 were waited for; matrix products, arithmetic and copies ran while one was open for 0% of the time, Pallas kernels for 0%

profile of v7, /device:TPU:1, one launch (start us, length us, event | category | flops | bytes accessed | tf_op | source)
XLA Modules:
  0.0 75.8 jit_solution(1827702008072401235)
XLA Ops:
  1.3 1.1 %pack.1 = (f32[7,8,8,128]{3,2,1,0:T(8,128)S(1)}, f32[51,8,128]{2,1,0:T(8,128)S(1)}, f32[51,8,128]{2,1,0:T(8,128)S(1)}) custom-call(s32[1]{0:T(128)S(6)} %copy.8.column, f32[4,8,8,128]{3,2,1,0:T(8,128)} %basis.2, f32[3,8,8,128]{3,2,1,0:T(8,128)} %diffusivity_in.1, f32[3,8,8,128]{3,2,1,0:T(8,128)} %speed_in.1, s32[3,8,8,128]{3,2,1,0:T(8,128)} %upwind_in.1), custom_call_target="tpu_custom_call" | custom-call | tf_op jit(solution)/shard_map/pack/pallas_call | solution.py:389
  2.4 0.7 collective-permute-start
  3.1 10.0 %collective-permute-start.1 = (f32[51,8,128]{2,1,0:T(8,128)S(1)}, f32[51,8,128]{2,1,0:T(8,128)S(1)}, u32[]{:S(2)}, u32[]{:S(2)}) collective-permute-start(f32[51,8,128]{2,1,0:T(8,128)S(1)} %get-tuple-element.16), channel_id=1, source_target_pairs={{0,16},{32,48},{64,80},{96,112},{128,144},{160,176},{192,208},{224... | collective-permute-start | bytes 626696 | tf_op jit(solution)/shard_map/ppermute | solution.py:378
  13.0 4.2 %collective-permute-start.2 = (f32[7,8,8,128]{3,2,1,0:T(8,128)S(1)}, f32[7,8,8,128]{3,2,1,0:T(8,128)S(1)}, u32[]{:S(2)}, u32[]{:S(2)}) collective-permute-start(f32[7,8,8,128]{3,2,1,0:T(8,128)S(1)} %get-tuple-element.14.own), channel_id=1, source_target_pairs={{1,2},{3,4},{5,6},{7,8},{9,10},{11,12},{13,14},{2,1},{4,3},{6,5},{... | collective-permute-start | bytes 688136 | tf_op jit(solution)/shard_map/ppermute | solution.py:378
  17.3 4.4 %collective-permute-start.3 = (f32[7,8,8,128]{3,2,1,0:T(8,128)S(1)}, f32[7,8,8,128]{3,2,1,0:T(8,128)S(1)}, u32[]{:S(2)}, u32[]{:S(2)}) collective-permute-start(f32[7,8,8,128]{3,2,1,0:T(8,128)S(1)} %get-tuple-element.14.own), channel_id=1, source_target_pairs={{0,1},{2,3},{4,5},{6,7},{8,9},{10,11},{12,13},{14,15},{1,0},{3,2},... | collective-permute-start | bytes 688136 | tf_op jit(solution)/shard_map/ppermute | solution.py:378
  21.7 0.0 collective-permute-done.second
  21.8 0.0 collective-permute-done.1.first
  21.8 0.1 corners.1
  21.9 1.9 %collective-permute-start.4 = (f32[48,8,128]{2,1,0:T(8,128)S(1)}, f32[48,8,128]{2,1,0:T(8,128)S(1)}, u32[]{:S(2)}, u32[]{:S(2)}) collective-permute-start(f32[48,8,128]{2,1,0:T(8,128)S(1)} %get-tuple-element.18), channel_id=1, source_target_pairs={{1,2},{3,4},{5,6},{7,8},{9,10},{11,12},{13,14},{2,1},{4,3},{6,5},{... | collective-permute-start | bytes 589832 | tf_op jit(solution)/shard_map/ppermute | solution.py:378
  23.8 3.8 %collective-permute-start.5 = (f32[48,8,128]{2,1,0:T(8,128)S(1)}, f32[48,8,128]{2,1,0:T(8,128)S(1)}, u32[]{:S(2)}, u32[]{:S(2)}) collective-permute-start(f32[48,8,128]{2,1,0:T(8,128)S(1)} %get-tuple-element.19), channel_id=1, source_target_pairs={{0,1},{2,3},{4,5},{6,7},{8,9},{10,11},{12,13},{14,15},{1,0},{3,2},... | collective-permute-start | bytes 589832 | tf_op jit(solution)/shard_map/ppermute | solution.py:378
  27.6 0.0 collective-permute-done.2.second
  27.6 0.0 collective-permute-done.3.first
  27.6 1.2 %collective-permute-done.4.corner_second = f32[48,8,128]{2,1,0:T(8,128)S(1)} collective-permute-done((f32[48,8,128]{2,1,0:T(8,128)S(1)}, f32[48,8,128]{2,1,0:T(8,128)S(1)}, u32[]{:S(2)}, u32[]{:S(2)}) %collective-permute-start.4) | collective-permute-done | bytes 196640 | tf_op jit(solution)/shard_map/ppermute | solution.py:378
  28.8 0.0 collective-permute-done.5.corner_first
  28.9 2.4 %basis.3 = (f32[9,8,8,128]{3,2,1,0:T(8,128)S(1)}, f32[32,128]{1,0:T(8,128)S(1)}) custom-call(f32[7,8,8,128]{3,2,1,0:T(8,128)S(1)} %get-tuple-element.14.own, f32[7,16,8,128]{3,2,1,0:T(8,128)S(1)} %get-tuple-element.17.strip, f32[7,8,8,128]{3,2,1,0:T(8,128)S(1)} %collective-permute-done.2.second, f32[7,8,8,128]{3,2,1,0:T(8,128)S(1)} %collective-permute-done.3.first, ...), custom_call_target="tpu_custom_call" | custom-call | tf_op jit(solution)/shard_map/basis/pallas_call | solution.py:419
  31.3 12.5 %all_to_all.22 = f32[16,2,128]{2,1,0:T(2,128)S(1)} all-to-all(f32[16,2,128]{2,1,0:T(2,128)S(1)} %bitcast.8), channel_id=1, replica_groups=mesh['gx'=64,'gz'=16] {'gz'}, dimensions={0} | all-to-all | bytes 32768 | tf_op jit(solution)/shard_map/all_to_all | solution.py:436
  43.8 29.8 %all_to_all.23 = f32[64,2,128]{2,1,0:T(2,128)S(1)} all-to-all(f32[64,2,128]{2,1,0:T(2,128)S(1)} %bitcast.5), channel_id=1, replica_groups=mesh['gx'=64,'gz'=16] {'gx'}, dimensions={0} | all-to-all | bytes 131072 | tf_op jit(solution)/shard_map/all_to_all | solution.py:445
  73.6 2.2 %factor.1 = (f32[9,8,8,128]{3,2,1,0:T(8,128)}, f32[9,9]{1,0:T(8,128)}, f32[8,9]{1,0:T(8,128)}) custom-call(f32[128,128]{1,0:T(8,128)S(1)} %bitcast.6, f32[9,8,8,128]{3,2,1,0:T(8,128)S(1)} %get-tuple-element.21.refs_1_), custom_call_target="tpu_custom_call" | custom-call | tf_op jit(solution)/shard_map/factor/pallas_call | solution.py:447
  (1 shorter events, 0.0 us)
Async XLA Ops:
  2.4 19.4 %collective-permute-start = (f32[51,8,128]{2,1,0:T(8,128)S(1)}, f32[51,8,128]{2,1,0:T(8,128)S(1)}, u32[]{:S(2)}, u32[]{:S(2)}) collective-permute-start(f32[51,8,128]{2,1,0:T(8,128)S(1)} %get-tuple-element.15), channel_id=1, source_target_pairs={{16,32},{48,64},{80,96},{112,128},{144,160},{176,192},{208,224},{2... | collective-permute-start | bytes 626696 | tf_op jit(solution)/shard_map/ppermute | solution.py:378
  3.1 18.7 %collective-permute-start.1 = (f32[51,8,128]{2,1,0:T(8,128)S(1)}, f32[51,8,128]{2,1,0:T(8,128)S(1)}, u32[]{:S(2)}, u32[]{:S(2)}) collective-permute-start(f32[51,8,128]{2,1,0:T(8,128)S(1)} %get-tuple-element.16), channel_id=1, source_target_pairs={{0,16},{32,48},{64,80},{96,112},{128,144},{160,176},{192,208},{224... | collective-permute-start | bytes 626696 | tf_op jit(solution)/shard_map/ppermute | solution.py:378
  13.0 14.5 %collective-permute-start.2 = (f32[7,8,8,128]{3,2,1,0:T(8,128)S(1)}, f32[7,8,8,128]{3,2,1,0:T(8,128)S(1)}, u32[]{:S(2)}, u32[]{:S(2)}) collective-permute-start(f32[7,8,8,128]{3,2,1,0:T(8,128)S(1)} %get-tuple-element.14.own), channel_id=1, source_target_pairs={{1,2},{3,4},{5,6},{7,8},{9,10},{11,12},{13,14},{2,1},{4,3},{6,5},{... | collective-permute-start | bytes 688136 | tf_op jit(solution)/shard_map/ppermute | solution.py:378
  17.3 10.3 %collective-permute-start.3 = (f32[7,8,8,128]{3,2,1,0:T(8,128)S(1)}, f32[7,8,8,128]{3,2,1,0:T(8,128)S(1)}, u32[]{:S(2)}, u32[]{:S(2)}) collective-permute-start(f32[7,8,8,128]{3,2,1,0:T(8,128)S(1)} %get-tuple-element.14.own), channel_id=1, source_target_pairs={{0,1},{2,3},{4,5},{6,7},{8,9},{10,11},{12,13},{14,15},{1,0},{3,2},... | collective-permute-start | bytes 688136 | tf_op jit(solution)/shard_map/ppermute | solution.py:378
  21.9 7.0 %collective-permute-start.4 = (f32[48,8,128]{2,1,0:T(8,128)S(1)}, f32[48,8,128]{2,1,0:T(8,128)S(1)}, u32[]{:S(2)}, u32[]{:S(2)}) collective-permute-start(f32[48,8,128]{2,1,0:T(8,128)S(1)} %get-tuple-element.18), channel_id=1, source_target_pairs={{1,2},{3,4},{5,6},{7,8},{9,10},{11,12},{13,14},{2,1},{4,3},{6,5},{... | collective-permute-start | bytes 589832 | tf_op jit(solution)/shard_map/ppermute | solution.py:378
  23.8 5.1 %collective-permute-start.5 = (f32[48,8,128]{2,1,0:T(8,128)S(1)}, f32[48,8,128]{2,1,0:T(8,128)S(1)}, u32[]{:S(2)}, u32[]{:S(2)}) collective-permute-start(f32[48,8,128]{2,1,0:T(8,128)S(1)} %get-tuple-element.19), channel_id=1, source_target_pairs={{0,1},{2,3},{4,5},{6,7},{8,9},{10,11},{12,13},{14,15},{1,0},{3,2},... | collective-permute-start | bytes 589832 | tf_op jit(solution)/shard_map/ppermute | solution.py:378

commit v8 on v7

--- a/solution.py
+++ b/solution.py
@@ -110,12 +110,12 @@
         for n, f in enumerate(NEAR_X):
             target[FAR_X + (B - 1) * n : FAR_X + (B - 1) * (n + 1)] = out[f, start : start + B - 1]
 
-    @pl.when(lax.rem(lax.axis_index("gx"), 2) == 0)
+    @pl.when(lax.rem(lax.axis_index("gx") + lax.axis_index("gz"), 2) == 0)
     def _():
         emit(to_first, 1)
         emit(to_second, 0)
 
-    @pl.when(lax.rem(lax.axis_index("gx"), 2) == 1)
+    @pl.when(lax.rem(lax.axis_index("gx") + lax.axis_index("gz"), 2) == 1)
     def _():
         emit(to_first, 0)
         emit(to_second, 1)
@@ -129,12 +129,12 @@
             strip[f, B * side + start : B * (side + 1) - 1 + start] = part[FAR_X + (B - 1) * n : FAR_X + (B - 1) * (n + 1)]
             strip[f, 0 if side == 0 else 2 * B - 1] = jnp.zeros((B, LANES), F32)
 
-    @pl.when(lax.rem(lax.axis_index("gx"), 2) == 0)
+    @pl.when(lax.rem(lax.axis_index("gx") + lax.axis_index("gz"), 2) == 0)
     def _():
         place(second, 0, 1)
         place(first, 1, 0)
 
-    @pl.when(lax.rem(lax.axis_index("gx"), 2) == 1)
+    @pl.when(lax.rem(lax.axis_index("gx") + lax.axis_index("gz"), 2) == 1)
     def _():
         place(first, 0, 1)
         place(second, 1, 0)
@@ -372,10 +372,20 @@
         basis_q[j] = total
 
 
-def paired(array, axis, first):
-    count = lax.axis_size(axis)
-    lower = range(first, count - 1, 2)
-    return lax.ppermute(array, axis, [(i, i + 1) for i in lower] + [(i + 1, i) for i in lower])
+def paired_x(array, first):
+    count_x, count_y = lax.axis_size("gx"), lax.axis_size("gz")
+    route = []
+    for x in range(count_x - 1):
+        for y in range(count_y):
+            if (x + y + first) % 2 == 0:
+                here, there = x * count_y + y, (x + 1) * count_y + y
+                route += [(here, there), (there, here)]
+    return lax.ppermute(array, ("gx", "gz"), route)
+
+
+def paired_y(array, first):
+    lower = range(first, lax.axis_size("gz") - 1, 2)
+    return lax.ppermute(array, "gz", [(i, i + 1) for i in lower] + [(i + 1, i) for i in lower])
 
 
 def in_hbm(array):
@@ -400,11 +410,11 @@
         compiler_params=PARAMS,
         name="pack",
     )(restart_column, *(in_hbm(array) for array in (previous_basis, diffusivity, speed, upwind)))
-    second_x = paired(to_second, "gx", 1)
-    first_x = paired(to_first, "gx", 0)
+    second_x = paired_x(to_second, 1)
+    first_x = paired_x(to_first, 0)
     corner = jax.ShapeDtypeStruct((TILES_CORNER, B, LANES), F32)
-    second_y = paired(own, "gz", 1)
-    first_y = paired(own, "gz", 0)
+    second_y = paired_y(own, 1)
+    first_y = paired_y(own, 0)
     strip, to_first, to_second = pl.pallas_call(
         corner_kernel,
         out_shape=(jax.ShapeDtypeStruct((FIELDS, 2 * B, B, LANES), F32), corner, corner),
@@ -413,8 +423,8 @@
         compiler_params=PARAMS,
         name="corners",
     )(second_x, first_x)
-    second_corner = paired(to_second, "gz", 1)
-    first_corner = paired(to_first, "gz", 0)
+    second_corner = paired_y(to_second, 1)
+    first_corner = paired_y(to_first, 0)
     wide = (WIDE, WIDE, LANES)
     block, gram = pl.pallas_call(
         basis_kernel,

time: 76.2 us -> 76.5 us (level)
  no operation moved by 1% of the time
where the time goes in v8:
time: 76.5 us; the launch traced here: 76.1 us
  blocking collectives  42.6 us (56%)
  starting transfers between devices  25 us (33%)
  Pallas kernels  5.85 us (8%)
  between operations  1.38 us (2%)
  waiting for transfers between devices  1.26 us (2%)
    all_to_all x1, blocking collectives, body(): parts = lax.all_to_all(line, 'gx', 0, 0, tiled=True)  30.4 us
    ppermute x4, starting transfers between devices, paired_y(): lax.ppermute(array, 'gz', [(i, i + 1) for i in lower] + [(i + 1, i) for i...  18.6 us
    all_to_all x1, blocking collectives, body(): parts = lax.all_to_all(gram, 'gz', 0, 0, tiled=True)  12.2 us
    ppermute x2, starting transfers between devices, paired_x(): return lax.ppermute(array, ('gx', 'gz'), route)  6.41 us
    pallas_call x1, Pallas kernels, body(): pl.pallas_call(basis_kernel, out_shape=(jax.ShapeDtypeStruct((COLS, B, B,...  2.4 us
    pallas_call x1, Pallas kernels, body(): pl.pallas_call(lambda *refs: factor_kernel(scale, *refs), out_shape=(jax....  2.22 us
  transfers between devices with their start and end apart: 6, of which 1 were waited for; matrix products, arithmetic and copies ran while one was open for 0% of the time, Pallas kernels for 0%

profile of v8, /device:TPU:1, one launch (start us, length us, event | category | flops | bytes accessed | tf_op | source)
XLA Modules:
  0.0 76.1 jit_solution(3515640638989437355)
XLA Ops:
  1.3 1.1 %pack.1 = (f32[7,8,8,128]{3,2,1,0:T(8,128)S(1)}, f32[51,8,128]{2,1,0:T(8,128)S(1)}, f32[51,8,128]{2,1,0:T(8,128)S(1)}) custom-call(s32[1]{0:T(128)S(6)} %copy.8.column, f32[4,8,8,128]{3,2,1,0:T(8,128)} %basis.2, f32[3,8,8,128]{3,2,1,0:T(8,128)} %diffusivity_in.1, f32[3,8,8,128]{3,2,1,0:T(8,128)} %speed_in.1, s32[3,8,8,128]{3,2,1,0:T(8,128)} %upwind_in.1), custom_call_target="tpu_custom_call" | custom-call | tf_op jit(solution)/shard_map/pack/pallas_call | solution.py:399
  2.4 5.7 %collective-permute-start = (f32[51,8,128]{2,1,0:T(8,128)S(1)}, f32[51,8,128]{2,1,0:T(8,128)S(1)}, u32[]{:S(2)}, u32[]{:S(2)}) collective-permute-start(f32[51,8,128]{2,1,0:T(8,128)S(1)} %get-tuple-element.15), channel_id=1, source_target_pairs={{1,17},{17,1},{3,19},{19,3},{5,21},{21,5},{7,23},{23,7},{9,25},{25... | collective-permute-start | bytes 626696 | tf_op jit(solution)/shard_map/ppermute | solution.py:383
  8.1 0.7 collective-permute-start.1
  8.8 8.5 %collective-permute-start.2 = (f32[7,8,8,128]{3,2,1,0:T(8,128)S(1)}, f32[7,8,8,128]{3,2,1,0:T(8,128)S(1)}, u32[]{:S(2)}, u32[]{:S(2)}) collective-permute-start(f32[7,8,8,128]{3,2,1,0:T(8,128)S(1)} %get-tuple-element.14.own), channel_id=1, source_target_pairs={{1,2},{3,4},{5,6},{7,8},{9,10},{11,12},{13,14},{2,1},{4,3},{6,5},{... | collective-permute-start | bytes 688136 | tf_op jit(solution)/shard_map/ppermute | solution.py:388
  17.3 4.4 %collective-permute-start.3 = (f32[7,8,8,128]{3,2,1,0:T(8,128)S(1)}, f32[7,8,8,128]{3,2,1,0:T(8,128)S(1)}, u32[]{:S(2)}, u32[]{:S(2)}) collective-permute-start(f32[7,8,8,128]{3,2,1,0:T(8,128)S(1)} %get-tuple-element.14.own), channel_id=1, source_target_pairs={{0,1},{2,3},{4,5},{6,7},{8,9},{10,11},{12,13},{14,15},{1,0},{3,2},... | collective-permute-start | bytes 688136 | tf_op jit(solution)/shard_map/ppermute | solution.py:388
  21.7 0.0 collective-permute-done.second
  21.8 0.0 collective-permute-done.1.first
  21.8 0.1 corners.1
  21.9 1.9 %collective-permute-start.4 = (f32[48,8,128]{2,1,0:T(8,128)S(1)}, f32[48,8,128]{2,1,0:T(8,128)S(1)}, u32[]{:S(2)}, u32[]{:S(2)}) collective-permute-start(f32[48,8,128]{2,1,0:T(8,128)S(1)} %get-tuple-element.18), channel_id=1, source_target_pairs={{1,2},{3,4},{5,6},{7,8},{9,10},{11,12},{13,14},{2,1},{4,3},{6,5},{... | collective-permute-start | bytes 589832 | tf_op jit(solution)/shard_map/ppermute | solution.py:388
  23.8 3.8 %collective-permute-start.5 = (f32[48,8,128]{2,1,0:T(8,128)S(1)}, f32[48,8,128]{2,1,0:T(8,128)S(1)}, u32[]{:S(2)}, u32[]{:S(2)}) collective-permute-start(f32[48,8,128]{2,1,0:T(8,128)S(1)} %get-tuple-element.19), channel_id=1, source_target_pairs={{0,1},{2,3},{4,5},{6,7},{8,9},{10,11},{12,13},{14,15},{1,0},{3,2},... | collective-permute-start | bytes 589832 | tf_op jit(solution)/shard_map/ppermute | solution.py:388
  27.6 0.0 collective-permute-done.2.second
  27.6 0.0 collective-permute-done.3.first
  27.6 1.2 %collective-permute-done.4.corner_second = f32[48,8,128]{2,1,0:T(8,128)S(1)} collective-permute-done((f32[48,8,128]{2,1,0:T(8,128)S(1)}, f32[48,8,128]{2,1,0:T(8,128)S(1)}, u32[]{:S(2)}, u32[]{:S(2)}) %collective-permute-start.4) | collective-permute-done | bytes 196640 | tf_op jit(solution)/shard_map/ppermute | solution.py:388
  28.8 0.0 collective-permute-done.5.corner_first
  28.9 2.4 %basis.3 = (f32[9,8,8,128]{3,2,1,0:T(8,128)S(1)}, f32[32,128]{1,0:T(8,128)S(1)}) custom-call(f32[7,8,8,128]{3,2,1,0:T(8,128)S(1)} %get-tuple-element.14.own, f32[7,16,8,128]{3,2,1,0:T(8,128)S(1)} %get-tuple-element.17.strip, f32[7,8,8,128]{3,2,1,0:T(8,128)S(1)} %collective-permute-done.2.second, f32[7,8,8,128]{3,2,1,0:T(8,128)S(1)} %collective-permute-done.3.first, ...), custom_call_target="tpu_custom_call" | custom-call | tf_op jit(solution)/shard_map/basis/pallas_call | solution.py:429
  31.3 12.2 %all_to_all.22 = f32[16,2,128]{2,1,0:T(2,128)S(1)} all-to-all(f32[16,2,128]{2,1,0:T(2,128)S(1)} %bitcast.8), channel_id=1, replica_groups=mesh['gx'=64,'gz'=16] {'gz'}, dimensions={0} | all-to-all | bytes 32768 | tf_op jit(solution)/shard_map/all_to_all | solution.py:446
  43.5 30.4 %all_to_all.23 = f32[64,2,128]{2,1,0:T(2,128)S(1)} all-to-all(f32[64,2,128]{2,1,0:T(2,128)S(1)} %bitcast.5), channel_id=1, replica_groups=mesh['gx'=64,'gz'=16] {'gx'}, dimensions={0} | all-to-all | bytes 131072 | tf_op jit(solution)/shard_map/all_to_all | solution.py:455
  73.9 2.2 %factor.1 = (f32[9,8,8,128]{3,2,1,0:T(8,128)}, f32[9,9]{1,0:T(8,128)}, f32[8,9]{1,0:T(8,128)}) custom-call(f32[128,128]{1,0:T(8,128)S(1)} %bitcast.6, f32[9,8,8,128]{3,2,1,0:T(8,128)S(1)} %get-tuple-element.21.refs_1_), custom_call_target="tpu_custom_call" | custom-call | tf_op jit(solution)/shard_map/factor/pallas_call | solution.py:457
  (1 shorter events, 0.0 us)
Async XLA Ops:
  2.4 19.4 %collective-permute-start = (f32[51,8,128]{2,1,0:T(8,128)S(1)}, f32[51,8,128]{2,1,0:T(8,128)S(1)}, u32[]{:S(2)}, u32[]{:S(2)}) collective-permute-start(f32[51,8,128]{2,1,0:T(8,128)S(1)} %get-tuple-element.15), channel_id=1, source_target_pairs={{1,17},{17,1},{3,19},{19,3},{5,21},{21,5},{7,23},{23,7},{9,25},{25... | collective-permute-start | bytes 626696 | tf_op jit(solution)/shard_map/ppermute | solution.py:383
  8.1 13.6 %collective-permute-start.1 = (f32[51,8,128]{2,1,0:T(8,128)S(1)}, f32[51,8,128]{2,1,0:T(8,128)S(1)}, u32[]{:S(2)}, u32[]{:S(2)}) collective-permute-start(f32[51,8,128]{2,1,0:T(8,128)S(1)} %get-tuple-element.16), channel_id=1, source_target_pairs={{0,16},{16,0},{2,18},{18,2},{4,20},{20,4},{6,22},{22,6},{8,24},{24... | collective-permute-start | bytes 626696 | tf_op jit(solution)/shard_map/ppermute | solution.py:383
  8.8 18.8 %collective-permute-start.2 = (f32[7,8,8,128]{3,2,1,0:T(8,128)S(1)}, f32[7,8,8,128]{3,2,1,0:T(8,128)S(1)}, u32[]{:S(2)}, u32[]{:S(2)}) collective-permute-start(f32[7,8,8,128]{3,2,1,0:T(8,128)S(1)} %get-tuple-element.14.own), channel_id=1, source_target_pairs={{1,2},{3,4},{5,6},{7,8},{9,10},{11,12},{13,14},{2,1},{4,3},{6,5},{... | collective-permute-start | bytes 688136 | tf_op jit(solution)/shard_map/ppermute | solution.py:388
  17.3 10.3 %collective-permute-start.3 = (f32[7,8,8,128]{3,2,1,0:T(8,128)S(1)}, f32[7,8,8,128]{3,2,1,0:T(8,128)S(1)}, u32[]{:S(2)}, u32[]{:S(2)}) collective-permute-start(f32[7,8,8,128]{3,2,1,0:T(8,128)S(1)} %get-tuple-element.14.own), channel_id=1, source_target_pairs={{0,1},{2,3},{4,5},{6,7},{8,9},{10,11},{12,13},{14,15},{1,0},{3,2},... | collective-permute-start | bytes 688136 | tf_op jit(solution)/shard_map/ppermute | solution.py:388
  21.9 7.0 %collective-permute-start.4 = (f32[48,8,128]{2,1,0:T(8,128)S(1)}, f32[48,8,128]{2,1,0:T(8,128)S(1)}, u32[]{:S(2)}, u32[]{:S(2)}) collective-permute-start(f32[48,8,128]{2,1,0:T(8,128)S(1)} %get-tuple-element.18), channel_id=1, source_target_pairs={{1,2},{3,4},{5,6},{7,8},{9,10},{11,12},{13,14},{2,1},{4,3},{6,5},{... | collective-permute-start | bytes 589832 | tf_op jit(solution)/shard_map/ppermute | solution.py:388
  23.8 5.1 %collective-permute-start.5 = (f32[48,8,128]{2,1,0:T(8,128)S(1)}, f32[48,8,128]{2,1,0:T(8,128)S(1)}, u32[]{:S(2)}, u32[]{:S(2)}) collective-permute-start(f32[48,8,128]{2,1,0:T(8,128)S(1)} %get-tuple-element.19), channel_id=1, source_target_pairs={{0,1},{2,3},{4,5},{6,7},{8,9},{10,11},{12,13},{14,15},{1,0},{3,2},... | collective-permute-start | bytes 589832 | tf_op jit(solution)/shard_map/ppermute | solution.py:388

commit v9 on v7

--- a/solution.py
+++ b/solution.py
@@ -420,7 +420,7 @@
         basis_kernel,
         out_shape=(
             jax.ShapeDtypeStruct((COLS, B, B, LANES), F32),
-            jax.ShapeDtypeStruct((2 * count_y, LANES), F32),
+            jax.ShapeDtypeStruct((2 * count_x, LANES), F32),
         ),
         in_specs=[VMEM] * 6,
         out_specs=(VMEM, VMEM),
@@ -433,16 +433,16 @@
         compiler_params=PARAMS,
         name="basis",
     )(own, strip, second_y, first_y, second_corner, first_corner)
-    parts = lax.all_to_all(gram, "gz", 0, 0, tiled=True)
+    parts = lax.all_to_all(gram, "gx", 0, 0, tiled=True)
     line = pl.pallas_call(
         sum_kernel,
-        out_shape=jax.ShapeDtypeStruct((2 * count_x, LANES), F32),
+        out_shape=jax.ShapeDtypeStruct((2 * count_y, LANES), F32),
         in_specs=[VMEM],
         out_specs=VMEM,
         compiler_params=PARAMS,
         name="line_sum",
     )(parts)
-    parts = lax.all_to_all(line, "gx", 0, 0, tiled=True)
+    parts = lax.all_to_all(line, "gz", 0, 0, tiled=True)
     scale = math.sqrt(B * B * LANES * count_x * count_y)
     basis_q, factor_r, hessenberg = pl.pallas_call(
         lambda *refs: factor_kernel(scale, *refs),

time: 76.2 us -> 77.6 us (1.018)
  blocking collectives: 42.3 us -> 43.7 us
    all_to_all x2, blocking collectives: 42.3 us -> 43.7 us  [the longest x1 27 us: body(): parts = lax.all_to_all(gram, 'gx', 0, 0, tiled=True)]
where the time goes in v9:
time: 77.6 us; the launch traced here: 77.2 us
  blocking collectives  43.7 us (56%)
  starting transfers between devices  25 us (32%)
  Pallas kernels  5.85 us (8%)
  between operations  1.38 us (2%)
  waiting for transfers between devices  1.26 us (2%)
    all_to_all x1, blocking collectives, body(): parts = lax.all_to_all(gram, 'gx', 0, 0, tiled=True)  27 us
    ppermute x6, starting transfers between devices, paired(): lax.ppermute(array, axis, [(i, i + 1) for i in lower] + [(i + 1, i) for i...  25 us
    all_to_all x1, blocking collectives, body(): parts = lax.all_to_all(line, 'gz', 0, 0, tiled=True)  16.7 us
    pallas_call x1, Pallas kernels, body(): pl.pallas_call(basis_kernel, out_shape=(jax.ShapeDtypeStruct((COLS, B, B,...  2.41 us
    pallas_call x1, Pallas kernels, body(): pl.pallas_call(lambda *refs: factor_kernel(scale, *refs), out_shape=(jax....  2.2 us
  transfers between devices with their start and end apart: 6, of which 1 were waited for; matrix products, arithmetic and copies ran while one was open for 0% of the time, Pallas kernels for 0%

profile of v9, /device:TPU:1, one launch (start us, length us, event | category | flops | bytes accessed | tf_op | source)
XLA Modules:
  0.0 77.2 jit_solution(7565357966887057810)
XLA Ops:
  1.3 1.1 %pack.1 = (f32[7,8,8,128]{3,2,1,0:T(8,128)S(1)}, f32[51,8,128]{2,1,0:T(8,128)S(1)}, f32[51,8,128]{2,1,0:T(8,128)S(1)}) custom-call(s32[1]{0:T(128)S(6)} %copy.8.column, f32[4,8,8,128]{3,2,1,0:T(8,128)} %basis.2, f32[3,8,8,128]{3,2,1,0:T(8,128)} %diffusivity_in.1, f32[3,8,8,128]{3,2,1,0:T(8,128)} %speed_in.1, s32[3,8,8,128]{3,2,1,0:T(8,128)} %upwind_in.1), custom_call_target="tpu_custom_call" | custom-call | tf_op jit(solution)/shard_map/pack/pallas_call | solution.py:389
  2.4 0.7 collective-permute-start
  3.1 10.0 %collective-permute-start.1 = (f32[51,8,128]{2,1,0:T(8,128)S(1)}, f32[51,8,128]{2,1,0:T(8,128)S(1)}, u32[]{:S(2)}, u32[]{:S(2)}) collective-permute-start(f32[51,8,128]{2,1,0:T(8,128)S(1)} %get-tuple-element.16), channel_id=1, source_target_pairs={{0,16},{32,48},{64,80},{96,112},{128,144},{160,176},{192,208},{224... | collective-permute-start | bytes 626696 | tf_op jit(solution)/shard_map/ppermute | solution.py:378
  13.0 4.2 %collective-permute-start.2 = (f32[7,8,8,128]{3,2,1,0:T(8,128)S(1)}, f32[7,8,8,128]{3,2,1,0:T(8,128)S(1)}, u32[]{:S(2)}, u32[]{:S(2)}) collective-permute-start(f32[7,8,8,128]{3,2,1,0:T(8,128)S(1)} %get-tuple-element.14.own), channel_id=1, source_target_pairs={{1,2},{3,4},{5,6},{7,8},{9,10},{11,12},{13,14},{2,1},{4,3},{6,5},{... | collective-permute-start | bytes 688136 | tf_op jit(solution)/shard_map/ppermute | solution.py:378
  17.3 4.4 %collective-permute-start.3 = (f32[7,8,8,128]{3,2,1,0:T(8,128)S(1)}, f32[7,8,8,128]{3,2,1,0:T(8,128)S(1)}, u32[]{:S(2)}, u32[]{:S(2)}) collective-permute-start(f32[7,8,8,128]{3,2,1,0:T(8,128)S(1)} %get-tuple-element.14.own), channel_id=1, source_target_pairs={{0,1},{2,3},{4,5},{6,7},{8,9},{10,11},{12,13},{14,15},{1,0},{3,2},... | collective-permute-start | bytes 688136 | tf_op jit(solution)/shard_map/ppermute | solution.py:378
  21.7 0.0 collective-permute-done.second
  21.8 0.0 collective-permute-done.1.first
  21.8 0.1 corners.1
  21.9 1.9 %collective-permute-start.4 = (f32[48,8,128]{2,1,0:T(8,128)S(1)}, f32[48,8,128]{2,1,0:T(8,128)S(1)}, u32[]{:S(2)}, u32[]{:S(2)}) collective-permute-start(f32[48,8,128]{2,1,0:T(8,128)S(1)} %get-tuple-element.18), channel_id=1, source_target_pairs={{1,2},{3,4},{5,6},{7,8},{9,10},{11,12},{13,14},{2,1},{4,3},{6,5},{... | collective-permute-start | bytes 589832 | tf_op jit(solution)/shard_map/ppermute | solution.py:378
  23.8 3.8 %collective-permute-start.5 = (f32[48,8,128]{2,1,0:T(8,128)S(1)}, f32[48,8,128]{2,1,0:T(8,128)S(1)}, u32[]{:S(2)}, u32[]{:S(2)}) collective-permute-start(f32[48,8,128]{2,1,0:T(8,128)S(1)} %get-tuple-element.19), channel_id=1, source_target_pairs={{0,1},{2,3},{4,5},{6,7},{8,9},{10,11},{12,13},{14,15},{1,0},{3,2},... | collective-permute-start | bytes 589832 | tf_op jit(solution)/shard_map/ppermute | solution.py:378
  27.6 0.0 collective-permute-done.2.second
  27.6 0.0 collective-permute-done.3.first
  27.6 1.2 %collective-permute-done.4.corner_second = f32[48,8,128]{2,1,0:T(8,128)S(1)} collective-permute-done((f32[48,8,128]{2,1,0:T(8,128)S(1)}, f32[48,8,128]{2,1,0:T(8,128)S(1)}, u32[]{:S(2)}, u32[]{:S(2)}) %collective-permute-start.4) | collective-permute-done | bytes 196640 | tf_op jit(solution)/shard_map/ppermute | solution.py:378
  28.8 0.0 collective-permute-done.5.corner_first
  28.9 2.4 %basis.3 = (f32[9,8,8,128]{3,2,1,0:T(8,128)S(1)}, f32[128,128]{1,0:T(8,128)S(1)}) custom-call(f32[7,8,8,128]{3,2,1,0:T(8,128)S(1)} %get-tuple-element.14.own, f32[7,16,8,128]{3,2,1,0:T(8,128)S(1)} %get-tuple-element.17.strip, f32[7,8,8,128]{3,2,1,0:T(8,128)S(1)} %collective-permute-done.2.second, f32[7,8,8,128]{3,2,1,0:T(8,128)S(1)} %collective-permute-done.3.first, ...), custom_call_target="tpu_custom_call" | custom-call | tf_op jit(solution)/shard_map/basis/pallas_call | solution.py:419
  31.3 27.0 %all_to_all.22 = f32[64,2,128]{2,1,0:T(2,128)S(1)} all-to-all(f32[64,2,128]{2,1,0:T(2,128)S(1)} %bitcast.8), channel_id=1, replica_groups=mesh['gx'=64,'gz'=16] {'gx'}, dimensions={0} | all-to-all | bytes 131072 | tf_op jit(solution)/shard_map/all_to_all | solution.py:436
  58.3 0.1 line_sum.1
  58.3 16.7 %all_to_all.23 = f32[16,2,128]{2,1,0:T(2,128)S(1)} all-to-all(f32[16,2,128]{2,1,0:T(2,128)S(1)} %bitcast.7), channel_id=1, replica_groups=mesh['gx'=64,'gz'=16] {'gz'}, dimensions={0} | all-to-all | bytes 32768 | tf_op jit(solution)/shard_map/all_to_all | solution.py:445
  75.0 2.2 %factor.1 = (f32[9,8,8,128]{3,2,1,0:T(8,128)}, f32[9,9]{1,0:T(8,128)}, f32[8,9]{1,0:T(8,128)}) custom-call(f32[32,128]{1,0:T(8,128)S(1)} %bitcast.6, f32[9,8,8,128]{3,2,1,0:T(8,128)S(1)} %get-tuple-element.21.refs_1_), custom_call_target="tpu_custom_call" | custom-call | tf_op jit(solution)/shard_map/factor/pallas_call | solution.py:447
Async XLA Ops:
  2.4 19.4 %collective-permute-start = (f32[51,8,128]{2,1,0:T(8,128)S(1)}, f32[51,8,128]{2,1,0:T(8,128)S(1)}, u32[]{:S(2)}, u32[]{:S(2)}) collective-permute-start(f32[51,8,128]{2,1,0:T(8,128)S(1)} %get-tuple-element.15), channel_id=1, source_target_pairs={{16,32},{48,64},{80,96},{112,128},{144,160},{176,192},{208,224},{2... | collective-permute-start | bytes 626696 | tf_op jit(solution)/shard_map/ppermute | solution.py:378
  3.1 18.7 %collective-permute-start.1 = (f32[51,8,128]{2,1,0:T(8,128)S(1)}, f32[51,8,128]{2,1,0:T(8,128)S(1)}, u32[]{:S(2)}, u32[]{:S(2)}) collective-permute-start(f32[51,8,128]{2,1,0:T(8,128)S(1)} %get-tuple-element.16), channel_id=1, source_target_pairs={{0,16},{32,48},{64,80},{96,112},{128,144},{160,176},{192,208},{224... | collective-permute-start | bytes 626696 | tf_op jit(solution)/shard_map/ppermute | solution.py:378
  13.0 14.5 %collective-permute-start.2 = (f32[7,8,8,128]{3,2,1,0:T(8,128)S(1)}, f32[7,8,8,128]{3,2,1,0:T(8,128)S(1)}, u32[]{:S(2)}, u32[]{:S(2)}) collective-permute-start(f32[7,8,8,128]{3,2,1,0:T(8,128)S(1)} %get-tuple-element.14.own), channel_id=1, source_target_pairs={{1,2},{3,4},{5,6},{7,8},{9,10},{11,12},{13,14},{2,1},{4,3},{6,5},{... | collective-permute-start | bytes 688136 | tf_op jit(solution)/shard_map/ppermute | solution.py:378
  17.3 10.3 %collective-permute-start.3 = (f32[7,8,8,128]{3,2,1,0:T(8,128)S(1)}, f32[7,8,8,128]{3,2,1,0:T(8,128)S(1)}, u32[]{:S(2)}, u32[]{:S(2)}) collective-permute-start(f32[7,8,8,128]{3,2,1,0:T(8,128)S(1)} %get-tuple-element.14.own), channel_id=1, source_target_pairs={{0,1},{2,3},{4,5},{6,7},{8,9},{10,11},{12,13},{14,15},{1,0},{3,2},... | collective-permute-start | bytes 688136 | tf_op jit(solution)/shard_map/ppermute | solution.py:378
  21.9 7.0 %collective-permute-start.4 = (f32[48,8,128]{2,1,0:T(8,128)S(1)}, f32[48,8,128]{2,1,0:T(8,128)S(1)}, u32[]{:S(2)}, u32[]{:S(2)}) collective-permute-start(f32[48,8,128]{2,1,0:T(8,128)S(1)} %get-tuple-element.18), channel_id=1, source_target_pairs={{1,2},{3,4},{5,6},{7,8},{9,10},{11,12},{13,14},{2,1},{4,3},{6,5},{... | collective-permute-start | bytes 589832 | tf_op jit(solution)/shard_map/ppermute | solution.py:378
  23.8 5.1 %collective-permute-start.5 = (f32[48,8,128]{2,1,0:T(8,128)S(1)}, f32[48,8,128]{2,1,0:T(8,128)S(1)}, u32[]{:S(2)}, u32[]{:S(2)}) collective-permute-start(f32[48,8,128]{2,1,0:T(8,128)S(1)} %get-tuple-element.19), channel_id=1, source_target_pairs={{0,1},{2,3},{4,5},{6,7},{8,9},{10,11},{12,13},{14,15},{1,0},{3,2},... | collective-permute-start | bytes 589832 | tf_op jit(solution)/shard_map/ppermute | solution.py:378

commit v10 on v7

--- a/solution.py
+++ b/solution.py
@@ -81,13 +81,27 @@
 
 
 def pack_kernel(
-    column, basis, diffusivity_in, speed_in, upwind_in, out, to_first, to_second, diffusivity, speed, upwind, sems
+    column_in,
+    basis_in,
+    diffusivity_in,
+    speed_in,
+    upwind_in,
+    out,
+    to_first,
+    to_second,
+    column,
+    basis,
+    diffusivity,
+    speed,
+    upwind,
+    sems,
 ):
     copies = [
         pltpu.make_async_copy(src, dst, sems.at[n])
         for n, (src, dst) in enumerate(
             (
-                (basis.at[column[0]], out.at[0]),
+                (column_in, column),
+                (basis_in, basis),
                 (diffusivity_in, diffusivity),
                 (speed_in, speed),
                 (upwind_in, upwind),
@@ -98,6 +112,7 @@
         copy.start()
     for copy in copies:
         copy.wait()
+    out[0] = basis[column[0, 0]]
     factor = -2.0 / HALF
     for dim in range(3):
         flow = upwind[dim].astype(F32)
@@ -389,17 +404,19 @@
     own, to_first, to_second = pl.pallas_call(
         pack_kernel,
         out_shape=(pltpu.VMEM((FIELDS, B, B, LANES), F32), pltpu.VMEM(part, F32), pltpu.VMEM(part, F32)),
-        in_specs=[SMEM] + [HBM] * 4,
+        in_specs=[HBM] * 5,
         out_specs=(VMEM,) * 3,
         scratch_shapes=[
+            pltpu.SMEM((1, 1), jnp.int32),
+            pltpu.VMEM((4, B, B, LANES), F32),
             pltpu.VMEM(faces, F32),
             pltpu.VMEM(faces, F32),
             pltpu.VMEM(faces, jnp.int32),
-            pltpu.SemaphoreType.DMA((4,)),
+            pltpu.SemaphoreType.DMA((5,)),
         ],
         compiler_params=PARAMS,
         name="pack",
-    )(restart_column, *(in_hbm(array) for array in (previous_basis, diffusivity, speed, upwind)))
+    )(jnp.reshape(restart_column, (1, 1)), *(in_hbm(array) for array in (previous_basis, diffusivity, speed, upwind)))
     second_x = paired(to_second, "gx", 1)
     first_x = paired(to_first, "gx", 0)
     corner = jax.ShapeDtypeStruct((TILES_CORNER, B, LANES), F32)

time: 76.2 us -> 76.2 us (level)
  no operation moved by 1% of the time
where the time goes in v10:
time: 76.2 us; the launch traced here: 75.9 us
  blocking collectives  42.3 us (56%)
  starting transfers between devices  25 us (33%)
  Pallas kernels  5.9 us (8%)
  between operations  1.38 us (2%)
  waiting for transfers between devices  1.26 us (2%)
    all_to_all x1, blocking collectives, body(): parts = lax.all_to_all(line, 'gx', 0, 0, tiled=True)  29.8 us
    ppermute x6, starting transfers between devices, paired(): lax.ppermute(array, axis, [(i, i + 1) for i in lower] + [(i + 1, i) for i...  25 us
    all_to_all x1, blocking collectives, body(): parts = lax.all_to_all(gram, 'gz', 0, 0, tiled=True)  12.5 us
    pallas_call x1, Pallas kernels, body(): pl.pallas_call(basis_kernel, out_shape=(jax.ShapeDtypeStruct((COLS, B, B,...  2.4 us
    pallas_call x1, Pallas kernels, body(): pl.pallas_call(lambda *refs: factor_kernel(scale, *refs), out_shape=(jax....  2.22 us
  transfers between devices with their start and end apart: 6, of which 1 were waited for; matrix products, arithmetic and copies ran while one was open for 0% of the time, Pallas kernels for 0%

profile of v10, /device:TPU:1, one launch (start us, length us, event | category | flops | bytes accessed | tf_op | source)
XLA Modules:
  0.0 75.9 jit_solution(1402801955635511179)
XLA Ops:
  1.3 1.2 %pack.1 = (f32[7,8,8,128]{3,2,1,0:T(8,128)S(1)}, f32[51,8,128]{2,1,0:T(8,128)S(1)}, f32[51,8,128]{2,1,0:T(8,128)S(1)}) custom-call(s32[1,1]{1,0:T(1,128)} %bitcast.6.column_in, f32[4,8,8,128]{3,2,1,0:T(8,128)} %basis_in.1, f32[3,8,8,128]{3,2,1,0:T(8,128)} %diffusivity_in.1, f32[3,8,8,128]{3,2,1,0:T(8,128)} %speed_in.1, s32[3,8,8,128]{3,2,1,0:T(8,128)} %upwind_in.1), custom_call_target="tpu_custom_call" | custom-call | tf_op jit(solution)/shard_map/pack/pallas_call | solution.py:404
  2.4 0.7 collective-permute-start
  3.1 10.0 %collective-permute-start.1 = (f32[51,8,128]{2,1,0:T(8,128)S(1)}, f32[51,8,128]{2,1,0:T(8,128)S(1)}, u32[]{:S(2)}, u32[]{:S(2)}) collective-permute-start(f32[51,8,128]{2,1,0:T(8,128)S(1)} %get-tuple-element.16), channel_id=1, source_target_pairs={{0,16},{32,48},{64,80},{96,112},{128,144},{160,176},{192,208},{224... | collective-permute-start | bytes 626696 | tf_op jit(solution)/shard_map/ppermute | solution.py:393
  13.1 4.2 %collective-permute-start.2 = (f32[7,8,8,128]{3,2,1,0:T(8,128)S(1)}, f32[7,8,8,128]{3,2,1,0:T(8,128)S(1)}, u32[]{:S(2)}, u32[]{:S(2)}) collective-permute-start(f32[7,8,8,128]{3,2,1,0:T(8,128)S(1)} %get-tuple-element.14.own), channel_id=1, source_target_pairs={{1,2},{3,4},{5,6},{7,8},{9,10},{11,12},{13,14},{2,1},{4,3},{6,5},{... | collective-permute-start | bytes 688136 | tf_op jit(solution)/shard_map/ppermute | solution.py:393
  17.3 4.4 %collective-permute-start.3 = (f32[7,8,8,128]{3,2,1,0:T(8,128)S(1)}, f32[7,8,8,128]{3,2,1,0:T(8,128)S(1)}, u32[]{:S(2)}, u32[]{:S(2)}) collective-permute-start(f32[7,8,8,128]{3,2,1,0:T(8,128)S(1)} %get-tuple-element.14.own), channel_id=1, source_target_pairs={{0,1},{2,3},{4,5},{6,7},{8,9},{10,11},{12,13},{14,15},{1,0},{3,2},... | collective-permute-start | bytes 688136 | tf_op jit(solution)/shard_map/ppermute | solution.py:393
  21.8 0.0 collective-permute-done.second
  21.8 0.0 collective-permute-done.1.first
  21.8 0.1 corners.1
  21.9 1.9 %collective-permute-start.4 = (f32[48,8,128]{2,1,0:T(8,128)S(1)}, f32[48,8,128]{2,1,0:T(8,128)S(1)}, u32[]{:S(2)}, u32[]{:S(2)}) collective-permute-start(f32[48,8,128]{2,1,0:T(8,128)S(1)} %get-tuple-element.18), channel_id=1, source_target_pairs={{1,2},{3,4},{5,6},{7,8},{9,10},{11,12},{13,14},{2,1},{4,3},{6,5},{... | collective-permute-start | bytes 589832 | tf_op jit(solution)/shard_map/ppermute | solution.py:393
  23.8 3.8 %collective-permute-start.5 = (f32[48,8,128]{2,1,0:T(8,128)S(1)}, f32[48,8,128]{2,1,0:T(8,128)S(1)}, u32[]{:S(2)}, u32[]{:S(2)}) collective-permute-start(f32[48,8,128]{2,1,0:T(8,128)S(1)} %get-tuple-element.19), channel_id=1, source_target_pairs={{0,1},{2,3},{4,5},{6,7},{8,9},{10,11},{12,13},{14,15},{1,0},{3,2},... | collective-permute-start | bytes 589832 | tf_op jit(solution)/shard_map/ppermute | solution.py:393
  27.6 0.0 collective-permute-done.2.second
  27.7 0.0 collective-permute-done.3.first
  27.7 1.2 %collective-permute-done.4.corner_second = f32[48,8,128]{2,1,0:T(8,128)S(1)} collective-permute-done((f32[48,8,128]{2,1,0:T(8,128)S(1)}, f32[48,8,128]{2,1,0:T(8,128)S(1)}, u32[]{:S(2)}, u32[]{:S(2)}) %collective-permute-start.4) | collective-permute-done | bytes 196640 | tf_op jit(solution)/shard_map/ppermute | solution.py:393
  28.9 0.0 collective-permute-done.5.corner_first
  28.9 2.4 %basis.1 = (f32[9,8,8,128]{3,2,1,0:T(8,128)S(1)}, f32[32,128]{1,0:T(8,128)S(1)}) custom-call(f32[7,8,8,128]{3,2,1,0:T(8,128)S(1)} %get-tuple-element.14.own, f32[7,16,8,128]{3,2,1,0:T(8,128)S(1)} %get-tuple-element.17.strip, f32[7,8,8,128]{3,2,1,0:T(8,128)S(1)} %collective-permute-done.2.second, f32[7,8,8,128]{3,2,1,0:T(8,128)S(1)} %collective-permute-done.3.first, ...), custom_call_target="tpu_custom_call" | custom-call | tf_op jit(solution)/shard_map/basis/pallas_call | solution.py:436
  31.3 12.5 %all_to_all.22 = f32[16,2,128]{2,1,0:T(2,128)S(1)} all-to-all(f32[16,2,128]{2,1,0:T(2,128)S(1)} %bitcast.10), channel_id=1, replica_groups=mesh['gx'=64,'gz'=16] {'gz'}, dimensions={0} | all-to-all | bytes 32768 | tf_op jit(solution)/shard_map/all_to_all | solution.py:453
  43.8 29.8 %all_to_all.23 = f32[64,2,128]{2,1,0:T(2,128)S(1)} all-to-all(f32[64,2,128]{2,1,0:T(2,128)S(1)} %bitcast.7), channel_id=1, replica_groups=mesh['gx'=64,'gz'=16] {'gx'}, dimensions={0} | all-to-all | bytes 131072 | tf_op jit(solution)/shard_map/all_to_all | solution.py:462
  73.7 2.2 %factor.1 = (f32[9,8,8,128]{3,2,1,0:T(8,128)}, f32[9,9]{1,0:T(8,128)}, f32[8,9]{1,0:T(8,128)}) custom-call(f32[128,128]{1,0:T(8,128)S(1)} %bitcast.8, f32[9,8,8,128]{3,2,1,0:T(8,128)S(1)} %get-tuple-element.21.refs_1_), custom_call_target="tpu_custom_call" | custom-call | tf_op jit(solution)/shard_map/factor/pallas_call | solution.py:464
  (1 shorter events, 0.0 us)
Async XLA Ops:
  2.4 19.4 %collective-permute-start = (f32[51,8,128]{2,1,0:T(8,128)S(1)}, f32[51,8,128]{2,1,0:T(8,128)S(1)}, u32[]{:S(2)}, u32[]{:S(2)}) collective-permute-start(f32[51,8,128]{2,1,0:T(8,128)S(1)} %get-tuple-element.15), channel_id=1, source_target_pairs={{16,32},{48,64},{80,96},{112,128},{144,160},{176,192},{208,224},{2... | collective-permute-start | bytes 626696 | tf_op jit(solution)/shard_map/ppermute | solution.py:393
  3.1 18.7 %collective-permute-start.1 = (f32[51,8,128]{2,1,0:T(8,128)S(1)}, f32[51,8,128]{2,1,0:T(8,128)S(1)}, u32[]{:S(2)}, u32[]{:S(2)}) collective-permute-start(f32[51,8,128]{2,1,0:T(8,128)S(1)} %get-tuple-element.16), channel_id=1, source_target_pairs={{0,16},{32,48},{64,80},{96,112},{128,144},{160,176},{192,208},{224... | collective-permute-start | bytes 626696 | tf_op jit(solution)/shard_map/ppermute | solution.py:393
  13.1 14.5 %collective-permute-start.2 = (f32[7,8,8,128]{3,2,1,0:T(8,128)S(1)}, f32[7,8,8,128]{3,2,1,0:T(8,128)S(1)}, u32[]{:S(2)}, u32[]{:S(2)}) collective-permute-start(f32[7,8,8,128]{3,2,1,0:T(8,128)S(1)} %get-tuple-element.14.own), channel_id=1, source_target_pairs={{1,2},{3,4},{5,6},{7,8},{9,10},{11,12},{13,14},{2,1},{4,3},{6,5},{... | collective-permute-start | bytes 688136 | tf_op jit(solution)/shard_map/ppermute | solution.py:393
  17.3 10.3 %collective-permute-start.3 = (f32[7,8,8,128]{3,2,1,0:T(8,128)S(1)}, f32[7,8,8,128]{3,2,1,0:T(8,128)S(1)}, u32[]{:S(2)}, u32[]{:S(2)}) collective-permute-start(f32[7,8,8,128]{3,2,1,0:T(8,128)S(1)} %get-tuple-element.14.own), channel_id=1, source_target_pairs={{0,1},{2,3},{4,5},{6,7},{8,9},{10,11},{12,13},{14,15},{1,0},{3,2},... | collective-permute-start | bytes 688136 | tf_op jit(solution)/shard_map/ppermute | solution.py:393
  21.9 7.0 %collective-permute-start.4 = (f32[48,8,128]{2,1,0:T(8,128)S(1)}, f32[48,8,128]{2,1,0:T(8,128)S(1)}, u32[]{:S(2)}, u32[]{:S(2)}) collective-permute-start(f32[48,8,128]{2,1,0:T(8,128)S(1)} %get-tuple-element.18), channel_id=1, source_target_pairs={{1,2},{3,4},{5,6},{7,8},{9,10},{11,12},{13,14},{2,1},{4,3},{6,5},{... | collective-permute-start | bytes 589832 | tf_op jit(solution)/shard_map/ppermute | solution.py:393
  23.8 5.1 %collective-permute-start.5 = (f32[48,8,128]{2,1,0:T(8,128)S(1)}, f32[48,8,128]{2,1,0:T(8,128)S(1)}, u32[]{:S(2)}, u32[]{:S(2)}) collective-permute-start(f32[48,8,128]{2,1,0:T(8,128)S(1)} %get-tuple-element.19), channel_id=1, source_target_pairs={{0,1},{2,3},{4,5},{6,7},{8,9},{10,11},{12,13},{14,15},{1,0},{3,2},... | collective-permute-start | bytes 589832 | tf_op jit(solution)/shard_map/ppermute | solution.py:393

commit v11 on v7

--- a/solution.py
+++ b/solution.py
@@ -221,7 +221,7 @@
     for k in range(1, COLS):
         src, dst = (k - 1) % 2, k % 2
 
-        def layer(a, carry, k=k, src=src, dst=dst):
+        def layer(a, k=k, src=src, dst=dst):
             v = field[src, a]
             x = coeff[0, a] * v + coeff[1, a] * field[src, a + 1] + coeff[2, a] * field[src, a - 1]
             y = coeff[3, a] * pltpu.roll(v, WIDE - 1, 0) + coeff[4, a] * pltpu.roll(v, 1, 0)
@@ -230,11 +230,13 @@
             new = 0.5 * total if k == 1 else total - field[dst, a]
             if k == S:
                 block[k, a - B] = new[B : 2 * B]
+            elif a == k or a == WIDE - 1 - k:
+                field[dst, a, B : 2 * B] = new[B : 2 * B]
             else:
                 field[dst, a] = new
-            return carry
-
-        lax.fori_loop(k, WIDE - k, layer, 0, unroll=True)
+
+        for a in range(k, WIDE - k):
+            layer(a)
         if k < S:
             block[k] = field[dst, B : 2 * B, B : 2 * B, :]
 
@@ -298,11 +300,11 @@
     tiles = [ref[B * t : B * (t + 1), :] for t in range(ref.shape[0] // B)]
     pairs = [(t, pltpu.roll(t, B - 1, 0)) for t in tiles]
     while len(pairs) > 1:
-        pairs = [pair_add(pairs[t], pairs[t + 1]) for t in range(0, len(pairs), 2)]
+        pairs = [loose_add(pairs[t], pairs[t + 1]) for t in range(0, len(pairs), 2)]
     total = pairs[0]
     for distance in (2, 4):
-        total = pair_add(total, pair_roll(total, distance, 0))
-    return total
+        total = loose_add(total, pair_roll(total, distance, 0))
+    return fast_two_sum(*total)
 
 
 def sum_kernel(parts, out):

time: 76.2 us -> 76.1 us (level)
  no operation moved by 1% of the time
where the time goes in v11:
time: 76.1 us; the launch traced here: 75.8 us
  blocking collectives  42.3 us (56%)
  starting transfers between devices  25 us (33%)
  Pallas kernels  5.8 us (8%)
  between operations  1.37 us (2%)
  waiting for transfers between devices  1.26 us (2%)
    all_to_all x1, blocking collectives, body(): parts = lax.all_to_all(line, 'gx', 0, 0, tiled=True)  29.8 us
    ppermute x6, starting transfers between devices, paired(): lax.ppermute(array, axis, [(i, i + 1) for i in lower] + [(i + 1, i) for i...  25 us
    all_to_all x1, blocking collectives, body(): parts = lax.all_to_all(gram, 'gz', 0, 0, tiled=True)  12.5 us
    pallas_call x1, Pallas kernels, body(): pl.pallas_call(basis_kernel, out_shape=(jax.ShapeDtypeStruct((COLS, B, B,...  2.4 us
    pallas_call x1, Pallas kernels, body(): pl.pallas_call(lambda *refs: factor_kernel(scale, *refs), out_shape=(jax....  2.19 us
  transfers between devices with their start and end apart: 6, of which 1 were waited for; matrix products, arithmetic and copies ran while one was open for 0% of the time, Pallas kernels for 0%

profile of v11, /device:TPU:1, one launch (start us, length us, event | category | flops | bytes accessed | tf_op | source)
XLA Modules:
  0.0 75.8 jit_solution(13027401781971144267)
XLA Ops:
  1.3 1.1 %pack.1 = (f32[7,8,8,128]{3,2,1,0:T(8,128)S(1)}, f32[51,8,128]{2,1,0:T(8,128)S(1)}, f32[51,8,128]{2,1,0:T(8,128)S(1)}) custom-call(s32[1]{0:T(128)S(6)} %copy.8.column, f32[4,8,8,128]{3,2,1,0:T(8,128)} %basis.2, f32[3,8,8,128]{3,2,1,0:T(8,128)} %diffusivity_in.1, f32[3,8,8,128]{3,2,1,0:T(8,128)} %speed_in.1, s32[3,8,8,128]{3,2,1,0:T(8,128)} %upwind_in.1), custom_call_target="tpu_custom_call" | custom-call | tf_op jit(solution)/shard_map/pack/pallas_call | solution.py:391
  2.4 0.7 collective-permute-start
  3.1 10.0 %collective-permute-start.1 = (f32[51,8,128]{2,1,0:T(8,128)S(1)}, f32[51,8,128]{2,1,0:T(8,128)S(1)}, u32[]{:S(2)}, u32[]{:S(2)}) collective-permute-start(f32[51,8,128]{2,1,0:T(8,128)S(1)} %get-tuple-element.16), channel_id=1, source_target_pairs={{0,16},{32,48},{64,80},{96,112},{128,144},{160,176},{192,208},{224... | collective-permute-start | bytes 626696 | tf_op jit(solution)/shard_map/ppermute | solution.py:380
  13.0 4.2 %collective-permute-start.2 = (f32[7,8,8,128]{3,2,1,0:T(8,128)S(1)}, f32[7,8,8,128]{3,2,1,0:T(8,128)S(1)}, u32[]{:S(2)}, u32[]{:S(2)}) collective-permute-start(f32[7,8,8,128]{3,2,1,0:T(8,128)S(1)} %get-tuple-element.14.own), channel_id=1, source_target_pairs={{1,2},{3,4},{5,6},{7,8},{9,10},{11,12},{13,14},{2,1},{4,3},{6,5},{... | collective-permute-start | bytes 688136 | tf_op jit(solution)/shard_map/ppermute | solution.py:380
  17.3 4.4 %collective-permute-start.3 = (f32[7,8,8,128]{3,2,1,0:T(8,128)S(1)}, f32[7,8,8,128]{3,2,1,0:T(8,128)S(1)}, u32[]{:S(2)}, u32[]{:S(2)}) collective-permute-start(f32[7,8,8,128]{3,2,1,0:T(8,128)S(1)} %get-tuple-element.14.own), channel_id=1, source_target_pairs={{0,1},{2,3},{4,5},{6,7},{8,9},{10,11},{12,13},{14,15},{1,0},{3,2},... | collective-permute-start | bytes 688136 | tf_op jit(solution)/shard_map/ppermute | solution.py:380
  21.7 0.0 collective-permute-done.second
  21.8 0.0 collective-permute-done.1.first
  21.8 0.1 corners.1
  21.9 1.9 %collective-permute-start.4 = (f32[48,8,128]{2,1,0:T(8,128)S(1)}, f32[48,8,128]{2,1,0:T(8,128)S(1)}, u32[]{:S(2)}, u32[]{:S(2)}) collective-permute-start(f32[48,8,128]{2,1,0:T(8,128)S(1)} %get-tuple-element.18), channel_id=1, source_target_pairs={{1,2},{3,4},{5,6},{7,8},{9,10},{11,12},{13,14},{2,1},{4,3},{6,5},{... | collective-permute-start | bytes 589832 | tf_op jit(solution)/shard_map/ppermute | solution.py:380
  23.8 3.8 %collective-permute-start.5 = (f32[48,8,128]{2,1,0:T(8,128)S(1)}, f32[48,8,128]{2,1,0:T(8,128)S(1)}, u32[]{:S(2)}, u32[]{:S(2)}) collective-permute-start(f32[48,8,128]{2,1,0:T(8,128)S(1)} %get-tuple-element.19), channel_id=1, source_target_pairs={{0,1},{2,3},{4,5},{6,7},{8,9},{10,11},{12,13},{14,15},{1,0},{3,2},... | collective-permute-start | bytes 589832 | tf_op jit(solution)/shard_map/ppermute | solution.py:380
  27.6 0.0 collective-permute-done.2.second
  27.6 0.0 collective-permute-done.3.first
  27.6 1.2 %collective-permute-done.4.corner_second = f32[48,8,128]{2,1,0:T(8,128)S(1)} collective-permute-done((f32[48,8,128]{2,1,0:T(8,128)S(1)}, f32[48,8,128]{2,1,0:T(8,128)S(1)}, u32[]{:S(2)}, u32[]{:S(2)}) %collective-permute-start.4) | collective-permute-done | bytes 196640 | tf_op jit(solution)/shard_map/ppermute | solution.py:380
  28.8 0.0 collective-permute-done.5.corner_first
  28.9 2.4 %basis.3 = (f32[9,8,8,128]{3,2,1,0:T(8,128)S(1)}, f32[32,128]{1,0:T(8,128)S(1)}) custom-call(f32[7,8,8,128]{3,2,1,0:T(8,128)S(1)} %get-tuple-element.14.own, f32[7,16,8,128]{3,2,1,0:T(8,128)S(1)} %get-tuple-element.17.strip, f32[7,8,8,128]{3,2,1,0:T(8,128)S(1)} %collective-permute-done.2.second, f32[7,8,8,128]{3,2,1,0:T(8,128)S(1)} %collective-permute-done.3.first, ...), custom_call_target="tpu_custom_call" | custom-call | tf_op jit(solution)/shard_map/basis/pallas_call | solution.py:421
  31.2 12.5 %all_to_all.22 = f32[16,2,128]{2,1,0:T(2,128)S(1)} all-to-all(f32[16,2,128]{2,1,0:T(2,128)S(1)} %bitcast.8), channel_id=1, replica_groups=mesh['gx'=64,'gz'=16] {'gz'}, dimensions={0} | all-to-all | bytes 32768 | tf_op jit(solution)/shard_map/all_to_all | solution.py:438
  43.7 29.8 %all_to_all.23 = f32[64,2,128]{2,1,0:T(2,128)S(1)} all-to-all(f32[64,2,128]{2,1,0:T(2,128)S(1)} %bitcast.5), channel_id=1, replica_groups=mesh['gx'=64,'gz'=16] {'gx'}, dimensions={0} | all-to-all | bytes 131072 | tf_op jit(solution)/shard_map/all_to_all | solution.py:447
  73.6 2.2 %factor.1 = (f32[9,8,8,128]{3,2,1,0:T(8,128)}, f32[9,9]{1,0:T(8,128)}, f32[8,9]{1,0:T(8,128)}) custom-call(f32[128,128]{1,0:T(8,128)S(1)} %bitcast.6, f32[9,8,8,128]{3,2,1,0:T(8,128)S(1)} %get-tuple-element.21.refs_1_), custom_call_target="tpu_custom_call" | custom-call | tf_op jit(solution)/shard_map/factor/pallas_call | solution.py:449
  (1 shorter events, 0.0 us)
Async XLA Ops:
  2.4 19.4 %collective-permute-start = (f32[51,8,128]{2,1,0:T(8,128)S(1)}, f32[51,8,128]{2,1,0:T(8,128)S(1)}, u32[]{:S(2)}, u32[]{:S(2)}) collective-permute-start(f32[51,8,128]{2,1,0:T(8,128)S(1)} %get-tuple-element.15), channel_id=1, source_target_pairs={{16,32},{48,64},{80,96},{112,128},{144,160},{176,192},{208,224},{2... | collective-permute-start | bytes 626696 | tf_op jit(solution)/shard_map/ppermute | solution.py:380
  3.1 18.7 %collective-permute-start.1 = (f32[51,8,128]{2,1,0:T(8,128)S(1)}, f32[51,8,128]{2,1,0:T(8,128)S(1)}, u32[]{:S(2)}, u32[]{:S(2)}) collective-permute-start(f32[51,8,128]{2,1,0:T(8,128)S(1)} %get-tuple-element.16), channel_id=1, source_target_pairs={{0,16},{32,48},{64,80},{96,112},{128,144},{160,176},{192,208},{224... | collective-permute-start | bytes 626696 | tf_op jit(solution)/shard_map/ppermute | solution.py:380
  13.0 14.5 %collective-permute-start.2 = (f32[7,8,8,128]{3,2,1,0:T(8,128)S(1)}, f32[7,8,8,128]{3,2,1,0:T(8,128)S(1)}, u32[]{:S(2)}, u32[]{:S(2)}) collective-permute-start(f32[7,8,8,128]{3,2,1,0:T(8,128)S(1)} %get-tuple-element.14.own), channel_id=1, source_target_pairs={{1,2},{3,4},{5,6},{7,8},{9,10},{11,12},{13,14},{2,1},{4,3},{6,5},{... | collective-permute-start | bytes 688136 | tf_op jit(solution)/shard_map/ppermute | solution.py:380
  17.3 10.3 %collective-permute-start.3 = (f32[7,8,8,128]{3,2,1,0:T(8,128)S(1)}, f32[7,8,8,128]{3,2,1,0:T(8,128)S(1)}, u32[]{:S(2)}, u32[]{:S(2)}) collective-permute-start(f32[7,8,8,128]{3,2,1,0:T(8,128)S(1)} %get-tuple-element.14.own), channel_id=1, source_target_pairs={{0,1},{2,3},{4,5},{6,7},{8,9},{10,11},{12,13},{14,15},{1,0},{3,2},... | collective-permute-start | bytes 688136 | tf_op jit(solution)/shard_map/ppermute | solution.py:380
  21.9 7.0 %collective-permute-start.4 = (f32[48,8,128]{2,1,0:T(8,128)S(1)}, f32[48,8,128]{2,1,0:T(8,128)S(1)}, u32[]{:S(2)}, u32[]{:S(2)}) collective-permute-start(f32[48,8,128]{2,1,0:T(8,128)S(1)} %get-tuple-element.18), channel_id=1, source_target_pairs={{1,2},{3,4},{5,6},{7,8},{9,10},{11,12},{13,14},{2,1},{4,3},{6,5},{... | collective-permute-start | bytes 589832 | tf_op jit(solution)/shard_map/ppermute | solution.py:380
  23.8 5.1 %collective-permute-start.5 = (f32[48,8,128]{2,1,0:T(8,128)S(1)}, f32[48,8,128]{2,1,0:T(8,128)S(1)}, u32[]{:S(2)}, u32[]{:S(2)}) collective-permute-start(f32[48,8,128]{2,1,0:T(8,128)S(1)} %get-tuple-element.19), channel_id=1, source_target_pairs={{0,1},{2,3},{4,5},{6,7},{8,9},{10,11},{12,13},{14,15},{1,0},{3,2},... | collective-permute-start | bytes 589832 | tf_op jit(solution)/shard_map/ppermute | solution.py:380
